TPU v7x, 32 devices: a whole 2x2x4 slice. The times are simulated.
32 devices in a mesh: groups: 2 (over y), blk: 4 (over z), narrow: 4 (over x, core).
Axes of the slice: x: 2, y: 2, z: 4, core: 2. Of those that a mesh axis runs over, the one named last changes fastest.
Arguments:
- points: bfloat16 [8192, 128], P(('groups', 'blk', 'narrow')), parts along dimension 0, may hold values from -8 to 8
- inv_scale: float32 [128], replicated, may hold values from 0.08 to 0.25
- targets: float32 [8192, 64], P(('groups', 'blk', 'narrow')), parts along dimension 0, may hold values from -6 to 6
Outputs:
- solution: float32 [8192, 64], P(('groups', 'blk', 'narrow')), parts along dimension 0
- residual: float32 [8192, 64], P(('groups', 'blk', 'narrow')), parts along dimension 0
There are 2 independent parts, one for each index of `groups`. A program takes and returns all parts, laid end to end along the dimension named above; an argument that names none is the same for every part. Nothing has to cross between parts.
All inputs are finite; a program needn't handle non-finite values.
Results may differ from a plain program's by a relative error of at most 0.0074.
Values may be sent and summed in bfloat16 or wider, within the bound.
No kernel may reach another device: no remote copies, remote signals or barrier semaphores. Data moves between devices by JAX's collectives and lax.ppermute only.
A program may use at most 64 MiB of HBM per device.

v0:
```python
import jax
import jax.numpy as jnp
from jax import lax
from jax.sharding import PartitionSpec as P

ITERATIONS = 2


noise_level = 1.0


def make_tile(rows, row_sq, columns):
    col_sq = jnp.sum(jnp.square(columns.astype(jnp.float32)), axis=1)
    inner = lax.dot_general(
        rows, columns, (((1,), (1,)), ((), ())), preferred_element_type=jnp.float32
    )
    return jnp.exp(-0.5 * (row_sq[:, None] + col_sq[None, :] - 2.0 * inner)).astype(jnp.bfloat16)


def column_total(values):
    return lax.psum(jnp.sum(values, axis=0), ("blk", "narrow"))


def body(points, inv_scale, targets):
    scaled = (points.astype(jnp.float32) * inv_scale[None, :]).astype(jnp.bfloat16)
    own_rows = lax.all_gather(scaled, "narrow", axis=0, tiled=True)
    row_sq = jnp.sum(jnp.square(own_rows.astype(jnp.float32)), axis=1)
    solution = jnp.zeros_like(targets)
    residual = targets
    direction = targets
    norm_now = column_total(residual * residual)
    for step in range(ITERATIONS):
        vector = direction.astype(jnp.bfloat16)
        tile = make_tile(own_rows, row_sq, lax.all_gather(scaled, "blk", axis=0, tiled=True))
        total = jnp.dot(
            tile,
            lax.all_gather(vector, "blk", axis=0, tiled=True),
            preferred_element_type=jnp.float32,
        )
        mine = lax.psum_scatter(total, "narrow", scatter_dimension=0, tiled=True)
        image = mine + noise_level * direction
        alpha = norm_now / column_total(direction * image)
        solution = solution + alpha[None, :] * direction
        residual = residual - alpha[None, :] * image
        norm_next = column_total(residual * residual)
        if step + 1 < ITERATIONS:
            direction = residual + (norm_next / norm_now)[None, :] * direction
            norm_now = norm_next
    return (solution, residual)


def solution(mesh):
    placed = (P(("groups", "blk", "narrow"), None), P(), P(("groups", "blk", "narrow"), None))
    return jax.shard_map(
        body,
        mesh=mesh,
        in_specs=placed,
        out_specs=(P(("groups", "blk", "narrow"), None), P(("groups", "blk", "narrow"), None)),
        check_vma=False,
    )
```

profile of v0, /device:TPU:0, one launch (start us, length us, event | category | flops | bytes accessed | tf_op | source)
XLA Modules:
  0.0 204.7 jit_solution(14842852841772949236)
XLA Ops:
  7.2 0.0 reduce-scatter.3.cloned.1.call-start
  7.2 0.9 multiply_convert_fusion
  8.1 15.6 %all_gather.14 = bf16[1024,128]{1,0:T(8,128)(2,1)S(1)} all-gather(bf16[256,128]{1,0:T(8,128)(2,1)S(1)} %multiply_convert_fusion), channel_id=1, replica_groups=mesh['groups'=2,'blk'=4,'narrow'=4] {'blk'}, dimensions={0}, use_global_device_ids=true | all-gather | bytes 327680 | tf_op jit(solution)/shard_map/all_gather | solution.py:34
  23.7 5.8 %all_gather.13 = bf16[1024,128]{1,0:T(8,128)(2,1)S(1)} all-gather(bf16[256,128]{1,0:T(8,128)(2,1)S(1)} %multiply_convert_fusion), channel_id=1, replica_groups=mesh['groups'=2,'blk'=4,'narrow'=4] {'narrow'}, dimensions={0}, use_global_device_ids=true | all-gather | bytes 327680 | tf_op jit(solution)/shard_map/all_gather | solution.py:26
  29.5 0.2 multiply_reduce_fusion
  29.7 0.2 multiply_reduce_fusion.1
  29.9 0.8 convert_element_type.28
  30.8 13.4 %all_gather.15 = bf16[1024,64]{0,1:T(8,128)(2,1)S(1)} all-gather(bf16[256,64]{0,1:T(8,128)(2,1)S(1)} %convert_element_type.28), channel_id=1, replica_groups=mesh['groups'=2,'blk'=4,'narrow'=4] {'blk'}, dimensions={0}, use_global_device_ids=true | all-gather | bytes 163840 | tf_op jit(solution)/shard_map/all_gather | solution.py:37
  44.2 1.1 exponential_convert_fusion
  45.2 0.0 copy-start
  45.2 1.5 fusion.1
  46.7 0.0 reduce-scatter.3.cloned.1.call-update
  46.7 0.0 reduce-scatter.5.cloned.1.call-start
  46.8 21.7 %reduce-scatter.3.cloned.1.call-done = f32[256,64]{0,1:T(8,128)} async-done(((f32[1024,64]{0,1:T(8,128)}), f32[256,64]{0,1:T(8,128)}) %reduce-scatter.3.cloned.1.call-update) | async-done | bytes 65552 | tf_op jit(solution)/shard_map/reduce_scatter | solution.py:40
  68.5 0.0 copy-done
  68.5 0.9 multiply_reduce_fusion.4
  69.4 32.2 %all-reduce = (f32[64]{0:T(128)S(1)}, f32[64]{0:T(128)S(1)}) all-reduce(f32[64]{0:T(128)S(1)} %get-tuple-element.3, f32[64]{0:T(128)S(1)} %get-tuple-element.2), channel_id=1, replica_groups=mesh['groups'=2,'blk'=4,'narrow'=4] {'blk','narrow'}, use_global_device_ids=true, to_apply=%region_1.0 | all-reduce | flops 128 | bytes 1024 | tf_op jit(solution)/shard_map/psum | solution.py:21
  101.6 0.2 multiply_reduce_fusion.3
  101.8 29.5 %psum.30 = f32[64]{0:T(128)S(1)} all-reduce(f32[64]{0:T(128)S(1)} %multiply_reduce_fusion.3), channel_id=1, replica_groups=mesh['groups'=2,'blk'=4,'narrow'=4] {'blk','narrow'}, use_global_device_ids=true, to_apply=%region_8.0 | all-reduce | flops 64 | bytes 512 | tf_op jit(solution)/shard_map/psum | solution.py:21
  131.3 0.1 fusion
  131.4 13.6 %all_gather.16 = bf16[1024,64]{0,1:T(8,128)(2,1)S(1)} all-gather(bf16[256,64]{0,1:T(8,128)(2,1)S(1)} %get-tuple-element.8), channel_id=1, replica_groups=mesh['groups'=2,'blk'=4,'narrow'=4] {'blk'}, dimensions={0}, use_global_device_ids=true | all-gather | bytes 163840 | tf_op jit(solution)/shard_map/all_gather | solution.py:37
  145.0 1.5 fusion.2
  146.5 0.0 reduce-scatter.5.cloned.1.call-update
  146.5 17.5 %reduce-scatter.5.cloned.1.call-done = f32[256,64]{0,1:T(8,128)} async-done(((f32[1024,64]{0,1:T(8,128)}), f32[256,64]{0,1:T(8,128)}) %reduce-scatter.5.cloned.1.call-update) | async-done | bytes 65552 | tf_op jit(solution)/shard_map/reduce_scatter | solution.py:40
  164.0 0.9 multiply_reduce_fusion.2
  164.9 32.2 %psum.31 = f32[64]{0:T(128)S(1)} all-reduce(f32[64]{0:T(128)S(1)} %get-tuple-element.6), channel_id=1, replica_groups=mesh['groups'=2,'blk'=4,'narrow'=4] {'blk','narrow'}, use_global_device_ids=true, to_apply=%region_11.0 | all-reduce | flops 64 | bytes 512 | tf_op jit(solution)/shard_map/psum | solution.py:21
  197.2 0.7 multiply_subtract_fusion
  (3 shorter events, 0.0 us)
Async XLA Ops:
  7.2 61.3 %reduce-scatter.3.cloned.1.call-start = ((), (), s32[]{:S(2)}) async-start(), calls=%async_computation.2 | async-start | bytes 327680 | tf_op jit(solution)/shard_map/reduce_scatter | solution.py:40
  45.2 23.2 %copy-start = (f32[256,64]{0,1:T(8,128)S(1)}, f32[256,64]{0,1:T(8,128)}, u32[]{:S(2)}) copy-start(f32[256,64]{0,1:T(8,128)} %param.5) | copy-start | bytes 196612
  46.7 117.3 %reduce-scatter.5.cloned.1.call-start = ((), (), s32[]{:S(2)}) async-start(), calls=%async_computation.3 | async-start | bytes 327680 | tf_op jit(solution)/shard_map/reduce_scatter | solution.py:40
Sparse Core Ops, SparseCore 0:
  46.8 21.5 reduce-scatter.2
  146.6 17.3 reduce-scatter.4
where the time goes:
time: 205 us
  blocking collectives  142 us (69%)
  waiting for transfers between devices  39.2 us (19%)
  between operations  14.1 us (7%)
  other arithmetic  5.06 us (2%)
  matrix products  3.98 us (2%)
    psum x3, blocking collectives, column_total(): return lax.psum(jnp.sum(values, axis=0), ('blk', 'narrow'))  93.9 us
    reduce_scatter x2, waiting for transfers between devices, body(): mine = lax.psum_scatter(total, 'narrow', scatter_dimension=0, tiled=True)  39.2 us
    all_gather x2, blocking collectives, body(): lax.all_gather(vector, 'blk', axis=0, tiled=True)  27 us
    all_gather x1, blocking collectives, body(): lax.all_gather(scaled, 'blk', axis=0, tiled=True)  15.6 us
    all_gather x1, blocking collectives, body(): own_rows = lax.all_gather(scaled, 'narrow', axis=0, tiled=True)  5.77 us
  transfers between devices with their start and end apart: 2, of which 2 were waited for; matrix products, arithmetic and copies ran while one was open for 0% of the time, Pallas kernels for 0%

commit v1 on v0

v1 whole, which is shorter than its diff:
```python
import functools

import jax
import jax.numpy as jnp
from jax import lax
from jax.experimental import pallas as pl
from jax.experimental.pallas import tpu as pltpu
from jax.sharding import PartitionSpec as P

ITERATIONS = 2
noise_level = 1.0

BF16 = jnp.bfloat16
F32 = jnp.float32
LAST = (((1,), (1,)), ((), ()))
VMEM = pl.BlockSpec(memory_space=pltpu.VMEM)
LIMIT = 24 * 2**20


def call(kernel, outs, name, flops=0, exps=0, bytes_=0, scratch=()):
    return pl.pallas_call(
        kernel,
        out_shape=outs,
        out_specs=jax.tree.map(lambda _: VMEM, outs),
        scratch_shapes=list(scratch),
        name=name,
        cost_estimate=pl.CostEstimate(
            flops=flops, bytes_accessed=bytes_, transcendentals=exps
        ),
        compiler_params=pltpu.CompilerParams(vmem_limit_bytes=LIMIT),
    )


def pack_kernel(points_ref, scale_ref, targets_ref, pack_ref):
    n = points_ref.shape[0]
    half = n // 2
    m = targets_ref.shape[0]
    pack_ref[:n] = (points_ref[...].astype(F32) * scale_ref[...]).astype(BF16)
    pack_ref[n : n + m] = targets_ref[:, :half].astype(BF16)
    pack_ref[n + m :] = targets_ref[:, half:].astype(BF16)


def exponents(points, first):
    n, depth = points.shape
    value = -0.5 * jnp.sum(jnp.square(points.astype(F32)), axis=1, keepdims=True)
    high = value.astype(BF16).astype(F32)
    rest = value - high
    middle = rest.astype(BF16).astype(F32)
    low = rest - middle
    lane = lax.broadcasted_iota(jnp.int32, (n, depth), 1) - first
    other = lax.broadcasted_iota(jnp.int32, (n, depth), 1) - (3 - first)
    ones = jnp.where((other >= 0) & (other < 3), 1.0, 0.0)
    terms = jnp.where(lane == 0, high, jnp.where(lane == 1, middle, jnp.where(lane == 2, low, ones)))
    return terms.astype(BF16)


def fill(packs, n, first, out):
    depth = packs[0].shape[1]
    at = 0
    for ref in packs:
        for block in range(ref.shape[0] * 2 // (3 * n)):
            start = block * (n * 3 // 2)
            points = ref[start : start + n]
            out[at : at + n, :depth] = points
            out[at : at + n, depth:] = exponents(points, first)
            at += n


def vectors(packs, n, out):
    at = 0
    for ref in packs:
        for block in range(ref.shape[0] * 2 // (3 * n)):
            start = block * (n * 3 // 2) + n
            m = n // 4
            for part in range(2):
                out[:, at : at + n // 2] = ref[start + part * m : start + (part + 1) * m]
                at += n // 2


def make_tile(a_ref, b_ref, rows, cols, k_ref):
    step = min(rows, 512)

    def one(i, _):
        at = pl.multiple_of(i * step, step)
        inner = lax.dot_general(
            a_ref[pl.ds(at, step), :], b_ref[...], LAST, preferred_element_type=F32
        )
        k_ref[pl.ds(at, step), :] = jnp.exp(inner).astype(BF16)
        return 0

    lax.fori_loop(0, rows // step, one, 0)


def apply(vector_ref, k_ref, at, rows):
    return jnp.dot(
        vector_ref[:, at : at + rows], k_ref[...], preferred_element_type=F32
    )


def tile_kernel(n, n_rows, *refs):
    row_packs, (col_pack, *before, k_ref, y_ref, a, b, v) = refs[:n_rows], refs[n_rows:]
    fill(row_packs, n, 0, a)
    fill([col_pack], n, 3, b)
    vectors(row_packs, n, v)
    make_tile(a, b, a.shape[0], b.shape[0], k_ref)
    y = apply(v, k_ref, 0, a.shape[0])
    for ref in before:
        y = y + ref[...]
    y_ref[...] = y


def tile(n, m, row_packs, col_pack, before, name):
    depth = col_pack.shape[1]
    size = n + n // 2
    rows = sum(p.shape[0] for p in row_packs) // size * n
    cols = col_pack.shape[0] // size * n
    return call(
        functools.partial(tile_kernel, n, len(row_packs)),
        (jax.ShapeDtypeStruct((rows, cols), BF16), jax.ShapeDtypeStruct((m, cols), F32)),
        name,
        flops=rows * cols * (4 * depth + 2 * m),
        exps=rows * cols,
        bytes_=2 * rows * cols,
        scratch=[
            pltpu.VMEM((rows, 2 * depth), BF16),
            pltpu.VMEM((cols, 2 * depth), BF16),
            pltpu.VMEM((m, rows), BF16),
        ],
    )(*row_packs, col_pack, *before)


def columns_of(pieces, m):
    lane = lax.broadcasted_iota(jnp.int32, (m, 128), 1)
    out = jnp.zeros((m, 128), F32)
    for index, piece in enumerate(pieces):
        out = jnp.where(lane == index, piece, out)
    return out


def total(values):
    return jnp.sum(values, axis=1, keepdims=True)


def join_kernel(n, tz_ref, tx_ref, yz_ref, yx_ref, y_ref, sums_ref, v):
    vectors([tz_ref, tx_ref], n, v)
    half = yz_ref.shape[1]
    b = v[...].astype(F32)
    y_ref[:, :half] = yz_ref[...].astype(BF16)
    y_ref[:, half:] = yx_ref[...].astype(BF16)
    by = total(b[:, :half] * yz_ref[...]) + total(b[:, half:] * yx_ref[...])
    sums_ref[...] = columns_of([total(b * b), by], v.shape[0])


def first_step(mine, others):
    bb = mine[:, 0:1] + others[:, 0:1]
    by = mine[:, 1:2] + others[:, 1:2]
    bw = by + noise_level * bb
    return bb, bw, bb / bw


def second_kernel(
    n, tz_ref, tx_ref, yz_ref, yx_ref, y_ref, yu_ref, mine_ref, theirs_ref,
    kzz, kuz, kxz, kux, kx, kuxx, z_ref, sums_ref, v,
):
    half = yz_ref.shape[1]
    m = v.shape[0]
    vectors([tz_ref, tx_ref], n, v)
    _, _, a0 = first_step(mine_ref[...], theirs_ref[...])
    rows = kzz.shape[0]
    zz = (
        apply(y_ref, kzz, 0, rows) + apply(y_ref, kxz, rows, rows)
        + apply(yu_ref, kuz, 0, rows) + apply(yu_ref, kux, rows, rows)
    )
    yall = jnp.concatenate(
        [y_ref[:, :rows], yu_ref[:, :rows], y_ref[:, rows:]], axis=1
    )
    zx = jnp.dot(yall, kx[...], preferred_element_type=F32) + apply(
        yu_ref, kuxx, rows, rows
    )
    z_ref[...] = zz[:, :n]
    sums = [0.0] * 4
    for z, y, b in (
        (zz, yz_ref[...], v[:, :half].astype(F32)),
        (zx, yx_ref[...], v[:, half:].astype(F32)),
    ):
        w = y + noise_level * b
        r = b - a0 * w
        s = noise_level * r + (1.0 - noise_level * a0) * y - a0 * z
        for index, value in enumerate((r * r, r * s, b * s, r * w)):
            sums[index] = sums[index] + total(value)
    sums_ref[...] = columns_of(sums, m)


def last_kernel(
    n, b_ref, yz_ref, z_ref, mine_ref, theirs_ref, mine2_ref, theirs2_ref, x_ref, r_ref
):
    bb, bw, a0 = first_step(mine_ref[...], theirs_ref[...])
    sums = mine2_ref[...] + theirs2_ref[...]
    rr, rs, bs, rw = (sums[:, i : i + 1] for i in range(4))
    beta = rr / bb
    a1 = rr / (rs + beta * (bs + rw) + beta * beta * bw)
    b = b_ref[...]
    y = yz_ref[:, :n]
    r = b - a0 * (y + noise_level * b)
    p = r + beta * b
    image = (1.0 - noise_level * a0 + beta) * y - a0 * z_ref[...] + noise_level * p
    x_ref[...] = a0 * b + a1 * p
    r_ref[...] = r - a1 * image


def pair_body(blocks, points, inv_scale, targets):
    n, depth = points.shape
    m = targets.shape[1]
    own = targets.T

    def along(x, step):
        return lax.ppermute(x, "blk", [(i, i ^ step) for i in range(blocks)])

    def across(x):
        return lax.ppermute(x, "narrow", [(i, i ^ 2) for i in range(4)])

    def swap(x):
        return lax.ppermute(x, "narrow", [(i, i ^ 1) for i in range(4)])

    pack = call(
        pack_kernel, jax.ShapeDtypeStruct((n + 2 * m, depth), BF16), "pack"
    )(points, inv_scale[None, :], own)
    arrived = [pack] + [along(pack, step) for step in range(1, blocks)]
    tz = jnp.concatenate(arrived, axis=0)
    tx = jnp.concatenate([across(p) for p in arrived], axis=0)
    uz = swap(tz)
    ux = swap(tx)
    kzz, yz = tile(n, m, [tz], tz, [], "k_zz")
    kuz, yz = tile(n, m, [uz], tz, [yz], "k_uz")
    kx, yx = tile(n, m, [tz, uz, tx], tx, [], "k_x")
    kxz, yz = tile(n, m, [tx], tz, [yz], "k_xz")
    kux, yz = tile(n, m, [ux], tz, [yz], "k_ux_z")
    kuxx, yx = tile(n, m, [ux], tx, [yx], "k_ux_x")
    cols = yz.shape[1]
    vec = pltpu.VMEM((m, 2 * cols), BF16)
    sums_shape = jax.ShapeDtypeStruct((m, 128), F32)
    y, sums = call(
        functools.partial(join_kernel, n),
        (jax.ShapeDtypeStruct((m, 2 * cols), BF16), sums_shape),
        "join",
        scratch=[vec],
    )(tz, tx, yz, yx)
    yu = swap(y)
    sums_u = swap(sums)
    z, sums2 = call(
        functools.partial(second_kernel, n),
        (jax.ShapeDtypeStruct((m, n), F32), sums_shape),
        "second",
        scratch=[vec],
    )(tz, tx, yz, yx, y, yu, sums, sums_u, kzz, kuz, kxz, kux, kx, kuxx)
    sums2_u = swap(sums2)
    shape = jax.ShapeDtypeStruct((m, n), F32)
    x, r = call(functools.partial(last_kernel, n), (shape, shape), "last")(
        own, yz, z, sums, sums_u, sums2, sums2_u
    )
    return x.T, r.T


def spread_body(points, inv_scale, targets):
    def column_total(values):
        return lax.psum(jnp.sum(values, axis=0), ("blk", "narrow"))

    scaled = (points.astype(F32) * inv_scale[None, :]).astype(BF16)
    rows = lax.all_gather(scaled, "narrow", axis=0, tiled=True)
    columns = lax.all_gather(scaled, "blk", axis=0, tiled=True)
    row_sq = jnp.sum(jnp.square(rows.astype(F32)), axis=1)
    col_sq = jnp.sum(jnp.square(columns.astype(F32)), axis=1)
    inner = lax.dot_general(rows, columns, LAST, preferred_element_type=F32)
    kernel = jnp.exp(-0.5 * (row_sq[:, None] + col_sq[None, :] - 2.0 * inner)).astype(BF16)
    answer = jnp.zeros_like(targets)
    residual = targets
    direction = targets
    norm_now = column_total(residual * residual)
    for step in range(ITERATIONS):
        vector = lax.all_gather(direction.astype(BF16), "blk", axis=0, tiled=True)
        image = jnp.dot(kernel, vector, preferred_element_type=F32)
        image = lax.psum_scatter(image, "narrow", scatter_dimension=0, tiled=True)
        image = image + noise_level * direction
        alpha = norm_now / column_total(direction * image)
        answer = answer + alpha[None, :] * direction
        residual = residual - alpha[None, :] * image
        if step + 1 < ITERATIONS:
            norm_next = column_total(residual * residual)
            direction = residual + (norm_next / norm_now)[None, :] * direction
            norm_now = norm_next
    return answer, residual


def solution(mesh):
    blocks, narrow = mesh.shape["blk"], mesh.shape["narrow"]
    sharded = P(("groups", "blk", "narrow"), None)

    def whole(points, inv_scale, targets):
        fits = narrow == 4 and blocks in (1, 2, 4)
        n = points.shape[0] // mesh.size
        fits = fits and n * blocks <= 1024 and n == 4 * targets.shape[1]
        body = functools.partial(pair_body, blocks) if fits else spread_body
        return jax.shard_map(
            body,
            mesh=mesh,
            in_specs=(sharded, P(), sharded),
            out_specs=(sharded, sharded),
            check_vma=False,
        )(points, inv_scale, targets)

    return whole
```

time: 205 us -> 48.6 us (0.24)
  blocking collectives: 142 us -> 0 us
  waiting for transfers between devices: 39.2 us -> 13.8 us
  Pallas kernels: 0 us -> 19.1 us
  between operations: 14.1 us -> 0.79 us
  starting transfers between devices: 0.08 us -> 12.2 us
  other arithmetic: 5.06 us -> 0.03 us
  matrix products: 3.98 us -> 0 us
  local copies, waits for them, and re-layouts: 0.01 us -> 2.38 us
    psum x3 -> x0, blocking collectives: 93.9 us -> none  [column_total(): return lax.psum(jnp.sum(values, axis=0), ('blk', 'narrow'))]
    all_gather x4 -> x0, blocking collectives: 48.4 us -> none  [the longest x2 27 us: body(): lax.all_gather(vector, 'blk', axis=0, tiled=True)]
    reduce_scatter x2 -> x0, waiting for transfers between devices: 39.2 us -> none  [body(): mine = lax.psum_scatter(total, 'narrow', scatter_dimension=0, tiled=True)]
    pallas_call x0 -> x10, Pallas kernels: none -> 19.1 us  [the longest x6 14.7 us: tile(): call(functools.partial(tile_kernel, n, len(row_packs)), (jax.ShapeDtypeSt...]
    ppermute x0 -> x12, waiting for transfers between devices: none -> 13.8 us  [the longest x3 5.99 us: along(): return lax.ppermute(x, 'blk', [(i, i ^ step) for i in range(blocks)])]
    ppermute x0 -> x12, starting transfers between devices: none -> 12.2 us  [the longest x3 5.76 us: along(): return lax.ppermute(x, 'blk', [(i, i ^ step) for i in range(blocks)])]
    dot_general x3 -> x0, matrix products: 3.98 us -> none  [the longest x2 2.92 us: body(): jnp.dot(tile, lax.all_gather(vector, 'blk', axis=0, tiled=True), preferre...]
    reduce_sum x5 -> x0, other arithmetic: 2.5 us -> none  [the longest x3 2.08 us: column_total(): return lax.psum(jnp.sum(values, axis=0), ('blk', 'narrow'))]
  transfers between devices with their start and end apart: 2 -> 12, of which waited for: 2 -> 5; matrix products, arithmetic and copies ran while one was open for 0% -> 0% of each run, Pallas kernels for 0% -> 22%
where the time goes in v1:
time: 48.6 us; the launch traced here: 48.3 us
  Pallas kernels  19.1 us (39%)
  waiting for transfers between devices  13.8 us (28%)
  starting transfers between devices  12.2 us (25%)
  local copies, waits for them, and re-layouts  2.38 us (5%)
  between operations  0.79 us (2%)
    pallas_call x6, Pallas kernels, tile(): call(functools.partial(tile_kernel, n, len(row_packs)), (jax.ShapeDtypeSt...  14.7 us
    ppermute x3, waiting for transfers between devices, along(): return lax.ppermute(x, 'blk', [(i, i ^ step) for i in range(blocks)])  5.99 us
    ppermute x4, waiting for transfers between devices, across(): return lax.ppermute(x, 'narrow', [(i, i ^ 2) for i in range(4)])  5.83 us
    ppermute x3, starting transfers between devices, along(): return lax.ppermute(x, 'blk', [(i, i ^ step) for i in range(blocks)])  5.76 us
    ppermute x4, starting transfers between devices, across(): return lax.ppermute(x, 'narrow', [(i, i ^ 2) for i in range(4)])  5.22 us
    pallas_call x1, Pallas kernels, pair_body(): call(functools.partial(second_kernel, n), (jax.ShapeDtypeStruct((m, n), F...  3.25 us
    unnamed x9, local copies, waits for them, and re-layouts  2.36 us
    ppermute x5, waiting for transfers between devices, swap(): return lax.ppermute(x, 'narrow', [(i, i ^ 1) for i in range(4)])  2 us
  transfers between devices with their start and end apart: 12, of which 5 were waited for; matrix products, arithmetic and copies ran while one was open for 0% of the time, Pallas kernels for 22%

profile of v1, /device:TPU:0, one launch (start us, length us, event | category | flops | bytes accessed | tf_op | source)
XLA Modules:
  0.0 48.3 jit_solution(4436868037030557616)
XLA Ops:
  0.6 0.0 copy-start
  0.6 0.8 %copy-done = f32[256,64]{0,1:T(8,128)S(1)} copy-done((f32[256,64]{0,1:T(8,128)S(1)}, f32[256,64]{0,1:T(8,128)}, u32[]{:S(2)}) %copy-start) | copy-done | bytes 65560
  1.5 0.0 copy-start.1
  1.5 0.8 %copy-done.1 = bf16[256,128]{1,0:T(8,128)(2,1)S(1)} copy-done((bf16[256,128]{1,0:T(8,128)(2,1)S(1)}, bf16[256,128]{1,0:T(8,128)(2,1)}, u32[]{:S(2)}) %copy-start.1) | copy-done | bytes 65560
  2.3 0.0 copy-start.2
  2.3 0.7 %copy-done.2 = f32[128]{0:T(128)S(1)} copy-done((f32[128]{0:T(128)S(1)}, f32[128]{0:T(128)}, u32[]{:S(2)}) %copy-start.2) | copy-done | bytes 536
  3.0 5.1 %collective-permute-start.5 = (bf16[384,128]{1,0:T(8,128)(2,1)S(1)}, bf16[384,128]{1,0:T(8,128)(2,1)S(1)}, u32[]{:S(2)}, u32[]{:S(2)}) collective-permute-start(bf16[384,128]{1,0:T(8,128)(2,1)S(1)} %pack.1), channel_id=1, source_target_pairs={{0,12},{4,8},{8,4},{12,0},{1,13},{5,9},{9,5},{13,1},{2,14},{6,10},... | collective-permute-start | bytes 294920 | tf_op jit(solution)/shard_map/ppermute | solution.py:217
  8.1 0.0 collective-permute-start.3
  8.1 0.6 %collective-permute-start.1 = (bf16[384,128]{1,0:T(8,128)(2,1)S(1)}, bf16[384,128]{1,0:T(8,128)(2,1)S(1)}, u32[]{:S(2)}, u32[]{:S(2)}) collective-permute-start(bf16[384,128]{1,0:T(8,128)(2,1)S(1)} %pack.1), channel_id=1, source_target_pairs={{0,4},{4,0},{8,12},{12,8},{1,5},{5,1},{9,13},{13,9},{2,6},{6,2},{1... | collective-permute-start | bytes 294920 | tf_op jit(solution)/shard_map/ppermute | solution.py:217
  8.7 1.6 %collective-permute-start = (bf16[384,128]{1,0:T(8,128)(2,1)S(1)}, bf16[384,128]{1,0:T(8,128)(2,1)S(1)}, u32[]{:S(2)}, u32[]{:S(2)}) collective-permute-start(bf16[384,128]{1,0:T(8,128)(2,1)S(1)} %pack.1), channel_id=1, source_target_pairs={{0,2},{1,3},{2,0},{3,1},{4,6},{5,7},{6,4},{7,5},{8,10},{9,11},{10,... | collective-permute-start | bytes 294920 | tf_op jit(solution)/shard_map/ppermute | solution.py:220
  10.4 1.4 %collective-permute-done.5 = bf16[384,128]{1,0:T(8,128)(2,1)S(1)} collective-permute-done((bf16[384,128]{1,0:T(8,128)(2,1)S(1)}, bf16[384,128]{1,0:T(8,128)(2,1)S(1)}, u32[]{:S(2)}, u32[]{:S(2)}) %collective-permute-start.5) | collective-permute-done | bytes 98336 | tf_op jit(solution)/shard_map/ppermute | solution.py:217
  11.8 4.6 %collective-permute-done.3 = bf16[384,128]{1,0:T(8,128)(2,1)S(1)} collective-permute-done((bf16[384,128]{1,0:T(8,128)(2,1)S(1)}, bf16[384,128]{1,0:T(8,128)(2,1)S(1)}, u32[]{:S(2)}, u32[]{:S(2)}) %collective-permute-start.3) | collective-permute-done | bytes 98336 | tf_op jit(solution)/shard_map/ppermute | solution.py:217
  16.4 0.0 collective-permute-done.1
  16.4 0.1 collective-permute-start.8
  16.5 1.6 %collective-permute-start.6 = (bf16[384,128]{1,0:T(8,128)(2,1)S(1)}, bf16[384,128]{1,0:T(8,128)(2,1)S(1)}, u32[]{:S(2)}, u32[]{:S(2)}) collective-permute-start(bf16[384,128]{1,0:T(8,128)(2,1)S(1)} %collective-permute-done.5), channel_id=1, source_target_pairs={{0,2},{1,3},{2,0},{3,1},{4,6},{5,7},{6,4},{7,5},{8,10},{9,11},{10,... | collective-permute-start | bytes 294920 | tf_op jit(solution)/shard_map/ppermute | solution.py:220
  18.0 0.5 %collective-permute-start.4 = (bf16[384,128]{1,0:T(8,128)(2,1)S(1)}, bf16[384,128]{1,0:T(8,128)(2,1)S(1)}, u32[]{:S(2)}, u32[]{:S(2)}) collective-permute-start(bf16[384,128]{1,0:T(8,128)(2,1)S(1)} %collective-permute-done.3), channel_id=1, source_target_pairs={{0,2},{1,3},{2,0},{3,1},{4,6},{5,7},{6,4},{7,5},{8,10},{9,11},{10,... | collective-permute-start | bytes 294920 | tf_op jit(solution)/shard_map/ppermute | solution.py:220
  18.6 1.5 %collective-permute-start.2 = (bf16[384,128]{1,0:T(8,128)(2,1)S(1)}, bf16[384,128]{1,0:T(8,128)(2,1)S(1)}, u32[]{:S(2)}, u32[]{:S(2)}) collective-permute-start(bf16[384,128]{1,0:T(8,128)(2,1)S(1)} %collective-permute-done.1), channel_id=1, source_target_pairs={{0,2},{1,3},{2,0},{3,1},{4,6},{5,7},{6,4},{7,5},{8,10},{9,11},{10,... | collective-permute-start | bytes 294920 | tf_op jit(solution)/shard_map/ppermute | solution.py:220
  20.1 0.0 collective-permute-done
  20.1 5.8 %collective-permute-done.2 = bf16[384,128]{1,0:T(8,128)(2,1)S(1)} collective-permute-done((bf16[384,128]{1,0:T(8,128)(2,1)S(1)}, bf16[384,128]{1,0:T(8,128)(2,1)S(1)}, u32[]{:S(2)}, u32[]{:S(2)}) %collective-permute-start.2) | collective-permute-done | bytes 98336 | tf_op jit(solution)/shard_map/ppermute | solution.py:220
  25.9 0.0 collective-permute-done.4
  26.0 0.0 collective-permute-done.6
  26.0 0.1 collective-permute-start.7
  26.1 1.9 %k_zz.1 = (bf16[1024,1024]{1,0:T(8,128)(2,1)S(1)}, f32[64,1024]{1,0:T(8,128)S(1)}) custom-call(bf16[1536,128]{1,0:T(8,128)(2,1)S(1)} %pad_maximum_fusion.refs_0_.refs_1_.tz_ref, bf16[1536,128]{1,0:T(8,128)(2,1)S(1)} %pad_maximum_fusion.refs_0_.refs_1_.tz_ref), custom_call_target="tpu_custom_call" | custom-call | flops 671088640 | bytes 2097152 | tf_op jit(solution)/shard_map/k_zz/pallas_call | solution.py:117
  28.0 0.0 collective-permute-done.8.refs_0_.refs_1_
  28.0 1.9 %k_uz.1 = (bf16[1024,1024]{1,0:T(8,128)(2,1)S(1)}, f32[64,1024]{1,0:T(8,128)S(1)}) custom-call(bf16[1536,128]{1,0:T(8,128)(2,1)S(1)} %collective-permute-done.8.refs_0_.refs_1_, bf16[1536,128]{1,0:T(8,128)(2,1)S(1)} %pad_maximum_fusion.refs_0_.refs_1_.tz_ref, f32[64,1024]{1,0:T(8,128)S(1)} %get-tuple-element.20.refs_2_), custom_call_target="tpu_custom_call" | custom-call | flops 671088640 | bytes 2097152 | tf_op jit(solution)/shard_map/k_uz/pallas_call | solution.py:117
  30.0 1.9 %k_xz.1 = (bf16[1024,1024]{1,0:T(8,128)(2,1)S(1)}, f32[64,1024]{1,0:T(8,128)S(1)}) custom-call(bf16[1536,128]{1,0:T(8,128)(2,1)S(1)} %constant_dynamic-update-slice_fusion.refs_0_.refs_2_.refs_3_.refs_1_.tx_ref, bf16[1536,128]{1,0:T(8,128)(2,1)S(1)} %pad_maximum_fusion.refs_0_.refs_1_.tz_ref, f32[64,1024]{1,0:T(8,128)S(1)} %get-tuple-element.21.refs_2_), custom_call_target="tpu_custom_call" | custom-call | flops 671088640 | bytes 2097152 | tf_op jit(solution)/shard_map/k_xz/pallas_call | solution.py:117
  31.9 5.0 %k_x.1 = (bf16[3072,1024]{1,0:T(8,128)(2,1)S(1)}, f32[64,1024]{1,0:T(8,128)S(1)}) custom-call(bf16[1536,128]{1,0:T(8,128)(2,1)S(1)} %pad_maximum_fusion.refs_0_.refs_1_.tz_ref, bf16[1536,128]{1,0:T(8,128)(2,1)S(1)} %collective-permute-done.8.refs_0_.refs_1_, bf16[1536,128]{1,0:T(8,128)(2,1)S(1)} %constant_dynamic-update-slice_fusion.refs_0_.refs_2_.refs_3_.refs_1_.tx_ref, ...), custom_call_target="tpu_custom_call" | custom-call | flops 2013265920 | bytes 6291456 | tf_op jit(solution)/shard_map/k_x/pallas_call | solution.py:117
  36.9 0.0 collective-permute-done.7.refs_0_
  36.9 1.9 %k_ux_z.1 = (bf16[1024,1024]{1,0:T(8,128)(2,1)S(1)}, f32[64,1024]{1,0:T(8,128)S(1)}) custom-call(bf16[1536,128]{1,0:T(8,128)(2,1)S(1)} %collective-permute-done.7.refs_0_, bf16[1536,128]{1,0:T(8,128)(2,1)S(1)} %pad_maximum_fusion.refs_0_.refs_1_.tz_ref, f32[64,1024]{1,0:T(8,128)S(1)} %get-tuple-element.22.refs_2_), custom_call_target="tpu_custom_call" | custom-call | flops 671088640 | bytes 2097152 | tf_op jit(solution)/shard_map/k_ux_z/pallas_call | solution.py:117
  38.9 1.9 %k_ux_x.1 = (bf16[1024,1024]{1,0:T(8,128)(2,1)S(1)}, f32[64,1024]{1,0:T(8,128)S(1)}) custom-call(bf16[1536,128]{1,0:T(8,128)(2,1)S(1)} %collective-permute-done.7.refs_0_, bf16[1536,128]{1,0:T(8,128)(2,1)S(1)} %constant_dynamic-update-slice_fusion.refs_0_.refs_2_.refs_3_.refs_1_.tx_ref, f32[64,1024]{1,0:T(8,128)S(1)} %get-tuple-element.24.refs_2_), custom_call_target="tpu_custom_call" | custom-call | flops 671088640 | bytes 2097152 | tf_op jit(solution)/shard_map/k_ux_x/pallas_call | solution.py:117
  40.8 0.2 join.1
  41.0 0.6 %collective-permute-start.9 = (bf16[64,2048]{1,0:T(8,128)(2,1)S(1)}, bf16[64,2048]{1,0:T(8,128)(2,1)S(1)}, u32[]{:S(2)}, u32[]{:S(2)}) collective-permute-start(bf16[64,2048]{1,0:T(8,128)(2,1)S(1)} %get-tuple-element.26.y_ref), channel_id=1, source_target_pairs={{0,1},{1,0},{2,3},{3,2},{4,5},{5,4},{6,7},{7,6},{8,9},{9,8},{10,11... | collective-permute-start | bytes 786440 | tf_op jit(solution)/shard_map/ppermute | solution.py:223
  41.6 0.1 collective-permute-start.10
  41.6 1.1 %collective-permute-done.10.theirs_ref = f32[64,128]{1,0:T(8,128)S(1)} collective-permute-done((f32[64,128]{1,0:T(8,128)S(1)}, f32[64,128]{1,0:T(8,128)S(1)}, u32[]{:S(2)}, u32[]{:S(2)}) %collective-permute-start.10) | collective-permute-done | bytes 32800 | tf_op jit(solution)/shard_map/ppermute | solution.py:223
  42.8 0.0 collective-permute-done.9.yu_ref
  42.8 3.3 %second.1 = (f32[64,256]{1,0:T(8,128)S(1)}, f32[64,128]{1,0:T(8,128)S(1)}) custom-call(bf16[1536,128]{1,0:T(8,128)(2,1)S(1)} %pad_maximum_fusion.refs_0_.refs_1_.tz_ref, bf16[1536,128]{1,0:T(8,128)(2,1)S(1)} %constant_dynamic-update-slice_fusion.refs_0_.refs_2_.refs_3_.refs_1_.tx_ref, f32[64,1024]{1,0:T(8,128)S(1)} %get-tuple-element.23.yz_ref, ...), custom_call_target="tpu_custom_call" | custom-call | tf_op jit(solution)/shard_map/second/pallas_call | solution.py:250
  46.0 0.4 collective-permute-start.11
  46.5 0.9 %collective-permute-done.11.theirs2_ref = f32[64,128]{1,0:T(8,128)S(1)} collective-permute-done((f32[64,128]{1,0:T(8,128)S(1)}, f32[64,128]{1,0:T(8,128)S(1)}, u32[]{:S(2)}, u32[]{:S(2)}) %collective-permute-start.11) | collective-permute-done | bytes 32800 | tf_op jit(solution)/shard_map/ppermute | solution.py:223
  47.3 1.0 %last.1 = (f32[64,256]{1,0:T(8,128)}, f32[64,256]{1,0:T(8,128)}) custom-call(f32[64,256]{1,0:T(8,128)S(1)} %bitcast.5, f32[64,1024]{1,0:T(8,128)S(1)} %get-tuple-element.23.yz_ref, f32[64,256]{1,0:T(8,128)S(1)} %get-tuple-element.34.z_ref, f32[64,128]{1,0:T(8,128)S(1)} %get-tuple-element.27.mine_ref, f32[64,128]{1,0:T(8,128)S(1)} %collective-permute-done.10.theirs_ref, ...), custom_call_target="tpu_custom_call" | custom-call | tf_op jit(solution)/shard_map/last/pallas_call | solution.py:258
  (6 shorter events, 0.1 us)
Async XLA Ops:
  0.6 0.8 %copy-start = (f32[256,64]{0,1:T(8,128)S(1)}, f32[256,64]{0,1:T(8,128)}, u32[]{:S(2)}) copy-start(f32[256,64]{0,1:T(8,128)} %param.5) | copy-start | bytes 196612
  1.5 0.8 %copy-start.1 = (bf16[256,128]{1,0:T(8,128)(2,1)S(1)}, bf16[256,128]{1,0:T(8,128)(2,1)}, u32[]{:S(2)}) copy-start(bf16[256,128]{1,0:T(8,128)(2,1)} %points_ref.1) | copy-start | bytes 196612
  2.3 0.7 %copy-start.2 = (f32[128]{0:T(128)S(1)}, f32[128]{0:T(128)}, u32[]{:S(2)}) copy-start(f32[128]{0:T(128)} %param.4) | copy-start | bytes 1540
  3.0 8.8 %collective-permute-start.5 = (bf16[384,128]{1,0:T(8,128)(2,1)S(1)}, bf16[384,128]{1,0:T(8,128)(2,1)S(1)}, u32[]{:S(2)}, u32[]{:S(2)}) collective-permute-start(bf16[384,128]{1,0:T(8,128)(2,1)S(1)} %pack.1), channel_id=1, source_target_pairs={{0,12},{4,8},{8,4},{12,0},{1,13},{5,9},{9,5},{13,1},{2,14},{6,10},... | collective-permute-start | bytes 294920 | tf_op jit(solution)/shard_map/ppermute | solution.py:217
  8.1 8.3 %collective-permute-start.3 = (bf16[384,128]{1,0:T(8,128)(2,1)S(1)}, bf16[384,128]{1,0:T(8,128)(2,1)S(1)}, u32[]{:S(2)}, u32[]{:S(2)}) collective-permute-start(bf16[384,128]{1,0:T(8,128)(2,1)S(1)} %pack.1), channel_id=1, source_target_pairs={{0,8},{4,12},{8,0},{12,4},{1,9},{5,13},{9,1},{13,5},{2,10},{6,14},... | collective-permute-start | bytes 294920 | tf_op jit(solution)/shard_map/ppermute | solution.py:217
  8.1 8.3 %collective-permute-start.1 = (bf16[384,128]{1,0:T(8,128)(2,1)S(1)}, bf16[384,128]{1,0:T(8,128)(2,1)S(1)}, u32[]{:S(2)}, u32[]{:S(2)}) collective-permute-start(bf16[384,128]{1,0:T(8,128)(2,1)S(1)} %pack.1), channel_id=1, source_target_pairs={{0,4},{4,0},{8,12},{12,8},{1,5},{5,1},{9,13},{13,9},{2,6},{6,2},{1... | collective-permute-start | bytes 294920 | tf_op jit(solution)/shard_map/ppermute | solution.py:217
  8.7 11.3 %collective-permute-start = (bf16[384,128]{1,0:T(8,128)(2,1)S(1)}, bf16[384,128]{1,0:T(8,128)(2,1)S(1)}, u32[]{:S(2)}, u32[]{:S(2)}) collective-permute-start(bf16[384,128]{1,0:T(8,128)(2,1)S(1)} %pack.1), channel_id=1, source_target_pairs={{0,2},{1,3},{2,0},{3,1},{4,6},{5,7},{6,4},{7,5},{8,10},{9,11},{10,... | collective-permute-start | bytes 294920 | tf_op jit(solution)/shard_map/ppermute | solution.py:220
  16.4 11.6 %collective-permute-start.8 = (bf16[1536,128]{1,0:T(8,128)(2,1)S(1)}, bf16[1536,128]{1,0:T(8,128)(2,1)S(1)}, u32[]{:S(2)}, u32[]{:S(2)}) collective-permute-start(bf16[1536,128]{1,0:T(8,128)(2,1)S(1)} %pad_maximum_fusion.refs_0_.refs_1_.tz_ref), channel_id=1, source_target_pairs={{0,1},{1,0},{2,3},{3,2},{4,5},{5,4},{6,7},{7,6},{8,9},{9,8},{10,11... | collective-permute-start | bytes 1179656 | tf_op jit(solution)/shard_map/ppermute | solution.py:223
  16.5 9.5 %collective-permute-start.6 = (bf16[384,128]{1,0:T(8,128)(2,1)S(1)}, bf16[384,128]{1,0:T(8,128)(2,1)S(1)}, u32[]{:S(2)}, u32[]{:S(2)}) collective-permute-start(bf16[384,128]{1,0:T(8,128)(2,1)S(1)} %collective-permute-done.5), channel_id=1, source_target_pairs={{0,2},{1,3},{2,0},{3,1},{4,6},{5,7},{6,4},{7,5},{8,10},{9,11},{10,... | collective-permute-start | bytes 294920 | tf_op jit(solution)/shard_map/ppermute | solution.py:220
  18.0 7.9 %collective-permute-start.4 = (bf16[384,128]{1,0:T(8,128)(2,1)S(1)}, bf16[384,128]{1,0:T(8,128)(2,1)S(1)}, u32[]{:S(2)}, u32[]{:S(2)}) collective-permute-start(bf16[384,128]{1,0:T(8,128)(2,1)S(1)} %collective-permute-done.3), channel_id=1, source_target_pairs={{0,2},{1,3},{2,0},{3,1},{4,6},{5,7},{6,4},{7,5},{8,10},{9,11},{10,... | collective-permute-start | bytes 294920 | tf_op jit(solution)/shard_map/ppermute | solution.py:220
  18.6 7.3 %collective-permute-start.2 = (bf16[384,128]{1,0:T(8,128)(2,1)S(1)}, bf16[384,128]{1,0:T(8,128)(2,1)S(1)}, u32[]{:S(2)}, u32[]{:S(2)}) collective-permute-start(bf16[384,128]{1,0:T(8,128)(2,1)S(1)} %collective-permute-done.1), channel_id=1, source_target_pairs={{0,2},{1,3},{2,0},{3,1},{4,6},{5,7},{6,4},{7,5},{8,10},{9,11},{10,... | collective-permute-start | bytes 294920 | tf_op jit(solution)/shard_map/ppermute | solution.py:220
  26.0 10.9 %collective-permute-start.7 = (bf16[1536,128]{1,0:T(8,128)(2,1)S(1)}, bf16[1536,128]{1,0:T(8,128)(2,1)S(1)}, u32[]{:S(2)}, u32[]{:S(2)}) collective-permute-start(bf16[1536,128]{1,0:T(8,128)(2,1)S(1)} %constant_dynamic-update-slice_fusion.refs_0_.refs_2_.refs_3_.refs_1_.tx_ref), channel_id=1, source_target_pairs={{0,1},{1,0},{2,3},{3,2},{4,5},{5,4},{6,7},{7,6},{8,9},{9,8},{10,11... | collective-permute-start | bytes 1179656 | tf_op jit(solution)/shard_map/ppermute | solution.py:223
  41.0 1.8 %collective-permute-start.9 = (bf16[64,2048]{1,0:T(8,128)(2,1)S(1)}, bf16[64,2048]{1,0:T(8,128)(2,1)S(1)}, u32[]{:S(2)}, u32[]{:S(2)}) collective-permute-start(bf16[64,2048]{1,0:T(8,128)(2,1)S(1)} %get-tuple-element.26.y_ref), channel_id=1, source_target_pairs={{0,1},{1,0},{2,3},{3,2},{4,5},{5,4},{6,7},{7,6},{8,9},{9,8},{10,11... | collective-permute-start | bytes 786440 | tf_op jit(solution)/shard_map/ppermute | solution.py:223
  41.6 1.2 %collective-permute-start.10 = (f32[64,128]{1,0:T(8,128)S(1)}, f32[64,128]{1,0:T(8,128)S(1)}, u32[]{:S(2)}, u32[]{:S(2)}) collective-permute-start(f32[64,128]{1,0:T(8,128)S(1)} %get-tuple-element.27.mine_ref), channel_id=1, source_target_pairs={{0,1},{1,0},{2,3},{3,2},{4,5},{5,4},{6,7},{7,6},{8,9},{9,8},{10,11... | collective-permute-start | bytes 98312 | tf_op jit(solution)/shard_map/ppermute | solution.py:223
  46.0 1.3 %collective-permute-start.11 = (f32[64,128]{1,0:T(8,128)S(1)}, f32[64,128]{1,0:T(8,128)S(1)}, u32[]{:S(2)}, u32[]{:S(2)}) collective-permute-start(f32[64,128]{1,0:T(8,128)S(1)} %get-tuple-element.35.mine2_ref), channel_id=1, source_target_pairs={{0,1},{1,0},{2,3},{3,2},{4,5},{5,4},{6,7},{7,6},{8,9},{9,8},{10,11... | collective-permute-start | bytes 98312 | tf_op jit(solution)/shard_map/ppermute | solution.py:223

commit v2 on v1

v2 whole, which is shorter than its diff:
```python
import functools

import jax
import jax.numpy as jnp
from jax import lax
from jax.experimental import pallas as pl
from jax.experimental.pallas import tpu as pltpu
from jax.sharding import PartitionSpec as P

ITERATIONS = 2
noise_level = 1.0

BF16 = jnp.bfloat16
F32 = jnp.float32
LAST = (((1,), (1,)), ((), ()))
VMEM = pl.BlockSpec(memory_space=pltpu.VMEM)
LIMIT = 20 * 2**20


def call(kernel, outs, name, flops=0, exps=0, bytes_=0, scratch=(), ins=None):
    return pl.pallas_call(
        kernel,
        **({} if ins is None else {"in_specs": ins}),
        out_shape=outs,
        out_specs=jax.tree.map(lambda _: VMEM, outs),
        scratch_shapes=list(scratch),
        name=name,
        cost_estimate=pl.CostEstimate(
            flops=flops, bytes_accessed=bytes_, transcendentals=exps
        ),
        compiler_params=pltpu.CompilerParams(vmem_limit_bytes=LIMIT),
    )


def pack_kernel(points_hbm, scale_hbm, targets_hbm, pack_ref, points_ref, scale_ref, targets_ref, sems):
    copies = [
        pltpu.make_async_copy(source, target, sems.at[index])
        for index, (source, target) in enumerate(
            ((points_hbm, points_ref), (scale_hbm, scale_ref), (targets_hbm, targets_ref))
        )
    ]
    for copy in copies:
        copy.start()
    for copy in copies:
        copy.wait()
    n = points_ref.shape[0]
    half = n // 2
    m = targets_ref.shape[0]
    pack_ref[:n] = (points_ref[...].astype(F32) * scale_ref[...]).astype(BF16)
    pack_ref[n : n + m] = targets_ref[:, :half].astype(BF16)
    pack_ref[n + m :] = targets_ref[:, half:].astype(BF16)


def exponents(points, first):
    n, depth = points.shape
    value = -0.5 * jnp.sum(jnp.square(points.astype(F32)), axis=1, keepdims=True)
    high = value.astype(BF16).astype(F32)
    rest = value - high
    middle = rest.astype(BF16).astype(F32)
    low = rest - middle
    lane = lax.broadcasted_iota(jnp.int32, (n, depth), 1) - first
    other = lax.broadcasted_iota(jnp.int32, (n, depth), 1) - (3 - first)
    ones = jnp.where((other >= 0) & (other < 3), 1.0, 0.0)
    terms = jnp.where(lane == 0, high, jnp.where(lane == 1, middle, jnp.where(lane == 2, low, ones)))
    return terms.astype(BF16)


def fill(packs, n, first, out):
    depth = packs[0].shape[1]
    at = 0
    for ref in packs:
        for block in range(ref.shape[0] * 2 // (3 * n)):
            start = block * (n * 3 // 2)
            points = ref[start : start + n]
            out[at : at + n, :depth] = points
            out[at : at + n, depth:] = exponents(points, first)
            at += n


def vectors(packs, n, out):
    at = 0
    for ref in packs:
        for block in range(ref.shape[0] * 2 // (3 * n)):
            start = block * (n * 3 // 2) + n
            m = n // 4
            for part in range(2):
                out[:, at : at + n // 2] = ref[start + part * m : start + (part + 1) * m]
                at += n // 2


def tile(a, b):
    return jnp.exp(lax.dot_general(a, b, LAST, preferred_element_type=F32)).astype(BF16)


def across_rows(v, k):
    return jnp.dot(v, k, preferred_element_type=F32)


def across_columns(v, k):
    return lax.dot_general(v, k, LAST, preferred_element_type=F32)


def early_kernel(n, z_ref, x_ref, a_ref, b_ref, v_ref, k_ref, y_ref):
    fill([z_ref, x_ref], n, 0, a_ref)
    fill([z_ref, x_ref], n, 3, b_ref)
    vectors([z_ref, x_ref], n, v_ref)
    k_ref[...] = tile(a_ref[...], b_ref[...])
    y_ref[...] = across_rows(v_ref[...], k_ref[...])


def early_other_kernel(n, u_ref, b_ref, y0_ref, a_ref, v_ref, k_ref, y_ref):
    fill([u_ref], n, 0, a_ref)
    vectors([u_ref], n, v_ref)
    k_ref[...] = tile(a_ref[...], b_ref[...])
    y_ref[...] = y0_ref[...] + across_rows(v_ref[...], k_ref[...])


def late_kernel(
    n, x_ref, ae_ref, au_ref, ve_ref, vu_ref, y0_ref, b_ref, v_ref, k_ref, ye_ref, yl_ref, a
):
    fill([x_ref], n, 0, a)
    fill([x_ref], n, 3, b_ref)
    vectors([x_ref], n, v_ref)
    early = ae_ref.shape[0]
    b = b_ref[...]
    k_ref[:early] = tile(ae_ref[...], b)
    k_ref[early : 2 * early] = tile(au_ref[...], b)
    k_ref[2 * early :] = tile(a[...], b)
    ye_ref[...] = y0_ref[...] + across_columns(v_ref[...], k_ref[:early])
    yl_ref[...] = (
        across_rows(ve_ref[...], k_ref[:early])
        + across_rows(vu_ref[...], k_ref[early : 2 * early])
        + across_rows(v_ref[...], k_ref[2 * early :])
    )


def columns_of(pieces, m):
    lane = lax.broadcasted_iota(jnp.int32, (m, 128), 1)
    out = jnp.zeros((m, 128), F32)
    for index, piece in enumerate(pieces):
        out = jnp.where(lane == index, piece, out)
    return out


def total(values):
    return jnp.sum(values, axis=1, keepdims=True)


def late_other_kernel(
    n, u_ref, be_ref, bl_ref, ve_ref, vl_ref, ye_ref, yl_ref,
    k_ref, y_ref, round_ref, sums_ref, a, v,
):
    fill([u_ref], n, 0, a)
    vectors([u_ref], n, v)
    early = be_ref.shape[0]
    k_ref[:, :early] = tile(a[...], be_ref[...])
    k_ref[:, early:] = tile(a[...], bl_ref[...])
    ye = ye_ref[...] + across_rows(v[...], k_ref[:, :early])
    yl = yl_ref[...] + across_rows(v[...], k_ref[:, early:])
    y_ref[:, :early] = ye
    y_ref[:, early:] = yl
    round_ref[:, :early] = ye.astype(BF16)
    round_ref[:, early:] = yl.astype(BF16)
    be = ve_ref[...].astype(F32)
    bl = vl_ref[...].astype(F32)
    sums_ref[...] = columns_of(
        [total(be * be) + total(bl * bl), total(be * ye) + total(bl * yl)], v.shape[0]
    )


def near_kernel(y_ref, ke_ref, kl_ref, z_ref):
    early = ke_ref.shape[0]
    ye, yl = y_ref[:, :early], y_ref[:, early:]
    z_ref[:, :early] = across_rows(ye, ke_ref[...]) + across_columns(yl, kl_ref[:early])
    z_ref[:, early:] = across_rows(ye, kl_ref[:early]) + across_rows(yl, kl_ref[2 * early :])


def first_step(mine, others):
    bb = mine[:, 0:1] + others[:, 0:1]
    by = mine[:, 1:2] + others[:, 1:2]
    bw = by + noise_level * bb
    return bb, bw, bb / bw


def far_kernel(
    n, y_ref, yu_ref, near_ref, mine_ref, theirs_ref, ve_ref, vl_ref, keu_ref, kl_ref, ku_ref,
    z_ref, sums_ref,
):
    early = keu_ref.shape[0]
    _, _, a0 = first_step(mine_ref[...], theirs_ref[...])
    ue, ul = yu_ref[:, :early], yu_ref[:, early:]
    ze = near_ref[:, :early] + across_rows(ue, keu_ref[...]) + across_rows(ul, ku_ref[:, :early])
    zl = (
        near_ref[:, early:]
        + across_rows(ue, kl_ref[early : 2 * early])
        + across_rows(ul, ku_ref[:, early:])
    )
    z_ref[...] = ze[:, :n]
    sums = [0.0] * 4
    for z, y, v in ((ze, y_ref[:, :early], ve_ref), (zl, y_ref[:, early:], vl_ref)):
        b = v[...].astype(F32)
        w = y + noise_level * b
        r = b - a0 * w
        s = noise_level * r + (1.0 - noise_level * a0) * y - a0 * z
        for index, value in enumerate((r * r, r * s, b * s, r * w)):
            sums[index] = sums[index] + total(value)
    sums_ref[...] = columns_of(sums, y_ref.shape[0])


def last_kernel(
    n, b_ref, y_ref, z_ref, mine_ref, theirs_ref, mine2_ref, theirs2_ref, x_ref, r_ref
):
    bb, bw, a0 = first_step(mine_ref[...], theirs_ref[...])
    sums = mine2_ref[...] + theirs2_ref[...]
    rr, rs, bs, rw = (sums[:, i : i + 1] for i in range(4))
    beta = rr / bb
    a1 = rr / (rs + beta * (bs + rw) + beta * beta * bw)
    b = b_ref[...]
    y = y_ref[:, :n]
    r = b - a0 * (y + noise_level * b)
    p = r + beta * b
    image = (1.0 - noise_level * a0 + beta) * y - a0 * z_ref[...] + noise_level * p
    x_ref[...] = a0 * b + a1 * p
    r_ref[...] = r - a1 * image


def pair_body(points, inv_scale, targets):
    n, depth = points.shape
    m = targets.shape[1]
    own = targets.T
    early, late = 6 * n, 2 * n

    def along(x, step):
        return lax.ppermute(x, "blk", [(i, i ^ step) for i in range(4)])

    def across(x):
        return lax.ppermute(x, "narrow", [(i, i ^ 2) for i in range(4)])

    def swap(x):
        return lax.ppermute(x, "narrow", [(i, i ^ 1) for i in range(4)])

    def f32(*shape):
        return jax.ShapeDtypeStruct(shape, F32)

    def bf16(*shape):
        return jax.ShapeDtypeStruct(shape, BF16)

    def named(kernel, outs, name, tiles=0, scratch=()):
        return call(
            functools.partial(kernel, n), outs, name,
            flops=tiles * (4 * depth + 2 * m), exps=tiles, bytes_=2 * tiles, scratch=scratch,
        )

    pack = call(
        pack_kernel, bf16(n + 2 * m, depth), "pack",
        scratch=[
            pltpu.VMEM((n, depth), BF16), pltpu.VMEM((1, depth), F32), pltpu.VMEM((m, n), F32),
            pltpu.SemaphoreType.DMA((3,)),
        ],
        ins=[pl.BlockSpec(memory_space=pltpu.HBM)] * 3,
    )(points, inv_scale[None, :], own)
    far = [along(pack, 3), along(pack, 2)]
    next_ = along(pack, 1)
    x_own = across(pack)
    x_next = across(next_)
    late_z = jnp.concatenate(far, axis=0)
    late_x = across(late_z)
    z_all = jnp.concatenate([pack, next_, late_z], axis=0)
    early_x = jnp.concatenate([x_own, x_next], axis=0)
    early_u = swap(jnp.concatenate([z_all, early_x], axis=0))
    a_e, b_e, v_e, k_e, y_e = named(
        early_kernel,
        (bf16(early, 2 * depth), bf16(early, 2 * depth), bf16(m, early), bf16(early, early), f32(m, early)),
        "early", early * early,
    )(z_all, early_x)
    a_u, v_u, k_eu, y_e = named(
        early_other_kernel,
        (bf16(early, 2 * depth), bf16(m, early), bf16(early, early), f32(m, early)),
        "early_other", early * early,
    )(early_u, b_e, y_e)
    late_x, y_e = lax.optimization_barrier((late_x, y_e))
    late_u = swap(late_x)
    b_l, v_l, k_l, y_e, y_l = named(
        late_kernel,
        (bf16(late, 2 * depth), bf16(m, late), bf16(2 * early + late, late), f32(m, early), f32(m, late)),
        "late", (2 * early + late) * late,
        scratch=[pltpu.VMEM((late, 2 * depth), BF16)],
    )(late_x, a_e, a_u, v_e, v_u, y_e)
    k_u, y, y_round, sums = named(
        late_other_kernel,
        (bf16(late, early + late), f32(m, early + late), bf16(m, early + late), f32(m, 128)),
        "late_other", late * (early + late),
        scratch=[pltpu.VMEM((late, 2 * depth), BF16), pltpu.VMEM((m, late), BF16)],
    )(late_u, b_e, b_l, v_e, v_l, y_e, y_l)
    y_u = swap(y_round)
    sums_u = swap(sums)
    near = call(
        near_kernel, f32(m, early + late), "near", flops=2 * m * (early + late) ** 2
    )(y_round, k_e, k_l)
    z, sums2 = named(far_kernel, (f32(m, n), f32(m, 128)), "far")(
        y, y_u, near, sums, sums_u, v_e, v_l, k_eu, k_l, k_u
    )
    sums2_u = swap(sums2)
    x, r = named(last_kernel, (f32(m, n), f32(m, n)), "last")(
        own, y, z, sums, sums_u, sums2, sums2_u
    )
    return x.T, r.T


def spread_body(points, inv_scale, targets):
    def column_total(values):
        return lax.psum(jnp.sum(values, axis=0), ("blk", "narrow"))

    scaled = (points.astype(F32) * inv_scale[None, :]).astype(BF16)
    rows = lax.all_gather(scaled, "narrow", axis=0, tiled=True)
    columns = lax.all_gather(scaled, "blk", axis=0, tiled=True)
    row_sq = jnp.sum(jnp.square(rows.astype(F32)), axis=1)
    col_sq = jnp.sum(jnp.square(columns.astype(F32)), axis=1)
    inner = lax.dot_general(rows, columns, LAST, preferred_element_type=F32)
    kernel = jnp.exp(-0.5 * (row_sq[:, None] + col_sq[None, :] - 2.0 * inner)).astype(BF16)
    answer = jnp.zeros_like(targets)
    residual = targets
    direction = targets
    norm_now = column_total(residual * residual)
    for step in range(ITERATIONS):
        vector = lax.all_gather(direction.astype(BF16), "blk", axis=0, tiled=True)
        image = jnp.dot(kernel, vector, preferred_element_type=F32)
        image = lax.psum_scatter(image, "narrow", scatter_dimension=0, tiled=True)
        image = image + noise_level * direction
        alpha = norm_now / column_total(direction * image)
        answer = answer + alpha[None, :] * direction
        residual = residual - alpha[None, :] * image
        if step + 1 < ITERATIONS:
            norm_next = column_total(residual * residual)
            direction = residual + (norm_next / norm_now)[None, :] * direction
            norm_now = norm_next
    return answer, residual


def solution(mesh):
    blocks, narrow = mesh.shape["blk"], mesh.shape["narrow"]
    sharded = P(("groups", "blk", "narrow"), None)

    def whole(points, inv_scale, targets):
        n = points.shape[0] // mesh.size
        fits = narrow == 4 and blocks == 4 and n <= 256 and n == 4 * targets.shape[1]
        body = pair_body if fits else spread_body
        return jax.shard_map(
            body,
            mesh=mesh,
            in_specs=(sharded, P(), sharded),
            out_specs=(sharded, sharded),
            check_vma=False,
        )(points, inv_scale, targets)

    return whole
```

time: 48.6 us -> 35.8 us (0.74)
  Pallas kernels: 19.1 us -> 13.5 us
  waiting for transfers between devices: 13.8 us -> 9.64 us
  starting transfers between devices: 12.2 us -> 9.21 us
    pallas_call x10 -> x8, Pallas kernels: 19.1 us -> 13.5 us  [the longest x1 2.78 us: pair_body(): named(early_kernel, (bf16(early, 2 * depth), bf16(early, 2 * depth), bf16...]
    ppermute x4 -> x3, waiting for transfers between devices: 5.83 us -> 1.49 us  [across(): return lax.ppermute(x, 'narrow', [(i, i ^ 2) for i in range(4)])]
    ppermute x4 -> x3, starting transfers between devices: 5.22 us -> 3.61 us  [across(): return lax.ppermute(x, 'narrow', [(i, i ^ 2) for i in range(4)])]
    ppermute x3, starting transfers between devices: 5.76 us -> 4.39 us  [along(): return lax.ppermute(x, 'blk', [(i, i ^ step) for i in range(4)])]
    ppermute x3, waiting for transfers between devices: 5.99 us -> 7.28 us  [along(): return lax.ppermute(x, 'blk', [(i, i ^ step) for i in range(4)])]
    ppermute x5, waiting for transfers between devices: 2 us -> 0.87 us  [swap(): return lax.ppermute(x, 'narrow', [(i, i ^ 1) for i in range(4)])]
    unnamed x9 -> x13, local copies, waits for them, and re-layouts: 2.36 us -> 2.4 us
  transfers between devices with their start and end apart: 12 -> 11, of which waited for: 5 -> 5; matrix products, arithmetic and copies ran while one was open for 0% -> 0% of each run, Pallas kernels for 22% -> 26%
where the time goes in v2:
time: 35.8 us; the launch traced here: 35.6 us
  Pallas kernels  13.5 us (38%)
  waiting for transfers between devices  9.64 us (27%)
  starting transfers between devices  9.21 us (26%)
  local copies, waits for them, and re-layouts  2.42 us (7%)
  between operations  0.77 us (2%)
    ppermute x3, waiting for transfers between devices, along(): return lax.ppermute(x, 'blk', [(i, i ^ step) for i in range(4)])  7.28 us
    ppermute x3, starting transfers between devices, along(): return lax.ppermute(x, 'blk', [(i, i ^ step) for i in range(4)])  4.39 us
    ppermute x3, starting transfers between devices, across(): return lax.ppermute(x, 'narrow', [(i, i ^ 2) for i in range(4)])  3.61 us
    pallas_call x1, Pallas kernels, pair_body(): named(early_kernel, (bf16(early, 2 * depth), bf16(early, 2 * depth), bf16...  2.78 us
    pallas_call x1, Pallas kernels, pair_body(): named(early_other_kernel, (bf16(early, 2 * depth), bf16(m, early), bf16(e...  2.44 us
    unnamed x13, local copies, waits for them, and re-layouts  2.4 us
    pallas_call x1, Pallas kernels, pair_body(): named(late_kernel, (bf16(late, 2 * depth), bf16(m, late), bf16(2 * early...  2.35 us
    pallas_call x1, Pallas kernels, pair_body(): call(near_kernel, f32(m, early + late), 'near', flops=2 * m * (early + la...  1.76 us
  transfers between devices with their start and end apart: 11, of which 5 were waited for; matrix products, arithmetic and copies ran while one was open for 0% of the time, Pallas kernels for 26%

profile of v2, /device:TPU:0, one launch (start us, length us, event | category | flops | bytes accessed | tf_op | source)
XLA Modules:
  0.0 35.6 jit_solution(14727114271698413606)
XLA Ops:
  0.6 0.0 copy-start
  0.6 0.8 %copy-done = f32[256,64]{0,1:T(8,128)S(1)} copy-done((f32[256,64]{0,1:T(8,128)S(1)}, f32[256,64]{0,1:T(8,128)}, u32[]{:S(2)}) %copy-start) | copy-done | bytes 65560
  1.5 0.0 copy-start.2
  1.5 0.8 %copy-done.2 = bf16[256,128]{1,0:T(8,128)(2,1)S(1)} copy-done((bf16[256,128]{1,0:T(8,128)(2,1)S(1)}, bf16[256,128]{1,0:T(8,128)(2,1)}, u32[]{:S(2)}) %copy-start.2) | copy-done | bytes 65560
  2.3 0.0 copy-start.3
  2.3 0.7 %copy-done.3 = f32[128]{0:T(128)S(1)} copy-done((f32[128]{0:T(128)S(1)}, f32[128]{0:T(128)}, u32[]{:S(2)}) %copy-start.3) | copy-done | bytes 536
  3.0 0.2 pack.1
  3.2 3.0 %collective-permute-start.4 = (bf16[384,128]{1,0:T(8,128)(2,1)S(1)}, bf16[384,128]{1,0:T(8,128)(2,1)S(1)}, u32[]{:S(2)}, u32[]{:S(2)}) collective-permute-start(bf16[384,128]{1,0:T(8,128)(2,1)S(1)} %pack.1), channel_id=1, source_target_pairs={{0,2},{1,3},{2,0},{3,1},{4,6},{5,7},{6,4},{7,5},{8,10},{9,11},{10,... | collective-permute-start | bytes 294920 | tf_op jit(solution)/shard_map/ppermute | solution.py:237
  6.2 1.6 %collective-permute-start.3 = (bf16[384,128]{1,0:T(8,128)(2,1)S(1)}, bf16[384,128]{1,0:T(8,128)(2,1)S(1)}, u32[]{:S(2)}, u32[]{:S(2)}) collective-permute-start(bf16[384,128]{1,0:T(8,128)(2,1)S(1)} %pack.1), channel_id=1, source_target_pairs={{0,4},{4,0},{8,12},{12,8},{1,5},{5,1},{9,13},{13,9},{2,6},{6,2},{1... | collective-permute-start | bytes 294920 | tf_op jit(solution)/shard_map/ppermute | solution.py:234
  7.7 2.6 %collective-permute-start.1 = (bf16[384,128]{1,0:T(8,128)(2,1)S(1)}, bf16[384,128]{1,0:T(8,128)(2,1)S(1)}, u32[]{:S(2)}, u32[]{:S(2)}) collective-permute-start(bf16[384,128]{1,0:T(8,128)(2,1)S(1)} %pack.1), channel_id=1, source_target_pairs={{0,8},{4,12},{8,0},{12,4},{1,9},{5,13},{9,1},{13,5},{2,10},{6,14},... | collective-permute-start | bytes 294920 | tf_op jit(solution)/shard_map/ppermute | solution.py:234
  10.3 0.2 collective-permute-start
  10.6 1.2 %collective-permute-done.3 = bf16[384,128]{1,0:T(8,128)(2,1)S(1)} collective-permute-done((bf16[384,128]{1,0:T(8,128)(2,1)S(1)}, bf16[384,128]{1,0:T(8,128)(2,1)S(1)}, u32[]{:S(2)}, u32[]{:S(2)}) %collective-permute-start.3) | collective-permute-done | bytes 98336 | tf_op jit(solution)/shard_map/ppermute | solution.py:234
  11.8 0.0 collective-permute-start.5
  11.8 5.0 %collective-permute-done = bf16[384,128]{1,0:T(8,128)(2,1)S(1)} collective-permute-done((bf16[384,128]{1,0:T(8,128)(2,1)S(1)}, bf16[384,128]{1,0:T(8,128)(2,1)S(1)}, u32[]{:S(2)}, u32[]{:S(2)}) %collective-permute-start) | collective-permute-done | bytes 98336 | tf_op jit(solution)/shard_map/ppermute | solution.py:234
  16.8 1.1 %collective-permute-done.1 = bf16[384,128]{1,0:T(8,128)(2,1)S(1)} collective-permute-done((bf16[384,128]{1,0:T(8,128)(2,1)S(1)}, bf16[384,128]{1,0:T(8,128)(2,1)S(1)}, u32[]{:S(2)}, u32[]{:S(2)}) %collective-permute-start.1) | collective-permute-done | bytes 98336 | tf_op jit(solution)/shard_map/ppermute | solution.py:234
  17.9 0.0 collective-permute-done.4
  17.9 0.0 collective-permute-done.5
  18.0 0.1 collective-permute-start.6
  18.1 0.6 %collective-permute-start.2 = (bf16[768,128]{1,0:T(8,128)(2,1)S(1)}, bf16[768,128]{1,0:T(8,128)(2,1)S(1)}, u32[]{:S(2)}, u32[]{:S(2)}) collective-permute-start(bf16[768,128]{1,0:T(8,128)(2,1)S(1)} %pad_maximum_fusion.1), channel_id=1, source_target_pairs={{0,2},{1,3},{2,0},{3,1},{4,6},{5,7},{6,4},{7,5},{8,10},{9,11},{10,... | collective-permute-start | bytes 589832 | tf_op jit(solution)/shard_map/ppermute | solution.py:237
  18.7 2.8 %early.1 = (bf16[1536,256]{1,0:T(8,128)(2,1)S(1)}, bf16[1536,256]{1,0:T(8,128)(2,1)S(1)}, bf16[64,1536]{1,0:T(8,128)(2,1)S(1)}, bf16[1536,1536]{1,0:T(8,128)(2,1)S(1)}, f32[64,1536]{1,0:T(8,128)S(1)}) custom-call(bf16[1536,128]{1,0:T(8,128)(2,1)S(1)} %pad_maximum_fusion.z_ref, bf16[768,128]{1,0:T(8,128)(2,1)S(1)} %pad_maximum_fusion.2.x_ref), custom_call_target="tpu_custom_call" | custom-call | flops 1509949440 | bytes 4718592 | tf_op jit(solution)/shard_map/early/pallas_call | solution.py:271
  21.5 0.0 collective-permute-done.6.u_ref
  21.5 2.4 %early_other.1 = (bf16[1536,256]{1,0:T(8,128)(2,1)S(1)}, bf16[64,1536]{1,0:T(8,128)(2,1)S(1)}, bf16[1536,1536]{1,0:T(8,128)(2,1)S(1)}, f32[64,1536]{1,0:T(8,128)S(1)}) custom-call(bf16[2304,128]{1,0:T(8,128)(2,1)S(1)} %collective-permute-done.6.u_ref, bf16[1536,256]{1,0:T(8,128)(2,1)S(1)} %get-tuple-element.26.b_ref.be_ref, ...), custom_call_target="tpu_custom_call" | custom-call | flops 1509949440 | bytes 4718592 | tf_op jit(solution)/shard_map/early_other/pallas_call | solution.py:276
  23.9 1.5 %collective-permute-done.2.x_ref = bf16[768,128]{1,0:T(8,128)(2,1)S(1)} collective-permute-done((bf16[768,128]{1,0:T(8,128)(2,1)S(1)}, bf16[768,128]{1,0:T(8,128)(2,1)S(1)}, u32[]{:S(2)}, u32[]{:S(2)}) %collective-permute-start.2) | collective-permute-done | bytes 196640 | tf_op jit(solution)/shard_map/ppermute | solution.py:237
  25.4 0.0 collective-permute-start.7
  25.4 2.4 %late.1 = (bf16[512,256]{1,0:T(8,128)(2,1)S(1)}, bf16[64,512]{1,0:T(8,128)(2,1)S(1)}, bf16[3584,512]{1,0:T(8,128)(2,1)S(1)}, f32[64,1536]{1,0:T(8,128)S(1)}, f32[64,512]{1,0:T(8,128)S(1)}) custom-call(bf16[768,128]{1,0:T(8,128)(2,1)S(1)} %collective-permute-done.2.x_ref, bf16[1536,256]{1,0:T(8,128)(2,1)S(1)} %get-tuple-element.30.ae_ref, ...), custom_call_target="tpu_custom_call" | custom-call | flops 1174405120 | bytes 3670016 | tf_op jit(solution)/shard_map/late/pallas_call | solution.py:283
  27.8 0.0 collective-permute-done.7.u_ref
  27.8 1.2 %late_other.1 = (bf16[512,2048]{1,0:T(8,128)(2,1)S(1)}, f32[64,2048]{1,0:T(8,128)S(1)}, bf16[64,2048]{1,0:T(8,128)(2,1)S(1)}, f32[64,128]{1,0:T(8,128)S(1)}) custom-call(bf16[768,128]{1,0:T(8,128)(2,1)S(1)} %collective-permute-done.7.u_ref, bf16[1536,256]{1,0:T(8,128)(2,1)S(1)} %get-tuple-element.26.b_ref.be_ref, ...), custom_call_target="tpu_custom_call" | custom-call | flops 671088640 | bytes 2097152 | tf_op jit(solution)/shard_map/late_other/pallas_call | solution.py:289
  29.0 0.6 %collective-permute-start.8 = (bf16[64,2048]{1,0:T(8,128)(2,1)S(1)}, bf16[64,2048]{1,0:T(8,128)(2,1)S(1)}, u32[]{:S(2)}, u32[]{:S(2)}) collective-permute-start(bf16[64,2048]{1,0:T(8,128)(2,1)S(1)} %get-tuple-element.40.y_ref), channel_id=1, source_target_pairs={{0,1},{1,0},{2,3},{3,2},{4,5},{5,4},{6,7},{7,6},{8,9},{9,8},{10,11... | collective-permute-start | bytes 786440 | tf_op jit(solution)/shard_map/ppermute | solution.py:240
  29.6 0.1 collective-permute-start.9
  29.7 1.8 %near.1.near_ref = f32[64,2048]{1,0:T(8,128)S(1)} custom-call(bf16[64,2048]{1,0:T(8,128)(2,1)S(1)} %get-tuple-element.40.y_ref, bf16[1536,1536]{1,0:T(8,128)(2,1)S(1)} %get-tuple-element.41.ke_ref, bf16[3584,512]{1,0:T(8,128)(2,1)S(1)} %get-tuple-element.42.kl_ref), custom_call_target="tpu_custom_call" | custom-call | flops 536870912 | tf_op jit(solution)/shard_map/near/pallas_call | solution.py:297
  31.4 0.0 collective-permute-done.9.theirs_ref
  31.4 0.0 collective-permute-done.8.yu_ref
  31.4 0.0 copy-start.1
  31.5 1.7 %far.1 = (f32[64,256]{1,0:T(8,128)S(1)}, f32[64,128]{1,0:T(8,128)S(1)}) custom-call(f32[64,2048]{1,0:T(8,128)S(1)} %get-tuple-element.39.y_ref, bf16[64,2048]{1,0:T(8,128)(2,1)S(1)} %collective-permute-done.8.yu_ref, f32[64,2048]{1,0:T(8,128)S(1)} %near.1.near_ref, f32[64,128]{1,0:T(8,128)S(1)} %get-tuple-element.43.mine_ref, ...), custom_call_target="tpu_custom_call" | custom-call | tf_op jit(solution)/shard_map/far/pallas_call | solution.py:300
  33.2 0.5 %collective-permute-start.10 = (f32[64,128]{1,0:T(8,128)S(1)}, f32[64,128]{1,0:T(8,128)S(1)}, u32[]{:S(2)}, u32[]{:S(2)}) collective-permute-start(f32[64,128]{1,0:T(8,128)S(1)} %get-tuple-element.47.mine2_ref), channel_id=1, source_target_pairs={{0,1},{1,0},{2,3},{3,2},{4,5},{5,4},{6,7},{7,6},{8,9},{9,8},{10,11... | collective-permute-start | bytes 98312 | tf_op jit(solution)/shard_map/ppermute | solution.py:240
  33.7 0.9 %collective-permute-done.10.theirs2_ref = f32[64,128]{1,0:T(8,128)S(1)} collective-permute-done((f32[64,128]{1,0:T(8,128)S(1)}, f32[64,128]{1,0:T(8,128)S(1)}, u32[]{:S(2)}, u32[]{:S(2)}) %collective-permute-start.10) | collective-permute-done | bytes 32800 | tf_op jit(solution)/shard_map/ppermute | solution.py:240
  34.5 0.0 copy-done.1
  34.5 1.0 %last.1 = (f32[64,256]{1,0:T(8,128)}, f32[64,256]{1,0:T(8,128)}) custom-call(f32[64,256]{1,0:T(8,128)S(1)} %bitcast.5, f32[64,2048]{1,0:T(8,128)S(1)} %get-tuple-element.39.y_ref, f32[64,256]{1,0:T(8,128)S(1)} %get-tuple-element.46.z_ref, f32[64,128]{1,0:T(8,128)S(1)} %get-tuple-element.43.mine_ref, f32[64,128]{1,0:T(8,128)S(1)} %collective-permute-done.9.theirs_ref, ...), custom_call_target="tpu_custom_call" | custom-call | tf_op jit(solution)/shard_map/last/pallas_call | solution.py:304
  (9 shorter events, 0.1 us)
Async XLA Ops:
  0.6 0.8 %copy-start = (f32[256,64]{0,1:T(8,128)S(1)}, f32[256,64]{0,1:T(8,128)}, u32[]{:S(2)}) copy-start(f32[256,64]{0,1:T(8,128)} %param.5) | copy-start | bytes 196612
  1.5 0.8 %copy-start.2 = (bf16[256,128]{1,0:T(8,128)(2,1)S(1)}, bf16[256,128]{1,0:T(8,128)(2,1)}, u32[]{:S(2)}) copy-start(bf16[256,128]{1,0:T(8,128)(2,1)} %points_hbm.1) | copy-start | bytes 196612
  2.3 0.7 %copy-start.3 = (f32[128]{0:T(128)S(1)}, f32[128]{0:T(128)}, u32[]{:S(2)}) copy-start(f32[128]{0:T(128)} %param.4) | copy-start | bytes 1540
  3.2 14.7 %collective-permute-start.4 = (bf16[384,128]{1,0:T(8,128)(2,1)S(1)}, bf16[384,128]{1,0:T(8,128)(2,1)S(1)}, u32[]{:S(2)}, u32[]{:S(2)}) collective-permute-start(bf16[384,128]{1,0:T(8,128)(2,1)S(1)} %pack.1), channel_id=1, source_target_pairs={{0,2},{1,3},{2,0},{3,1},{4,6},{5,7},{6,4},{7,5},{8,10},{9,11},{10,... | collective-permute-start | bytes 294920 | tf_op jit(solution)/shard_map/ppermute | solution.py:237
  6.2 5.6 %collective-permute-start.3 = (bf16[384,128]{1,0:T(8,128)(2,1)S(1)}, bf16[384,128]{1,0:T(8,128)(2,1)S(1)}, u32[]{:S(2)}, u32[]{:S(2)}) collective-permute-start(bf16[384,128]{1,0:T(8,128)(2,1)S(1)} %pack.1), channel_id=1, source_target_pairs={{0,4},{4,0},{8,12},{12,8},{1,5},{5,1},{9,13},{13,9},{2,6},{6,2},{1... | collective-permute-start | bytes 294920 | tf_op jit(solution)/shard_map/ppermute | solution.py:234
  7.7 10.1 %collective-permute-start.1 = (bf16[384,128]{1,0:T(8,128)(2,1)S(1)}, bf16[384,128]{1,0:T(8,128)(2,1)S(1)}, u32[]{:S(2)}, u32[]{:S(2)}) collective-permute-start(bf16[384,128]{1,0:T(8,128)(2,1)S(1)} %pack.1), channel_id=1, source_target_pairs={{0,8},{4,12},{8,0},{12,4},{1,9},{5,13},{9,1},{13,5},{2,10},{6,14},... | collective-permute-start | bytes 294920 | tf_op jit(solution)/shard_map/ppermute | solution.py:234
  10.3 6.4 %collective-permute-start = (bf16[384,128]{1,0:T(8,128)(2,1)S(1)}, bf16[384,128]{1,0:T(8,128)(2,1)S(1)}, u32[]{:S(2)}, u32[]{:S(2)}) collective-permute-start(bf16[384,128]{1,0:T(8,128)(2,1)S(1)} %pack.1), channel_id=1, source_target_pairs={{0,12},{4,8},{8,4},{12,0},{1,13},{5,9},{9,5},{13,1},{2,14},{6,10},... | collective-permute-start | bytes 294920 | tf_op jit(solution)/shard_map/ppermute | solution.py:234
  11.8 6.2 %collective-permute-start.5 = (bf16[384,128]{1,0:T(8,128)(2,1)S(1)}, bf16[384,128]{1,0:T(8,128)(2,1)S(1)}, u32[]{:S(2)}, u32[]{:S(2)}) collective-permute-start(bf16[384,128]{1,0:T(8,128)(2,1)S(1)} %collective-permute-done.3), channel_id=1, source_target_pairs={{0,2},{1,3},{2,0},{3,1},{4,6},{5,7},{6,4},{7,5},{8,10},{9,11},{10,... | collective-permute-start | bytes 294920 | tf_op jit(solution)/shard_map/ppermute | solution.py:237
  18.0 3.5 %collective-permute-start.6 = (bf16[2304,128]{1,0:T(8,128)(2,1)S(1)}, bf16[2304,128]{1,0:T(8,128)(2,1)S(1)}, u32[]{:S(2)}, u32[]{:S(2)}) collective-permute-start(bf16[2304,128]{1,0:T(8,128)(2,1)S(1)} %constant_dynamic-update-slice_fusion), channel_id=1, source_target_pairs={{0,1},{1,0},{2,3},{3,2},{4,5},{5,4},{6,7},{7,6},{8,9},{9,8},{10,11... | collective-permute-start | bytes 1769480 | tf_op jit(solution)/shard_map/ppermute | solution.py:240
  18.1 7.4 %collective-permute-start.2 = (bf16[768,128]{1,0:T(8,128)(2,1)S(1)}, bf16[768,128]{1,0:T(8,128)(2,1)S(1)}, u32[]{:S(2)}, u32[]{:S(2)}) collective-permute-start(bf16[768,128]{1,0:T(8,128)(2,1)S(1)} %pad_maximum_fusion.1), channel_id=1, source_target_pairs={{0,2},{1,3},{2,0},{3,1},{4,6},{5,7},{6,4},{7,5},{8,10},{9,11},{10,... | collective-permute-start | bytes 589832 | tf_op jit(solution)/shard_map/ppermute | solution.py:237
  25.4 2.4 %collective-permute-start.7 = (bf16[768,128]{1,0:T(8,128)(2,1)S(1)}, bf16[768,128]{1,0:T(8,128)(2,1)S(1)}, u32[]{:S(2)}, u32[]{:S(2)}) collective-permute-start(bf16[768,128]{1,0:T(8,128)(2,1)S(1)} %collective-permute-done.2.x_ref), channel_id=1, source_target_pairs={{0,1},{1,0},{2,3},{3,2},{4,5},{5,4},{6,7},{7,6},{8,9},{9,8},{10,11... | collective-permute-start | bytes 589832 | tf_op jit(solution)/shard_map/ppermute | solution.py:240
  29.0 2.4 %collective-permute-start.8 = (bf16[64,2048]{1,0:T(8,128)(2,1)S(1)}, bf16[64,2048]{1,0:T(8,128)(2,1)S(1)}, u32[]{:S(2)}, u32[]{:S(2)}) collective-permute-start(bf16[64,2048]{1,0:T(8,128)(2,1)S(1)} %get-tuple-element.40.y_ref), channel_id=1, source_target_pairs={{0,1},{1,0},{2,3},{3,2},{4,5},{5,4},{6,7},{7,6},{8,9},{9,8},{10,11... | collective-permute-start | bytes 786440 | tf_op jit(solution)/shard_map/ppermute | solution.py:240
  29.6 1.8 %collective-permute-start.9 = (f32[64,128]{1,0:T(8,128)S(1)}, f32[64,128]{1,0:T(8,128)S(1)}, u32[]{:S(2)}, u32[]{:S(2)}) collective-permute-start(f32[64,128]{1,0:T(8,128)S(1)} %get-tuple-element.43.mine_ref), channel_id=1, source_target_pairs={{0,1},{1,0},{2,3},{3,2},{4,5},{5,4},{6,7},{7,6},{8,9},{9,8},{10,11... | collective-permute-start | bytes 98312 | tf_op jit(solution)/shard_map/ppermute | solution.py:240
  31.4 3.1 %copy-start.1 = (f32[256,64]{0,1:T(8,128)S(1)}, f32[256,64]{0,1:T(8,128)}, u32[]{:S(2)}) copy-start(f32[256,64]{0,1:T(8,128)} %param.5) | copy-start | bytes 196612
  33.2 1.4 %collective-permute-start.10 = (f32[64,128]{1,0:T(8,128)S(1)}, f32[64,128]{1,0:T(8,128)S(1)}, u32[]{:S(2)}, u32[]{:S(2)}) collective-permute-start(f32[64,128]{1,0:T(8,128)S(1)} %get-tuple-element.47.mine2_ref), channel_id=1, source_target_pairs={{0,1},{1,0},{2,3},{3,2},{4,5},{5,4},{6,7},{7,6},{8,9},{9,8},{10,11... | collective-permute-start | bytes 98312 | tf_op jit(solution)/shard_map/ppermute | solution.py:240

commit v3 on v2

--- a/solution.py
+++ b/solution.py
@@ -17,10 +17,9 @@
 LIMIT = 20 * 2**20
 
 
-def call(kernel, outs, name, flops=0, exps=0, bytes_=0, scratch=(), ins=None):
+def call(kernel, outs, name, flops=0, exps=0, bytes_=0, scratch=()):
     return pl.pallas_call(
         kernel,
-        **({} if ins is None else {"in_specs": ins}),
         out_shape=outs,
         out_specs=jax.tree.map(lambda _: VMEM, outs),
         scratch_shapes=list(scratch),
@@ -30,25 +29,6 @@
         ),
         compiler_params=pltpu.CompilerParams(vmem_limit_bytes=LIMIT),
     )
-
-
-def pack_kernel(points_hbm, scale_hbm, targets_hbm, pack_ref, points_ref, scale_ref, targets_ref, sems):
-    copies = [
-        pltpu.make_async_copy(source, target, sems.at[index])
-        for index, (source, target) in enumerate(
-            ((points_hbm, points_ref), (scale_hbm, scale_ref), (targets_hbm, targets_ref))
-        )
-    ]
-    for copy in copies:
-        copy.start()
-    for copy in copies:
-        copy.wait()
-    n = points_ref.shape[0]
-    half = n // 2
-    m = targets_ref.shape[0]
-    pack_ref[:n] = (points_ref[...].astype(F32) * scale_ref[...]).astype(BF16)
-    pack_ref[n : n + m] = targets_ref[:, :half].astype(BF16)
-    pack_ref[n + m :] = targets_ref[:, half:].astype(BF16)
 
 
 def exponents(points, first):
@@ -251,14 +231,9 @@
             flops=tiles * (4 * depth + 2 * m), exps=tiles, bytes_=2 * tiles, scratch=scratch,
         )
 
-    pack = call(
-        pack_kernel, bf16(n + 2 * m, depth), "pack",
-        scratch=[
-            pltpu.VMEM((n, depth), BF16), pltpu.VMEM((1, depth), F32), pltpu.VMEM((m, n), F32),
-            pltpu.SemaphoreType.DMA((3,)),
-        ],
-        ins=[pl.BlockSpec(memory_space=pltpu.HBM)] * 3,
-    )(points, inv_scale[None, :], own)
+    scaled = (points.astype(F32) * inv_scale[None, :]).astype(BF16)
+    rounded = own.astype(BF16)
+    pack = jnp.concatenate([scaled, rounded[:, : n // 2], rounded[:, n // 2 :]], axis=0)
     far = [along(pack, 3), along(pack, 2)]
     next_ = along(pack, 1)
     x_own = across(pack)

time: 35.8 us -> 35 us (0.978)
  local copies, waits for them, and re-layouts: 2.42 us -> 0.18 us
  other arithmetic: 0.06 us -> 1.76 us
    unnamed x13 -> x9, local copies, waits for them, and re-layouts: 2.4 us -> 0.13 us
    unnamed x0 -> x1, other arithmetic: none -> 0.88 us
    convert_element_type x0 -> x1, other arithmetic: none -> 0.85 us  [pair_body(): rounded = own.astype(BF16)]
  transfers between devices with their start and end apart: 11 -> 11, of which waited for: 5 -> 5; matrix products, arithmetic and copies ran while one was open for 0% -> 0% of each run, Pallas kernels for 26% -> 27%
where the time goes in v3:
time: 35 us; the launch traced here: 34.8 us
  Pallas kernels  13.3 us (38%)
  waiting for transfers between devices  9.64 us (28%)
  starting transfers between devices  9.21 us (26%)
  other arithmetic  1.76 us (5%)
  between operations  0.77 us (2%)
    ppermute x3, waiting for transfers between devices, along(): return lax.ppermute(x, 'blk', [(i, i ^ step) for i in range(4)])  7.24 us
    ppermute x3, starting transfers between devices, along(): return lax.ppermute(x, 'blk', [(i, i ^ step) for i in range(4)])  4.39 us
    ppermute x3, starting transfers between devices, across(): return lax.ppermute(x, 'narrow', [(i, i ^ 2) for i in range(4)])  3.61 us
    pallas_call x1, Pallas kernels, pair_body(): named(early_kernel, (bf16(early, 2 * depth), bf16(early, 2 * depth), bf16...  2.77 us
    pallas_call x1, Pallas kernels, pair_body(): named(early_other_kernel, (bf16(early, 2 * depth), bf16(m, early), bf16(e...  2.44 us
    pallas_call x1, Pallas kernels, pair_body(): named(late_kernel, (bf16(late, 2 * depth), bf16(m, late), bf16(2 * early...  2.35 us
    pallas_call x1, Pallas kernels, pair_body(): call(near_kernel, f32(m, early + late), 'near', flops=2 * m * (early + la...  1.76 us
    pallas_call x1, Pallas kernels, pair_body(): named(far_kernel, (f32(m, n), f32(m, 128)), 'far')  1.71 us
  transfers between devices with their start and end apart: 11, of which 5 were waited for; matrix products, arithmetic and copies ran while one was open for 0% of the time, Pallas kernels for 27%

profile of v3, /device:TPU:0, one launch (start us, length us, event | category | flops | bytes accessed | tf_op | source)
XLA Modules:
  0.0 34.8 jit_solution(11065673122060671914)
XLA Ops:
  0.6 0.8 %bitcast_convert_fusion = bf16[64,256]{1,0:T(8,128)(2,1)S(1)} fusion(f32[256,64]{0,1:T(8,128)} %param.5), kind=kLoop, calls=%fused_computation.18 | loop fusion | flops 16384 | bytes 98304 | tf_op jit(solution)/shard_map/convert_element_type | solution.py:235
  1.5 0.9 %constant_dynamic-update-slice_fusion.13 = (bf16[1536,128]{1,0:T(8,128)(2,1)S(1)}, bf16[256,128]{1,0:T(8,128)(2,1)S(1)}) fusion(f32[128]{0:T(128)} %param.4, bf16[256,128]{1,0:T(8,128)(2,1)} %param.3), kind=kLoop, calls=%fused_computation.17 | loop fusion | flops 98303 | bytes 197120
  2.4 3.0 %collective-permute-start.4 = (bf16[384,128]{1,0:T(8,128)(2,1)S(1)}, bf16[384,128]{1,0:T(8,128)(2,1)S(1)}, u32[]{:S(2)}, u32[]{:S(2)}) collective-permute-start(bf16[384,128]{1,0:T(8,128)(2,1)S(1)} %pad_maximum_fusion.2), channel_id=1, source_target_pairs={{0,2},{1,3},{2,0},{3,1},{4,6},{5,7},{6,4},{7,5},{8,10},{9,11},{10,... | collective-permute-start | bytes 294920 | tf_op jit(solution)/shard_map/ppermute | solution.py:217
  5.4 1.6 %collective-permute-start.3 = (bf16[384,128]{1,0:T(8,128)(2,1)S(1)}, bf16[384,128]{1,0:T(8,128)(2,1)S(1)}, u32[]{:S(2)}, u32[]{:S(2)}) collective-permute-start(bf16[384,128]{1,0:T(8,128)(2,1)S(1)} %pad_maximum_fusion.2), channel_id=1, source_target_pairs={{0,4},{4,0},{8,12},{12,8},{1,5},{5,1},{9,13},{13,9},{2,6},{6,2},{1... | collective-permute-start | bytes 294920 | tf_op jit(solution)/shard_map/ppermute | solution.py:214
  7.0 2.6 %collective-permute-start.1 = (bf16[384,128]{1,0:T(8,128)(2,1)S(1)}, bf16[384,128]{1,0:T(8,128)(2,1)S(1)}, u32[]{:S(2)}, u32[]{:S(2)}) collective-permute-start(bf16[384,128]{1,0:T(8,128)(2,1)S(1)} %pad_maximum_fusion.2), channel_id=1, source_target_pairs={{0,8},{4,12},{8,0},{12,4},{1,9},{5,13},{9,1},{13,5},{2,10},{6,14},... | collective-permute-start | bytes 294920 | tf_op jit(solution)/shard_map/ppermute | solution.py:214
  9.6 0.2 collective-permute-start
  9.8 1.2 %collective-permute-done.3 = bf16[384,128]{1,0:T(8,128)(2,1)S(1)} collective-permute-done((bf16[384,128]{1,0:T(8,128)(2,1)S(1)}, bf16[384,128]{1,0:T(8,128)(2,1)S(1)}, u32[]{:S(2)}, u32[]{:S(2)}) %collective-permute-start.3) | collective-permute-done | bytes 98336 | tf_op jit(solution)/shard_map/ppermute | solution.py:214
  11.0 0.0 collective-permute-start.5
  11.1 4.9 %collective-permute-done = bf16[384,128]{1,0:T(8,128)(2,1)S(1)} collective-permute-done((bf16[384,128]{1,0:T(8,128)(2,1)S(1)}, bf16[384,128]{1,0:T(8,128)(2,1)S(1)}, u32[]{:S(2)}, u32[]{:S(2)}) %collective-permute-start) | collective-permute-done | bytes 98336 | tf_op jit(solution)/shard_map/ppermute | solution.py:214
  16.0 1.1 %collective-permute-done.1 = bf16[384,128]{1,0:T(8,128)(2,1)S(1)} collective-permute-done((bf16[384,128]{1,0:T(8,128)(2,1)S(1)}, bf16[384,128]{1,0:T(8,128)(2,1)S(1)}, u32[]{:S(2)}, u32[]{:S(2)}) %collective-permute-start.1) | collective-permute-done | bytes 98336 | tf_op jit(solution)/shard_map/ppermute | solution.py:214
  17.2 0.0 collective-permute-done.4
  17.2 0.0 collective-permute-done.5
  17.3 0.1 collective-permute-start.6
  17.4 0.6 %collective-permute-start.2 = (bf16[768,128]{1,0:T(8,128)(2,1)S(1)}, bf16[768,128]{1,0:T(8,128)(2,1)S(1)}, u32[]{:S(2)}, u32[]{:S(2)}) collective-permute-start(bf16[768,128]{1,0:T(8,128)(2,1)S(1)} %pad_maximum_fusion), channel_id=1, source_target_pairs={{0,2},{1,3},{2,0},{3,1},{4,6},{5,7},{6,4},{7,5},{8,10},{9,11},{10,... | collective-permute-start | bytes 589832 | tf_op jit(solution)/shard_map/ppermute | solution.py:217
  18.0 2.8 %early.1 = (bf16[1536,256]{1,0:T(8,128)(2,1)S(1)}, bf16[1536,256]{1,0:T(8,128)(2,1)S(1)}, bf16[64,1536]{1,0:T(8,128)(2,1)S(1)}, bf16[1536,1536]{1,0:T(8,128)(2,1)S(1)}, f32[64,1536]{1,0:T(8,128)S(1)}) custom-call(bf16[1536,128]{1,0:T(8,128)(2,1)S(1)} %get-tuple-element.52.z_ref, bf16[768,128]{1,0:T(8,128)(2,1)S(1)} %pad_maximum_fusion.1.x_ref), custom_call_target="tpu_custom_call" | custom-call | flops 1509949440 | bytes 4718592 | tf_op jit(solution)/shard_map/early/pallas_call | solution.py:246
  20.7 0.0 collective-permute-done.6.u_ref
  20.8 2.4 %early_other.1 = (bf16[1536,256]{1,0:T(8,128)(2,1)S(1)}, bf16[64,1536]{1,0:T(8,128)(2,1)S(1)}, bf16[1536,1536]{1,0:T(8,128)(2,1)S(1)}, f32[64,1536]{1,0:T(8,128)S(1)}) custom-call(bf16[2304,128]{1,0:T(8,128)(2,1)S(1)} %collective-permute-done.6.u_ref, bf16[1536,256]{1,0:T(8,128)(2,1)S(1)} %get-tuple-element.26.b_ref.be_ref, ...), custom_call_target="tpu_custom_call" | custom-call | flops 1509949440 | bytes 4718592 | tf_op jit(solution)/shard_map/early_other/pallas_call | solution.py:251
  23.2 1.5 %collective-permute-done.2.x_ref = bf16[768,128]{1,0:T(8,128)(2,1)S(1)} collective-permute-done((bf16[768,128]{1,0:T(8,128)(2,1)S(1)}, bf16[768,128]{1,0:T(8,128)(2,1)S(1)}, u32[]{:S(2)}, u32[]{:S(2)}) %collective-permute-start.2) | collective-permute-done | bytes 196640 | tf_op jit(solution)/shard_map/ppermute | solution.py:217
  24.7 0.0 collective-permute-start.7
  24.7 2.4 %late.1 = (bf16[512,256]{1,0:T(8,128)(2,1)S(1)}, bf16[64,512]{1,0:T(8,128)(2,1)S(1)}, bf16[3584,512]{1,0:T(8,128)(2,1)S(1)}, f32[64,1536]{1,0:T(8,128)S(1)}, f32[64,512]{1,0:T(8,128)S(1)}) custom-call(bf16[768,128]{1,0:T(8,128)(2,1)S(1)} %collective-permute-done.2.x_ref, bf16[1536,256]{1,0:T(8,128)(2,1)S(1)} %get-tuple-element.30.ae_ref, ...), custom_call_target="tpu_custom_call" | custom-call | flops 1174405120 | bytes 3670016 | tf_op jit(solution)/shard_map/late/pallas_call | solution.py:258
  27.1 0.0 collective-permute-done.7.u_ref
  27.1 1.2 %late_other.1 = (bf16[512,2048]{1,0:T(8,128)(2,1)S(1)}, f32[64,2048]{1,0:T(8,128)S(1)}, bf16[64,2048]{1,0:T(8,128)(2,1)S(1)}, f32[64,128]{1,0:T(8,128)S(1)}) custom-call(bf16[768,128]{1,0:T(8,128)(2,1)S(1)} %collective-permute-done.7.u_ref, bf16[1536,256]{1,0:T(8,128)(2,1)S(1)} %get-tuple-element.26.b_ref.be_ref, ...), custom_call_target="tpu_custom_call" | custom-call | flops 671088640 | bytes 2097152 | tf_op jit(solution)/shard_map/late_other/pallas_call | solution.py:264
  28.3 0.6 %collective-permute-start.8 = (bf16[64,2048]{1,0:T(8,128)(2,1)S(1)}, bf16[64,2048]{1,0:T(8,128)(2,1)S(1)}, u32[]{:S(2)}, u32[]{:S(2)}) collective-permute-start(bf16[64,2048]{1,0:T(8,128)(2,1)S(1)} %get-tuple-element.40.y_ref), channel_id=1, source_target_pairs={{0,1},{1,0},{2,3},{3,2},{4,5},{5,4},{6,7},{7,6},{8,9},{9,8},{10,11... | collective-permute-start | bytes 786440 | tf_op jit(solution)/shard_map/ppermute | solution.py:220
  28.9 0.1 collective-permute-start.9
  28.9 1.8 %near.1.near_ref = f32[64,2048]{1,0:T(8,128)S(1)} custom-call(bf16[64,2048]{1,0:T(8,128)(2,1)S(1)} %get-tuple-element.40.y_ref, bf16[1536,1536]{1,0:T(8,128)(2,1)S(1)} %get-tuple-element.41.ke_ref, bf16[3584,512]{1,0:T(8,128)(2,1)S(1)} %get-tuple-element.42.kl_ref), custom_call_target="tpu_custom_call" | custom-call | flops 536870912 | tf_op jit(solution)/shard_map/near/pallas_call | solution.py:272
  30.7 0.0 collective-permute-done.9.theirs_ref
  30.7 0.0 collective-permute-done.8.yu_ref
  30.7 0.0 copy-start
  30.7 1.7 %far.1 = (f32[64,256]{1,0:T(8,128)S(1)}, f32[64,128]{1,0:T(8,128)S(1)}) custom-call(f32[64,2048]{1,0:T(8,128)S(1)} %get-tuple-element.39.y_ref, bf16[64,2048]{1,0:T(8,128)(2,1)S(1)} %collective-permute-done.8.yu_ref, f32[64,2048]{1,0:T(8,128)S(1)} %near.1.near_ref, f32[64,128]{1,0:T(8,128)S(1)} %get-tuple-element.43.mine_ref, ...), custom_call_target="tpu_custom_call" | custom-call | tf_op jit(solution)/shard_map/far/pallas_call | solution.py:275
  32.5 0.5 %collective-permute-start.10 = (f32[64,128]{1,0:T(8,128)S(1)}, f32[64,128]{1,0:T(8,128)S(1)}, u32[]{:S(2)}, u32[]{:S(2)}) collective-permute-start(f32[64,128]{1,0:T(8,128)S(1)} %get-tuple-element.47.mine2_ref), channel_id=1, source_target_pairs={{0,1},{1,0},{2,3},{3,2},{4,5},{5,4},{6,7},{7,6},{8,9},{9,8},{10,11... | collective-permute-start | bytes 98312 | tf_op jit(solution)/shard_map/ppermute | solution.py:220
  33.0 0.9 %collective-permute-done.10.theirs2_ref = f32[64,128]{1,0:T(8,128)S(1)} collective-permute-done((f32[64,128]{1,0:T(8,128)S(1)}, f32[64,128]{1,0:T(8,128)S(1)}, u32[]{:S(2)}, u32[]{:S(2)}) %collective-permute-start.10) | collective-permute-done | bytes 32800 | tf_op jit(solution)/shard_map/ppermute | solution.py:220
  33.8 0.0 copy-done
  33.8 1.0 %last.1 = (f32[64,256]{1,0:T(8,128)}, f32[64,256]{1,0:T(8,128)}) custom-call(f32[64,256]{1,0:T(8,128)S(1)} %bitcast.4, f32[64,2048]{1,0:T(8,128)S(1)} %get-tuple-element.39.y_ref, f32[64,256]{1,0:T(8,128)S(1)} %get-tuple-element.46.z_ref, f32[64,128]{1,0:T(8,128)S(1)} %get-tuple-element.43.mine_ref, f32[64,128]{1,0:T(8,128)S(1)} %collective-permute-done.9.theirs_ref, ...), custom_call_target="tpu_custom_call" | custom-call | tf_op jit(solution)/shard_map/last/pallas_call | solution.py:279
  (12 shorter events, 0.2 us)
Async XLA Ops:
  2.4 14.8 %collective-permute-start.4 = (bf16[384,128]{1,0:T(8,128)(2,1)S(1)}, bf16[384,128]{1,0:T(8,128)(2,1)S(1)}, u32[]{:S(2)}, u32[]{:S(2)}) collective-permute-start(bf16[384,128]{1,0:T(8,128)(2,1)S(1)} %pad_maximum_fusion.2), channel_id=1, source_target_pairs={{0,2},{1,3},{2,0},{3,1},{4,6},{5,7},{6,4},{7,5},{8,10},{9,11},{10,... | collective-permute-start | bytes 294920 | tf_op jit(solution)/shard_map/ppermute | solution.py:217
  5.4 5.6 %collective-permute-start.3 = (bf16[384,128]{1,0:T(8,128)(2,1)S(1)}, bf16[384,128]{1,0:T(8,128)(2,1)S(1)}, u32[]{:S(2)}, u32[]{:S(2)}) collective-permute-start(bf16[384,128]{1,0:T(8,128)(2,1)S(1)} %pad_maximum_fusion.2), channel_id=1, source_target_pairs={{0,4},{4,0},{8,12},{12,8},{1,5},{5,1},{9,13},{13,9},{2,6},{6,2},{1... | collective-permute-start | bytes 294920 | tf_op jit(solution)/shard_map/ppermute | solution.py:214
  7.0 10.1 %collective-permute-start.1 = (bf16[384,128]{1,0:T(8,128)(2,1)S(1)}, bf16[384,128]{1,0:T(8,128)(2,1)S(1)}, u32[]{:S(2)}, u32[]{:S(2)}) collective-permute-start(bf16[384,128]{1,0:T(8,128)(2,1)S(1)} %pad_maximum_fusion.2), channel_id=1, source_target_pairs={{0,8},{4,12},{8,0},{12,4},{1,9},{5,13},{9,1},{13,5},{2,10},{6,14},... | collective-permute-start | bytes 294920 | tf_op jit(solution)/shard_map/ppermute | solution.py:214
  9.6 6.4 %collective-permute-start = (bf16[384,128]{1,0:T(8,128)(2,1)S(1)}, bf16[384,128]{1,0:T(8,128)(2,1)S(1)}, u32[]{:S(2)}, u32[]{:S(2)}) collective-permute-start(bf16[384,128]{1,0:T(8,128)(2,1)S(1)} %pad_maximum_fusion.2), channel_id=1, source_target_pairs={{0,12},{4,8},{8,4},{12,0},{1,13},{5,9},{9,5},{13,1},{2,14},{6,10},... | collective-permute-start | bytes 294920 | tf_op jit(solution)/shard_map/ppermute | solution.py:214
  11.0 6.2 %collective-permute-start.5 = (bf16[384,128]{1,0:T(8,128)(2,1)S(1)}, bf16[384,128]{1,0:T(8,128)(2,1)S(1)}, u32[]{:S(2)}, u32[]{:S(2)}) collective-permute-start(bf16[384,128]{1,0:T(8,128)(2,1)S(1)} %collective-permute-done.3), channel_id=1, source_target_pairs={{0,2},{1,3},{2,0},{3,1},{4,6},{5,7},{6,4},{7,5},{8,10},{9,11},{10,... | collective-permute-start | bytes 294920 | tf_op jit(solution)/shard_map/ppermute | solution.py:217
  17.3 3.5 %collective-permute-start.6 = (bf16[2304,128]{1,0:T(8,128)(2,1)S(1)}, bf16[2304,128]{1,0:T(8,128)(2,1)S(1)}, u32[]{:S(2)}, u32[]{:S(2)}) collective-permute-start(bf16[2304,128]{1,0:T(8,128)(2,1)S(1)} %constant_dynamic-update-slice_fusion), channel_id=1, source_target_pairs={{0,1},{1,0},{2,3},{3,2},{4,5},{5,4},{6,7},{7,6},{8,9},{9,8},{10,11... | collective-permute-start | bytes 1769480 | tf_op jit(solution)/shard_map/ppermute | solution.py:220
  17.4 7.4 %collective-permute-start.2 = (bf16[768,128]{1,0:T(8,128)(2,1)S(1)}, bf16[768,128]{1,0:T(8,128)(2,1)S(1)}, u32[]{:S(2)}, u32[]{:S(2)}) collective-permute-start(bf16[768,128]{1,0:T(8,128)(2,1)S(1)} %pad_maximum_fusion), channel_id=1, source_target_pairs={{0,2},{1,3},{2,0},{3,1},{4,6},{5,7},{6,4},{7,5},{8,10},{9,11},{10,... | collective-permute-start | bytes 589832 | tf_op jit(solution)/shard_map/ppermute | solution.py:217
  24.7 2.4 %collective-permute-start.7 = (bf16[768,128]{1,0:T(8,128)(2,1)S(1)}, bf16[768,128]{1,0:T(8,128)(2,1)S(1)}, u32[]{:S(2)}, u32[]{:S(2)}) collective-permute-start(bf16[768,128]{1,0:T(8,128)(2,1)S(1)} %collective-permute-done.2.x_ref), channel_id=1, source_target_pairs={{0,1},{1,0},{2,3},{3,2},{4,5},{5,4},{6,7},{7,6},{8,9},{9,8},{10,11... | collective-permute-start | bytes 589832 | tf_op jit(solution)/shard_map/ppermute | solution.py:220
  28.3 2.4 %collective-permute-start.8 = (bf16[64,2048]{1,0:T(8,128)(2,1)S(1)}, bf16[64,2048]{1,0:T(8,128)(2,1)S(1)}, u32[]{:S(2)}, u32[]{:S(2)}) collective-permute-start(bf16[64,2048]{1,0:T(8,128)(2,1)S(1)} %get-tuple-element.40.y_ref), channel_id=1, source_target_pairs={{0,1},{1,0},{2,3},{3,2},{4,5},{5,4},{6,7},{7,6},{8,9},{9,8},{10,11... | collective-permute-start | bytes 786440 | tf_op jit(solution)/shard_map/ppermute | solution.py:220
  28.9 1.8 %collective-permute-start.9 = (f32[64,128]{1,0:T(8,128)S(1)}, f32[64,128]{1,0:T(8,128)S(1)}, u32[]{:S(2)}, u32[]{:S(2)}) collective-permute-start(f32[64,128]{1,0:T(8,128)S(1)} %get-tuple-element.43.mine_ref), channel_id=1, source_target_pairs={{0,1},{1,0},{2,3},{3,2},{4,5},{5,4},{6,7},{7,6},{8,9},{9,8},{10,11... | collective-permute-start | bytes 98312 | tf_op jit(solution)/shard_map/ppermute | solution.py:220
  30.7 3.1 %copy-start = (f32[256,64]{0,1:T(8,128)S(1)}, f32[256,64]{0,1:T(8,128)}, u32[]{:S(2)}) copy-start(f32[256,64]{0,1:T(8,128)} %param.5) | copy-start | bytes 196612
  32.5 1.4 %collective-permute-start.10 = (f32[64,128]{1,0:T(8,128)S(1)}, f32[64,128]{1,0:T(8,128)S(1)}, u32[]{:S(2)}, u32[]{:S(2)}) collective-permute-start(f32[64,128]{1,0:T(8,128)S(1)} %get-tuple-element.47.mine2_ref), channel_id=1, source_target_pairs={{0,1},{1,0},{2,3},{3,2},{4,5},{5,4},{6,7},{7,6},{8,9},{9,8},{10,11... | collective-permute-start | bytes 98312 | tf_op jit(solution)/shard_map/ppermute | solution.py:220

commit v4 on v3

--- a/solution.py
+++ b/solution.py
@@ -49,22 +49,26 @@
     depth = packs[0].shape[1]
     at = 0
     for ref in packs:
-        for block in range(ref.shape[0] * 2 // (3 * n)):
-            start = block * (n * 3 // 2)
+        for block in range(ref.shape[0] // (2 * n)):
+            start = block * 2 * n
             points = ref[start : start + n]
             out[at : at + n, :depth] = points
             out[at : at + n, depth:] = exponents(points, first)
             at += n
 
 
-def vectors(packs, n, out):
+def vectors(packs, n, out, low=False):
     at = 0
+    m = n // 4
     for ref in packs:
-        for block in range(ref.shape[0] * 2 // (3 * n)):
-            start = block * (n * 3 // 2) + n
-            m = n // 4
+        for block in range(ref.shape[0] // (2 * n)):
+            start = block * 2 * n + n
             for part in range(2):
-                out[:, at : at + n // 2] = ref[start + part * m : start + (part + 1) * m]
+                value = ref[start + part * m : start + (part + 1) * m]
+                if low:
+                    rest = ref[start + (part + 2) * m : start + (part + 3) * m]
+                    value = value.astype(F32) + rest.astype(F32)
+                out[:, at : at + n // 2] = value
                 at += n // 2
 
 
@@ -126,82 +130,65 @@
     return jnp.sum(values, axis=1, keepdims=True)
 
 
-def late_other_kernel(
-    n, u_ref, be_ref, bl_ref, ve_ref, vl_ref, ye_ref, yl_ref,
-    k_ref, y_ref, round_ref, sums_ref, a, v,
-):
+def late_other_kernel(n, u_ref, be_ref, bl_ref, ye_ref, yl_ref, k_ref, y_ref, a, v):
     fill([u_ref], n, 0, a)
     vectors([u_ref], n, v)
     early = be_ref.shape[0]
     k_ref[:, :early] = tile(a[...], be_ref[...])
     k_ref[:, early:] = tile(a[...], bl_ref[...])
-    ye = ye_ref[...] + across_rows(v[...], k_ref[:, :early])
-    yl = yl_ref[...] + across_rows(v[...], k_ref[:, early:])
-    y_ref[:, :early] = ye
-    y_ref[:, early:] = yl
-    round_ref[:, :early] = ye.astype(BF16)
-    round_ref[:, early:] = yl.astype(BF16)
-    be = ve_ref[...].astype(F32)
-    bl = vl_ref[...].astype(F32)
-    sums_ref[...] = columns_of(
-        [total(be * be) + total(bl * bl), total(be * ye) + total(bl * yl)], v.shape[0]
-    )
-
-
-def near_kernel(y_ref, ke_ref, kl_ref, z_ref):
+    y_ref[:, :early] = ye_ref[...] + across_rows(v[...], k_ref[:, :early])
+    y_ref[:, early:] = yl_ref[...] + across_rows(v[...], k_ref[:, early:])
+
+
+def targets_kernel(n, z_ref, x_ref, late_ref, u_ref, late_u_ref, mine_ref, theirs_ref):
+    vectors([z_ref, x_ref, late_ref], n, mine_ref, low=True)
+    vectors([u_ref, late_u_ref], n, theirs_ref, low=True)
+
+
+def both(values):
+    return total(values[0]) + total(values[1])
+
+
+def second_kernel(
+    n, b_ref, bu_ref, y_ref, yu_ref, ke_ref, keu_ref, kl_ref, ku_ref, z_ref, sums_ref, p_ref, pu_ref
+):
     early = ke_ref.shape[0]
-    ye, yl = y_ref[:, :early], y_ref[:, early:]
-    z_ref[:, :early] = across_rows(ye, ke_ref[...]) + across_columns(yl, kl_ref[:early])
-    z_ref[:, early:] = across_rows(ye, kl_ref[:early]) + across_rows(yl, kl_ref[2 * early :])
-
-
-def first_step(mine, others):
-    bb = mine[:, 0:1] + others[:, 0:1]
-    by = mine[:, 1:2] + others[:, 1:2]
-    bw = by + noise_level * bb
-    return bb, bw, bb / bw
-
-
-def far_kernel(
-    n, y_ref, yu_ref, near_ref, mine_ref, theirs_ref, ve_ref, vl_ref, keu_ref, kl_ref, ku_ref,
-    z_ref, sums_ref,
-):
-    early = keu_ref.shape[0]
-    _, _, a0 = first_step(mine_ref[...], theirs_ref[...])
-    ue, ul = yu_ref[:, :early], yu_ref[:, early:]
-    ze = near_ref[:, :early] + across_rows(ue, keu_ref[...]) + across_rows(ul, ku_ref[:, :early])
+    b = (b_ref[...], bu_ref[...])
+    w = tuple(y[...] + noise_level * v for y, v in zip((y_ref, yu_ref), b))
+    bb = both([v * v for v in b])
+    a0 = bb / both([v * u for v, u in zip(b, w)])
+    r = [v - a0 * u for v, u in zip(b, w)]
+    rr = both([v * v for v in r])
+    beta = rr / bb
+    p = r[0] + beta * b[0]
+    p_ref[...] = p.astype(BF16)
+    pu_ref[...] = (r[1] + beta * b[1]).astype(BF16)
+    pe, pl_, ue, ul = p_ref[:, :early], p_ref[:, early:], pu_ref[:, :early], pu_ref[:, early:]
+    ze = (
+        across_rows(pe, ke_ref[...])
+        + across_columns(pl_, kl_ref[:early])
+        + across_rows(ue, keu_ref[...])
+        + across_rows(ul, ku_ref[:, :early])
+    ) + noise_level * p[:, :early]
     zl = (
-        near_ref[:, early:]
+        across_rows(pe, kl_ref[:early])
         + across_rows(ue, kl_ref[early : 2 * early])
+        + across_rows(pl_, kl_ref[2 * early :])
         + across_rows(ul, ku_ref[:, early:])
-    )
+    ) + noise_level * p[:, early:]
     z_ref[...] = ze[:, :n]
-    sums = [0.0] * 4
-    for z, y, v in ((ze, y_ref[:, :early], ve_ref), (zl, y_ref[:, early:], vl_ref)):
-        b = v[...].astype(F32)
-        w = y + noise_level * b
-        r = b - a0 * w
-        s = noise_level * r + (1.0 - noise_level * a0) * y - a0 * z
-        for index, value in enumerate((r * r, r * s, b * s, r * w)):
-            sums[index] = sums[index] + total(value)
-    sums_ref[...] = columns_of(sums, y_ref.shape[0])
-
-
-def last_kernel(
-    n, b_ref, y_ref, z_ref, mine_ref, theirs_ref, mine2_ref, theirs2_ref, x_ref, r_ref
-):
-    bb, bw, a0 = first_step(mine_ref[...], theirs_ref[...])
-    sums = mine2_ref[...] + theirs2_ref[...]
-    rr, rs, bs, rw = (sums[:, i : i + 1] for i in range(4))
-    beta = rr / bb
-    a1 = rr / (rs + beta * (bs + rw) + beta * beta * bw)
+    pz = total(p[:, :early] * ze) + total(p[:, early:] * zl)
+    sums_ref[...] = columns_of([pz, a0, beta, rr], y_ref.shape[0])
+
+
+def last_kernel(n, b_ref, y_ref, image_ref, mine_ref, theirs_ref, x_ref, r_ref):
+    a0, beta, rr = (mine_ref[:, i : i + 1] for i in (1, 2, 3))
+    a1 = rr / (mine_ref[:, 0:1] + theirs_ref[:, 0:1])
     b = b_ref[...]
-    y = y_ref[:, :n]
-    r = b - a0 * (y + noise_level * b)
+    r = b - a0 * (y_ref[:, :n] + noise_level * b)
     p = r + beta * b
-    image = (1.0 - noise_level * a0 + beta) * y - a0 * z_ref[...] + noise_level * p
     x_ref[...] = a0 * b + a1 * p
-    r_ref[...] = r - a1 * image
+    r_ref[...] = r - a1 * image_ref[...]
 
 
 def pair_body(points, inv_scale, targets):
@@ -232,8 +219,13 @@
         )
 
     scaled = (points.astype(F32) * inv_scale[None, :]).astype(BF16)
-    rounded = own.astype(BF16)
-    pack = jnp.concatenate([scaled, rounded[:, : n // 2], rounded[:, n // 2 :]], axis=0)
+    high = lax.reduce_precision(own, 8, 7)
+    low = (own - high).astype(BF16)
+    high = high.astype(BF16)
+    half = n // 2
+    pack = jnp.concatenate(
+        [scaled, high[:, :half], high[:, half:], low[:, :half], low[:, half:]], axis=0
+    )
     far = [along(pack, 3), along(pack, 2)]
     next_ = along(pack, 1)
     x_own = across(pack)
@@ -261,24 +253,22 @@
         "late", (2 * early + late) * late,
         scratch=[pltpu.VMEM((late, 2 * depth), BF16)],
     )(late_x, a_e, a_u, v_e, v_u, y_e)
-    k_u, y, y_round, sums = named(
+    k_u, y = named(
         late_other_kernel,
-        (bf16(late, early + late), f32(m, early + late), bf16(m, early + late), f32(m, 128)),
+        (bf16(late, early + late), f32(m, early + late)),
         "late_other", late * (early + late),
         scratch=[pltpu.VMEM((late, 2 * depth), BF16), pltpu.VMEM((m, late), BF16)],
-    )(late_u, b_e, b_l, v_e, v_l, y_e, y_l)
-    y_u = swap(y_round)
+    )(late_u, b_e, b_l, y_e, y_l)
+    y_u = swap(y)
+    b, b_u = named(targets_kernel, (f32(m, early + late), f32(m, early + late)), "targets")(
+        z_all, early_x, late_x, early_u, late_u
+    )
+    image, sums = named(
+        second_kernel, (f32(m, n), f32(m, 128)), "second",
+        scratch=[pltpu.VMEM((m, early + late), BF16), pltpu.VMEM((m, early + late), BF16)],
+    )(b, b_u, y, y_u, k_e, k_eu, k_l, k_u)
     sums_u = swap(sums)
-    near = call(
-        near_kernel, f32(m, early + late), "near", flops=2 * m * (early + late) ** 2
-    )(y_round, k_e, k_l)
-    z, sums2 = named(far_kernel, (f32(m, n), f32(m, 128)), "far")(
-        y, y_u, near, sums, sums_u, v_e, v_l, k_eu, k_l, k_u
-    )
-    sums2_u = swap(sums2)
-    x, r = named(last_kernel, (f32(m, n), f32(m, n)), "last")(
-        own, y, z, sums, sums_u, sums2, sums2_u
-    )
+    x, r = named(last_kernel, (f32(m, n), f32(m, n)), "last")(own, y, image, sums, sums_u)
     return x.T, r.T
 
 

time: 35 us -> 40.7 us (1.16)
  waiting for transfers between devices: 9.64 us -> 14.7 us
    ppermute x3, waiting for transfers between devices: 7.24 us -> 9.43 us  [along(): return lax.ppermute(x, 'blk', [(i, i ^ step) for i in range(4)])]
    ppermute x5 -> x4, waiting for transfers between devices: 0.87 us -> 2.29 us  [swap(): return lax.ppermute(x, 'narrow', [(i, i ^ 1) for i in range(4)])]
    ppermute x3, waiting for transfers between devices: 1.53 us -> 2.95 us  [across(): return lax.ppermute(x, 'narrow', [(i, i ^ 2) for i in range(4)])]
    pallas_call x1, Pallas kernels: 2.35 us -> 2.8 us  [pair_body(): named(late_kernel, (bf16(late, 2 * depth), bf16(m, late), bf16(2 * early...]
    ppermute x5 -> x4, starting transfers between devices: 1.21 us -> 1.09 us  [swap(): return lax.ppermute(x, 'narrow', [(i, i ^ 1) for i in range(4)])]
  transfers between devices with their start and end apart: 11 -> 10, of which waited for: 5 -> 6; matrix products, arithmetic and copies ran while one was open for 0% -> 0% of each run, Pallas kernels for 27% -> 20%
where the time goes in v4:
time: 40.7 us; the launch traced here: 40.5 us
  waiting for transfers between devices  14.7 us (36%)
  Pallas kernels  13.7 us (34%)
  starting transfers between devices  9.38 us (23%)
  other arithmetic  1.76 us (4%)
  between operations  0.74 us (2%)
    ppermute x3, waiting for transfers between devices, along(): return lax.ppermute(x, 'blk', [(i, i ^ step) for i in range(4)])  9.43 us
    ppermute x3, starting transfers between devices, along(): return lax.ppermute(x, 'blk', [(i, i ^ step) for i in range(4)])  4.39 us
    ppermute x3, starting transfers between devices, across(): return lax.ppermute(x, 'narrow', [(i, i ^ 2) for i in range(4)])  3.9 us
    pallas_call x1, Pallas kernels, pair_body(): named(second_kernel, (f32(m, n), f32(m, 128)), 'second', scratch=[pltpu.V...  3.66 us
    ppermute x3, waiting for transfers between devices, across(): return lax.ppermute(x, 'narrow', [(i, i ^ 2) for i in range(4)])  2.95 us
    pallas_call x1, Pallas kernels, pair_body(): named(late_kernel, (bf16(late, 2 * depth), bf16(m, late), bf16(2 * early...  2.8 us
    pallas_call x1, Pallas kernels, pair_body(): named(early_kernel, (bf16(early, 2 * depth), bf16(early, 2 * depth), bf16...  2.77 us
    pallas_call x1, Pallas kernels, pair_body(): named(early_other_kernel, (bf16(early, 2 * depth), bf16(m, early), bf16(e...  2.45 us
  transfers between devices with their start and end apart: 10, of which 6 were waited for; matrix products, arithmetic and copies ran while one was open for 0% of the time, Pallas kernels for 20%

profile of v4, /device:TPU:0, one launch (start us, length us, event | category | flops | bytes accessed | tf_op | source)
XLA Modules:
  0.0 40.5 jit_solution(13726217019557208138)
XLA Ops:
  0.6 0.9 %fusion = (bf16[64,256]{1,0:T(8,128)(2,1)S(1)}, bf16[64,256]{1,0:T(8,128)(2,1)S(1)}) fusion(f32[256,64]{0,1:T(8,128)} %param.5), kind=kLoop, calls=%fused_computation.4 | loop fusion | flops 65536 | bytes 131072 | tf_op jit(solution)/shard_map/convert_element_type | solution.py:223
  1.5 0.9 %constant_dynamic-update-slice_fusion.22 = (bf16[2048,128]{1,0:T(8,128)(2,1)S(1)}, bf16[3072,128]{1,0:T(8,128)(2,1)S(1)}, bf16[512,128]{1,0:T(8,128)(2,1)S(1)}) fusion(f32[128]{0:T(128)} %param.4, bf16[256,128]{1,0:T(8,128)(2,1)} %param.3), kind=kLoop, calls=%fused_computation.27 | loop fusion | flops 98301 | bytes 262656
  2.5 3.0 %collective-permute-start.4 = (bf16[512,128]{1,0:T(8,128)(2,1)S(1)}, bf16[512,128]{1,0:T(8,128)(2,1)S(1)}, u32[]{:S(2)}, u32[]{:S(2)}) collective-permute-start(bf16[512,128]{1,0:T(8,128)(2,1)S(1)} %get-tuple-element.65), channel_id=1, source_target_pairs={{0,2},{1,3},{2,0},{3,1},{4,6},{5,7},{6,4},{7,5},{8,10},{9,11},{10,... | collective-permute-start | bytes 393224 | tf_op jit(solution)/shard_map/ppermute | solution.py:204
  5.5 1.6 %collective-permute-start.3 = (bf16[512,128]{1,0:T(8,128)(2,1)S(1)}, bf16[512,128]{1,0:T(8,128)(2,1)S(1)}, u32[]{:S(2)}, u32[]{:S(2)}) collective-permute-start(bf16[512,128]{1,0:T(8,128)(2,1)S(1)} %get-tuple-element.65), channel_id=1, source_target_pairs={{0,4},{4,0},{8,12},{12,8},{1,5},{5,1},{9,13},{13,9},{2,6},{6,2},{1... | collective-permute-start | bytes 393224 | tf_op jit(solution)/shard_map/ppermute | solution.py:201
  7.0 2.6 %collective-permute-start.1 = (bf16[512,128]{1,0:T(8,128)(2,1)S(1)}, bf16[512,128]{1,0:T(8,128)(2,1)S(1)}, u32[]{:S(2)}, u32[]{:S(2)}) collective-permute-start(bf16[512,128]{1,0:T(8,128)(2,1)S(1)} %get-tuple-element.65), channel_id=1, source_target_pairs={{0,8},{4,12},{8,0},{12,4},{1,9},{5,13},{9,1},{13,5},{2,10},{6,14},... | collective-permute-start | bytes 393224 | tf_op jit(solution)/shard_map/ppermute | solution.py:201
  9.6 0.2 collective-permute-start
  9.9 2.0 %collective-permute-done.3 = bf16[512,128]{1,0:T(8,128)(2,1)S(1)} collective-permute-done((bf16[512,128]{1,0:T(8,128)(2,1)S(1)}, bf16[512,128]{1,0:T(8,128)(2,1)S(1)}, u32[]{:S(2)}, u32[]{:S(2)}) %collective-permute-start.3) | collective-permute-done | bytes 131104 | tf_op jit(solution)/shard_map/ppermute | solution.py:201
  11.9 0.3 collective-permute-start.5
  12.3 5.8 %collective-permute-done = bf16[512,128]{1,0:T(8,128)(2,1)S(1)} collective-permute-done((bf16[512,128]{1,0:T(8,128)(2,1)S(1)}, bf16[512,128]{1,0:T(8,128)(2,1)S(1)}, u32[]{:S(2)}, u32[]{:S(2)}) %collective-permute-start) | collective-permute-done | bytes 131104 | tf_op jit(solution)/shard_map/ppermute | solution.py:201
  18.1 1.6 %collective-permute-done.1 = bf16[512,128]{1,0:T(8,128)(2,1)S(1)} collective-permute-done((bf16[512,128]{1,0:T(8,128)(2,1)S(1)}, bf16[512,128]{1,0:T(8,128)(2,1)S(1)}, u32[]{:S(2)}, u32[]{:S(2)}) %collective-permute-start.1) | collective-permute-done | bytes 131104 | tf_op jit(solution)/shard_map/ppermute | solution.py:201
  19.7 0.0 collective-permute-done.4
  19.8 0.0 collective-permute-done.5
  19.8 0.1 collective-permute-start.6
  19.9 0.6 %collective-permute-start.2 = (bf16[1024,128]{1,0:T(8,128)(2,1)S(1)}, bf16[1024,128]{1,0:T(8,128)(2,1)S(1)}, u32[]{:S(2)}, u32[]{:S(2)}) collective-permute-start(bf16[1024,128]{1,0:T(8,128)(2,1)S(1)} %pad_maximum_fusion), channel_id=1, source_target_pairs={{0,2},{1,3},{2,0},{3,1},{4,6},{5,7},{6,4},{7,5},{8,10},{9,11},{10,... | collective-permute-start | bytes 786440 | tf_op jit(solution)/shard_map/ppermute | solution.py:204
  20.5 2.8 %early.1 = (bf16[1536,256]{1,0:T(8,128)(2,1)S(1)}, bf16[1536,256]{1,0:T(8,128)(2,1)S(1)}, bf16[64,1536]{1,0:T(8,128)(2,1)S(1)}, bf16[1536,1536]{1,0:T(8,128)(2,1)S(1)}, f32[64,1536]{1,0:T(8,128)S(1)}) custom-call(bf16[2048,128]{1,0:T(8,128)(2,1)S(1)} %get-tuple-element.52.z_ref, bf16[1024,128]{1,0:T(8,128)(2,1)S(1)} %get-tuple-element.48.x_ref), custom_call_target="tpu_custom_call" | custom-call | flops 1509949440 | bytes 4718592 | tf_op jit(solution)/shard_map/early/pallas_call | solution.py:238
  23.3 0.0 collective-permute-done.6.u_ref
  23.3 2.4 %early_other.1 = (bf16[1536,256]{1,0:T(8,128)(2,1)S(1)}, bf16[64,1536]{1,0:T(8,128)(2,1)S(1)}, bf16[1536,1536]{1,0:T(8,128)(2,1)S(1)}, f32[64,1536]{1,0:T(8,128)S(1)}) custom-call(bf16[3072,128]{1,0:T(8,128)(2,1)S(1)} %collective-permute-done.6.u_ref, bf16[1536,256]{1,0:T(8,128)(2,1)S(1)} %get-tuple-element.25.b_ref.be_ref, ...), custom_call_target="tpu_custom_call" | custom-call | flops 1509949440 | bytes 4718592 | tf_op jit(solution)/shard_map/early_other/pallas_call | solution.py:243
  25.8 2.9 %collective-permute-done.2.x_ref.late_ref = bf16[1024,128]{1,0:T(8,128)(2,1)S(1)} collective-permute-done((bf16[1024,128]{1,0:T(8,128)(2,1)S(1)}, bf16[1024,128]{1,0:T(8,128)(2,1)S(1)}, u32[]{:S(2)}, u32[]{:S(2)}) %collective-permute-start.2) | collective-permute-done | bytes 262176 | tf_op jit(solution)/shard_map/ppermute | solution.py:204
  28.7 0.0 collective-permute-start.7
  28.7 2.8 %late.1 = (bf16[512,256]{1,0:T(8,128)(2,1)S(1)}, bf16[64,512]{1,0:T(8,128)(2,1)}, bf16[3584,512]{1,0:T(8,128)(2,1)S(1)}, f32[64,1536]{1,0:T(8,128)S(1)}, f32[64,512]{1,0:T(8,128)S(1)}) custom-call(bf16[1024,128]{1,0:T(8,128)(2,1)S(1)} %collective-permute-done.2.x_ref.late_ref, bf16[1536,256]{1,0:T(8,128)(2,1)S(1)} %get-tuple-element.29.ae_ref, ...), custom_call_target="tpu_custom_call" | custom-call | flops 1174405120 | bytes 3670016 | tf_op jit(solution)/shard_map/late/pallas_call | solution.py:250
  31.5 0.0 collective-permute-done.7.u_ref.late_u_ref
  31.5 1.1 %late_other.1 = (bf16[512,2048]{1,0:T(8,128)(2,1)S(1)}, f32[64,2048]{1,0:T(8,128)S(1)}) custom-call(bf16[1024,128]{1,0:T(8,128)(2,1)S(1)} %collective-permute-done.7.u_ref.late_u_ref, bf16[1536,256]{1,0:T(8,128)(2,1)S(1)} %get-tuple-element.25.b_ref.be_ref, bf16[512,256]{1,0:T(8,128)(2,1)S(1)} %get-tuple-element.34.bl_ref, ...), custom_call_target="tpu_custom_call" | custom-call | flops 671088640 | bytes 2097152 | tf_op jit(solution)/shard_map/late_other/pallas_call | solution.py:256
  32.6 0.6 %collective-permute-start.8 = (f32[64,2048]{1,0:T(8,128)S(1)}, f32[64,2048]{1,0:T(8,128)S(1)}, u32[]{:S(2)}, u32[]{:S(2)}) collective-permute-start(f32[64,2048]{1,0:T(8,128)S(1)} %get-tuple-element.37.y_ref), channel_id=1, source_target_pairs={{0,1},{1,0},{2,3},{3,2},{4,5},{5,4},{6,7},{7,6},{8,9},{9,8},{10,11... | collective-permute-start | bytes 1572872 | tf_op jit(solution)/shard_map/ppermute | solution.py:207
  33.2 0.1 targets.1
  33.3 1.4 %collective-permute-done.8.yu_ref = f32[64,2048]{1,0:T(8,128)S(1)} collective-permute-done((f32[64,2048]{1,0:T(8,128)S(1)}, f32[64,2048]{1,0:T(8,128)S(1)}, u32[]{:S(2)}, u32[]{:S(2)}) %collective-permute-start.8) | collective-permute-done | bytes 524320 | tf_op jit(solution)/shard_map/ppermute | solution.py:207
  34.7 0.0 copy-start
  34.7 3.7 %second.1 = (f32[64,256]{1,0:T(8,128)S(1)}, f32[64,128]{1,0:T(8,128)S(1)}) custom-call(f32[64,2048]{1,0:T(8,128)S(1)} %get-tuple-element.38.b_ref, f32[64,2048]{1,0:T(8,128)S(1)} %get-tuple-element.39.bu_ref, f32[64,2048]{1,0:T(8,128)S(1)} %get-tuple-element.37.y_ref, f32[64,2048]{1,0:T(8,128)S(1)} %collective-permute-done.8.yu_ref, ...), custom_call_target="tpu_custom_call" | custom-call | tf_op jit(solution)/shard_map/second/pallas_call | solution.py:266
  38.4 0.4 %collective-permute-start.9 = (f32[64,128]{1,0:T(8,128)S(1)}, f32[64,128]{1,0:T(8,128)S(1)}, u32[]{:S(2)}, u32[]{:S(2)}) collective-permute-start(f32[64,128]{1,0:T(8,128)S(1)} %get-tuple-element.45.mine_ref), channel_id=1, source_target_pairs={{0,1},{1,0},{2,3},{3,2},{4,5},{5,4},{6,7},{7,6},{8,9},{9,8},{10,11... | collective-permute-start | bytes 98312 | tf_op jit(solution)/shard_map/ppermute | solution.py:207
  38.8 0.9 %collective-permute-done.9.theirs_ref = f32[64,128]{1,0:T(8,128)S(1)} collective-permute-done((f32[64,128]{1,0:T(8,128)S(1)}, f32[64,128]{1,0:T(8,128)S(1)}, u32[]{:S(2)}, u32[]{:S(2)}) %collective-permute-start.9) | collective-permute-done | bytes 32800 | tf_op jit(solution)/shard_map/ppermute | solution.py:207
  39.7 0.0 copy-done
  39.7 0.8 %last.1 = (f32[64,256]{1,0:T(8,128)}, f32[64,256]{1,0:T(8,128)}) custom-call(f32[64,256]{1,0:T(8,128)S(1)} %bitcast.5, f32[64,2048]{1,0:T(8,128)S(1)} %get-tuple-element.37.y_ref, f32[64,256]{1,0:T(8,128)S(1)} %get-tuple-element.44.image_ref, f32[64,128]{1,0:T(8,128)S(1)} %get-tuple-element.45.mine_ref, f32[64,128]{1,0:T(8,128)S(1)} %collective-permute-done.9.theirs_ref), custom_call_target="tpu_custom_call" | custom-call | tf_op jit(solution)/shard_map/last/pallas_call | solution.py:271
  (11 shorter events, 0.3 us)
Async XLA Ops:
  2.5 17.3 %collective-permute-start.4 = (bf16[512,128]{1,0:T(8,128)(2,1)S(1)}, bf16[512,128]{1,0:T(8,128)(2,1)S(1)}, u32[]{:S(2)}, u32[]{:S(2)}) collective-permute-start(bf16[512,128]{1,0:T(8,128)(2,1)S(1)} %get-tuple-element.65), channel_id=1, source_target_pairs={{0,2},{1,3},{2,0},{3,1},{4,6},{5,7},{6,4},{7,5},{8,10},{9,11},{10,... | collective-permute-start | bytes 393224 | tf_op jit(solution)/shard_map/ppermute | solution.py:204
  5.5 6.4 %collective-permute-start.3 = (bf16[512,128]{1,0:T(8,128)(2,1)S(1)}, bf16[512,128]{1,0:T(8,128)(2,1)S(1)}, u32[]{:S(2)}, u32[]{:S(2)}) collective-permute-start(bf16[512,128]{1,0:T(8,128)(2,1)S(1)} %get-tuple-element.65), channel_id=1, source_target_pairs={{0,4},{4,0},{8,12},{12,8},{1,5},{5,1},{9,13},{13,9},{2,6},{6,2},{1... | collective-permute-start | bytes 393224 | tf_op jit(solution)/shard_map/ppermute | solution.py:201
  7.0 12.6 %collective-permute-start.1 = (bf16[512,128]{1,0:T(8,128)(2,1)S(1)}, bf16[512,128]{1,0:T(8,128)(2,1)S(1)}, u32[]{:S(2)}, u32[]{:S(2)}) collective-permute-start(bf16[512,128]{1,0:T(8,128)(2,1)S(1)} %get-tuple-element.65), channel_id=1, source_target_pairs={{0,8},{4,12},{8,0},{12,4},{1,9},{5,13},{9,1},{13,5},{2,10},{6,14},... | collective-permute-start | bytes 393224 | tf_op jit(solution)/shard_map/ppermute | solution.py:201
  9.6 8.4 %collective-permute-start = (bf16[512,128]{1,0:T(8,128)(2,1)S(1)}, bf16[512,128]{1,0:T(8,128)(2,1)S(1)}, u32[]{:S(2)}, u32[]{:S(2)}) collective-permute-start(bf16[512,128]{1,0:T(8,128)(2,1)S(1)} %get-tuple-element.65), channel_id=1, source_target_pairs={{0,12},{4,8},{8,4},{12,0},{1,13},{5,9},{9,5},{13,1},{2,14},{6,10},... | collective-permute-start | bytes 393224 | tf_op jit(solution)/shard_map/ppermute | solution.py:201
  11.9 7.9 %collective-permute-start.5 = (bf16[512,128]{1,0:T(8,128)(2,1)S(1)}, bf16[512,128]{1,0:T(8,128)(2,1)S(1)}, u32[]{:S(2)}, u32[]{:S(2)}) collective-permute-start(bf16[512,128]{1,0:T(8,128)(2,1)S(1)} %collective-permute-done.3), channel_id=1, source_target_pairs={{0,2},{1,3},{2,0},{3,1},{4,6},{5,7},{6,4},{7,5},{8,10},{9,11},{10,... | collective-permute-start | bytes 393224 | tf_op jit(solution)/shard_map/ppermute | solution.py:204
  19.8 3.5 %collective-permute-start.6 = (bf16[3072,128]{1,0:T(8,128)(2,1)S(1)}, bf16[3072,128]{1,0:T(8,128)(2,1)S(1)}, u32[]{:S(2)}, u32[]{:S(2)}) collective-permute-start(bf16[3072,128]{1,0:T(8,128)(2,1)S(1)} %get-tuple-element.49), channel_id=1, source_target_pairs={{0,1},{1,0},{2,3},{3,2},{4,5},{5,4},{6,7},{7,6},{8,9},{9,8},{10,11... | collective-permute-start | bytes 2359304 | tf_op jit(solution)/shard_map/ppermute | solution.py:207
  19.9 8.8 %collective-permute-start.2 = (bf16[1024,128]{1,0:T(8,128)(2,1)S(1)}, bf16[1024,128]{1,0:T(8,128)(2,1)S(1)}, u32[]{:S(2)}, u32[]{:S(2)}) collective-permute-start(bf16[1024,128]{1,0:T(8,128)(2,1)S(1)} %pad_maximum_fusion), channel_id=1, source_target_pairs={{0,2},{1,3},{2,0},{3,1},{4,6},{5,7},{6,4},{7,5},{8,10},{9,11},{10,... | collective-permute-start | bytes 786440 | tf_op jit(solution)/shard_map/ppermute | solution.py:204
  28.7 2.8 %collective-permute-start.7 = (bf16[1024,128]{1,0:T(8,128)(2,1)S(1)}, bf16[1024,128]{1,0:T(8,128)(2,1)S(1)}, u32[]{:S(2)}, u32[]{:S(2)}) collective-permute-start(bf16[1024,128]{1,0:T(8,128)(2,1)S(1)} %collective-permute-done.2.x_ref.late_ref), channel_id=1, source_target_pairs={{0,1},{1,0},{2,3},{3,2},{4,5},{5,4},{6,7},{7,6},{8,9},{9,8},{10,11... | collective-permute-start | bytes 786440 | tf_op jit(solution)/shard_map/ppermute | solution.py:207
  32.6 2.1 %collective-permute-start.8 = (f32[64,2048]{1,0:T(8,128)S(1)}, f32[64,2048]{1,0:T(8,128)S(1)}, u32[]{:S(2)}, u32[]{:S(2)}) collective-permute-start(f32[64,2048]{1,0:T(8,128)S(1)} %get-tuple-element.37.y_ref), channel_id=1, source_target_pairs={{0,1},{1,0},{2,3},{3,2},{4,5},{5,4},{6,7},{7,6},{8,9},{9,8},{10,11... | collective-permute-start | bytes 1572872 | tf_op jit(solution)/shard_map/ppermute | solution.py:207
  34.7 5.0 %copy-start = (f32[256,64]{0,1:T(8,128)S(1)}, f32[256,64]{0,1:T(8,128)}, u32[]{:S(2)}) copy-start(f32[256,64]{0,1:T(8,128)} %param.5) | copy-start | bytes 196612
  38.4 1.3 %collective-permute-start.9 = (f32[64,128]{1,0:T(8,128)S(1)}, f32[64,128]{1,0:T(8,128)S(1)}, u32[]{:S(2)}, u32[]{:S(2)}) collective-permute-start(f32[64,128]{1,0:T(8,128)S(1)} %get-tuple-element.45.mine_ref), channel_id=1, source_target_pairs={{0,1},{1,0},{2,3},{3,2},{4,5},{5,4},{6,7},{7,6},{8,9},{9,8},{10,11... | collective-permute-start | bytes 98312 | tf_op jit(solution)/shard_map/ppermute | solution.py:207

commit v5 on v4

--- a/solution.py
+++ b/solution.py
@@ -228,7 +228,8 @@
     )
     far = [along(pack, 3), along(pack, 2)]
     next_ = along(pack, 1)
-    x_own = across(pack)
+    first, next_ = lax.optimization_barrier((pack, next_))
+    x_own = across(first)
     x_next = across(next_)
     late_z = jnp.concatenate(far, axis=0)
     late_x = across(late_z)

time: 40.7 us -> 39.5 us (0.971)
  waiting for transfers between devices: 14.7 us -> 12.5 us
  starting transfers between devices: 9.38 us -> 10.3 us
    ppermute x3, starting transfers between devices: 4.39 us -> 5.68 us  [along(): return lax.ppermute(x, 'blk', [(i, i ^ step) for i in range(4)])]
    ppermute x3, waiting for transfers between devices: 9.43 us -> 8.21 us  [along(): return lax.ppermute(x, 'blk', [(i, i ^ step) for i in range(4)])]
    ppermute x3, waiting for transfers between devices: 2.95 us -> 1.99 us  [across(): return lax.ppermute(x, 'narrow', [(i, i ^ 2) for i in range(4)])]
  transfers between devices with their start and end apart: 10 -> 10, of which waited for: 6 -> 6; matrix products, arithmetic and copies ran while one was open for 0% -> 0% of each run, Pallas kernels for 20% -> 21%
where the time goes in v5:
time: 39.5 us; the launch traced here: 39.3 us
  Pallas kernels  13.7 us (35%)
  waiting for transfers between devices  12.5 us (32%)
  starting transfers between devices  10.3 us (26%)
  other arithmetic  1.76 us (4%)
  between operations  0.74 us (2%)
    ppermute x3, waiting for transfers between devices, along(): return lax.ppermute(x, 'blk', [(i, i ^ step) for i in range(4)])  8.21 us
    ppermute x3, starting transfers between devices, along(): return lax.ppermute(x, 'blk', [(i, i ^ step) for i in range(4)])  5.68 us
    pallas_call x1, Pallas kernels, pair_body(): named(second_kernel, (f32(m, n), f32(m, 128)), 'second', scratch=[pltpu.V...  3.67 us
    ppermute x3, starting transfers between devices, across(): return lax.ppermute(x, 'narrow', [(i, i ^ 2) for i in range(4)])  3.58 us
    pallas_call x1, Pallas kernels, pair_body(): named(late_kernel, (bf16(late, 2 * depth), bf16(m, late), bf16(2 * early...  2.81 us
    pallas_call x1, Pallas kernels, pair_body(): named(early_kernel, (bf16(early, 2 * depth), bf16(early, 2 * depth), bf16...  2.77 us
    pallas_call x1, Pallas kernels, pair_body(): named(early_other_kernel, (bf16(early, 2 * depth), bf16(m, early), bf16(e...  2.45 us
    ppermute x4, waiting for transfers between devices, swap(): return lax.ppermute(x, 'narrow', [(i, i ^ 1) for i in range(4)])  2.29 us
  transfers between devices with their start and end apart: 10, of which 6 were waited for; matrix products, arithmetic and copies ran while one was open for 0% of the time, Pallas kernels for 21%

profile of v5, /device:TPU:0, one launch (start us, length us, event | category | flops | bytes accessed | tf_op | source)
XLA Modules:
  0.0 39.3 jit_solution(15777260490072786326)
XLA Ops:
  0.6 0.9 %fusion = (bf16[64,256]{1,0:T(8,128)(2,1)S(1)}, bf16[64,256]{1,0:T(8,128)(2,1)S(1)}) fusion(f32[256,64]{0,1:T(8,128)} %param.5), kind=kLoop, calls=%fused_computation.4 | loop fusion | flops 65536 | bytes 131072 | tf_op jit(solution)/shard_map/convert_element_type | solution.py:223
  1.5 0.9 %constant_dynamic-update-slice_fusion.22 = (bf16[2048,128]{1,0:T(8,128)(2,1)S(1)}, bf16[3072,128]{1,0:T(8,128)(2,1)S(1)}, bf16[512,128]{1,0:T(8,128)(2,1)S(1)}) fusion(f32[128]{0:T(128)} %param.4, bf16[256,128]{1,0:T(8,128)(2,1)} %param.3), kind=kLoop, calls=%fused_computation.27 | loop fusion | flops 98301 | bytes 262656
  2.5 3.1 %collective-permute-start.3 = (bf16[512,128]{1,0:T(8,128)(2,1)S(1)}, bf16[512,128]{1,0:T(8,128)(2,1)S(1)}, u32[]{:S(2)}, u32[]{:S(2)}) collective-permute-start(bf16[512,128]{1,0:T(8,128)(2,1)S(1)} %get-tuple-element.28), channel_id=1, source_target_pairs={{0,4},{4,0},{8,12},{12,8},{1,5},{5,1},{9,13},{13,9},{2,6},{6,2},{1... | collective-permute-start | bytes 393224 | tf_op jit(solution)/shard_map/ppermute | solution.py:201
  5.6 2.6 %collective-permute-start.1 = (bf16[512,128]{1,0:T(8,128)(2,1)S(1)}, bf16[512,128]{1,0:T(8,128)(2,1)S(1)}, u32[]{:S(2)}, u32[]{:S(2)}) collective-permute-start(bf16[512,128]{1,0:T(8,128)(2,1)S(1)} %get-tuple-element.28), channel_id=1, source_target_pairs={{0,8},{4,12},{8,0},{12,4},{1,9},{5,13},{9,1},{13,5},{2,10},{6,14},... | collective-permute-start | bytes 393224 | tf_op jit(solution)/shard_map/ppermute | solution.py:201
  8.1 0.0 collective-permute-start
  8.2 2.4 %collective-permute-done.3 = bf16[512,128]{1,0:T(8,128)(2,1)S(1)} collective-permute-done((bf16[512,128]{1,0:T(8,128)(2,1)S(1)}, bf16[512,128]{1,0:T(8,128)(2,1)S(1)}, u32[]{:S(2)}, u32[]{:S(2)}) %collective-permute-start.3) | collective-permute-done | bytes 131104 | tf_op jit(solution)/shard_map/ppermute | solution.py:201
  10.6 1.7 %collective-permute-start.4 = (bf16[512,128]{1,0:T(8,128)(2,1)S(1)}, bf16[512,128]{1,0:T(8,128)(2,1)S(1)}, u32[]{:S(2)}, u32[]{:S(2)}) collective-permute-start(bf16[512,128]{1,0:T(8,128)(2,1)S(1)} %get-tuple-element.28), channel_id=1, source_target_pairs={{0,2},{1,3},{2,0},{3,1},{4,6},{5,7},{6,4},{7,5},{8,10},{9,11},{10,... | collective-permute-start | bytes 393224 | tf_op jit(solution)/shard_map/ppermute | solution.py:204
  12.3 0.3 collective-permute-start.5
  12.7 4.3 %collective-permute-done = bf16[512,128]{1,0:T(8,128)(2,1)S(1)} collective-permute-done((bf16[512,128]{1,0:T(8,128)(2,1)S(1)}, bf16[512,128]{1,0:T(8,128)(2,1)S(1)}, u32[]{:S(2)}, u32[]{:S(2)}) %collective-permute-start) | collective-permute-done | bytes 131104 | tf_op jit(solution)/shard_map/ppermute | solution.py:201
  17.0 1.5 %collective-permute-done.1 = bf16[512,128]{1,0:T(8,128)(2,1)S(1)} collective-permute-done((bf16[512,128]{1,0:T(8,128)(2,1)S(1)}, bf16[512,128]{1,0:T(8,128)(2,1)S(1)}, u32[]{:S(2)}, u32[]{:S(2)}) %collective-permute-start.1) | collective-permute-done | bytes 131104 | tf_op jit(solution)/shard_map/ppermute | solution.py:201
  18.5 0.0 collective-permute-done.4
  18.6 0.0 collective-permute-done.5
  18.6 0.1 collective-permute-start.6
  18.7 1.6 %collective-permute-start.2 = (bf16[1024,128]{1,0:T(8,128)(2,1)S(1)}, bf16[1024,128]{1,0:T(8,128)(2,1)S(1)}, u32[]{:S(2)}, u32[]{:S(2)}) collective-permute-start(bf16[1024,128]{1,0:T(8,128)(2,1)S(1)} %pad_maximum_fusion), channel_id=1, source_target_pairs={{0,2},{1,3},{2,0},{3,1},{4,6},{5,7},{6,4},{7,5},{8,10},{9,11},{10,... | collective-permute-start | bytes 786440 | tf_op jit(solution)/shard_map/ppermute | solution.py:204
  20.3 2.8 %early.1 = (bf16[1536,256]{1,0:T(8,128)(2,1)S(1)}, bf16[1536,256]{1,0:T(8,128)(2,1)S(1)}, bf16[64,1536]{1,0:T(8,128)(2,1)S(1)}, bf16[1536,1536]{1,0:T(8,128)(2,1)S(1)}, f32[64,1536]{1,0:T(8,128)S(1)}) custom-call(bf16[2048,128]{1,0:T(8,128)(2,1)S(1)} %get-tuple-element.56.z_ref, bf16[1024,128]{1,0:T(8,128)(2,1)S(1)} %get-tuple-element.52.x_ref), custom_call_target="tpu_custom_call" | custom-call | flops 1509949440 | bytes 4718592 | tf_op jit(solution)/shard_map/early/pallas_call | solution.py:239
  23.1 0.0 collective-permute-done.6.u_ref
  23.1 2.4 %early_other.1 = (bf16[1536,256]{1,0:T(8,128)(2,1)S(1)}, bf16[64,1536]{1,0:T(8,128)(2,1)S(1)}, bf16[1536,1536]{1,0:T(8,128)(2,1)S(1)}, f32[64,1536]{1,0:T(8,128)S(1)}) custom-call(bf16[3072,128]{1,0:T(8,128)(2,1)S(1)} %collective-permute-done.6.u_ref, bf16[1536,256]{1,0:T(8,128)(2,1)S(1)} %get-tuple-element.29.b_ref.be_ref, ...), custom_call_target="tpu_custom_call" | custom-call | flops 1509949440 | bytes 4718592 | tf_op jit(solution)/shard_map/early_other/pallas_call | solution.py:244
  25.5 2.0 %collective-permute-done.2.x_ref.late_ref = bf16[1024,128]{1,0:T(8,128)(2,1)S(1)} collective-permute-done((bf16[1024,128]{1,0:T(8,128)(2,1)S(1)}, bf16[1024,128]{1,0:T(8,128)(2,1)S(1)}, u32[]{:S(2)}, u32[]{:S(2)}) %collective-permute-start.2) | collective-permute-done | bytes 262176 | tf_op jit(solution)/shard_map/ppermute | solution.py:204
  27.5 0.0 collective-permute-start.7
  27.5 2.8 %late.1 = (bf16[512,256]{1,0:T(8,128)(2,1)S(1)}, bf16[64,512]{1,0:T(8,128)(2,1)}, bf16[3584,512]{1,0:T(8,128)(2,1)S(1)}, f32[64,1536]{1,0:T(8,128)S(1)}, f32[64,512]{1,0:T(8,128)S(1)}) custom-call(bf16[1024,128]{1,0:T(8,128)(2,1)S(1)} %collective-permute-done.2.x_ref.late_ref, bf16[1536,256]{1,0:T(8,128)(2,1)S(1)} %get-tuple-element.33.ae_ref, ...), custom_call_target="tpu_custom_call" | custom-call | flops 1174405120 | bytes 3670016 | tf_op jit(solution)/shard_map/late/pallas_call | solution.py:251
  30.3 0.0 collective-permute-done.7.u_ref.late_u_ref
  30.3 1.1 %late_other.1 = (bf16[512,2048]{1,0:T(8,128)(2,1)S(1)}, f32[64,2048]{1,0:T(8,128)S(1)}) custom-call(bf16[1024,128]{1,0:T(8,128)(2,1)S(1)} %collective-permute-done.7.u_ref.late_u_ref, bf16[1536,256]{1,0:T(8,128)(2,1)S(1)} %get-tuple-element.29.b_ref.be_ref, bf16[512,256]{1,0:T(8,128)(2,1)S(1)} %get-tuple-element.38.bl_ref, ...), custom_call_target="tpu_custom_call" | custom-call | flops 671088640 | bytes 2097152 | tf_op jit(solution)/shard_map/late_other/pallas_call | solution.py:257
  31.4 0.6 %collective-permute-start.8 = (f32[64,2048]{1,0:T(8,128)S(1)}, f32[64,2048]{1,0:T(8,128)S(1)}, u32[]{:S(2)}, u32[]{:S(2)}) collective-permute-start(f32[64,2048]{1,0:T(8,128)S(1)} %get-tuple-element.41.y_ref), channel_id=1, source_target_pairs={{0,1},{1,0},{2,3},{3,2},{4,5},{5,4},{6,7},{7,6},{8,9},{9,8},{10,11... | collective-permute-start | bytes 1572872 | tf_op jit(solution)/shard_map/ppermute | solution.py:207
  32.0 0.1 targets.1
  32.1 1.4 %collective-permute-done.8.yu_ref = f32[64,2048]{1,0:T(8,128)S(1)} collective-permute-done((f32[64,2048]{1,0:T(8,128)S(1)}, f32[64,2048]{1,0:T(8,128)S(1)}, u32[]{:S(2)}, u32[]{:S(2)}) %collective-permute-start.8) | collective-permute-done | bytes 524320 | tf_op jit(solution)/shard_map/ppermute | solution.py:207
  33.5 0.0 copy-start
  33.5 3.7 %second.1 = (f32[64,256]{1,0:T(8,128)S(1)}, f32[64,128]{1,0:T(8,128)S(1)}) custom-call(f32[64,2048]{1,0:T(8,128)S(1)} %get-tuple-element.42.b_ref, f32[64,2048]{1,0:T(8,128)S(1)} %get-tuple-element.43.bu_ref, f32[64,2048]{1,0:T(8,128)S(1)} %get-tuple-element.41.y_ref, f32[64,2048]{1,0:T(8,128)S(1)} %collective-permute-done.8.yu_ref, ...), custom_call_target="tpu_custom_call" | custom-call | tf_op jit(solution)/shard_map/second/pallas_call | solution.py:267
  37.2 0.4 %collective-permute-start.9 = (f32[64,128]{1,0:T(8,128)S(1)}, f32[64,128]{1,0:T(8,128)S(1)}, u32[]{:S(2)}, u32[]{:S(2)}) collective-permute-start(f32[64,128]{1,0:T(8,128)S(1)} %get-tuple-element.49.mine_ref), channel_id=1, source_target_pairs={{0,1},{1,0},{2,3},{3,2},{4,5},{5,4},{6,7},{7,6},{8,9},{9,8},{10,11... | collective-permute-start | bytes 98312 | tf_op jit(solution)/shard_map/ppermute | solution.py:207
  37.6 0.9 %collective-permute-done.9.theirs_ref = f32[64,128]{1,0:T(8,128)S(1)} collective-permute-done((f32[64,128]{1,0:T(8,128)S(1)}, f32[64,128]{1,0:T(8,128)S(1)}, u32[]{:S(2)}, u32[]{:S(2)}) %collective-permute-start.9) | collective-permute-done | bytes 32800 | tf_op jit(solution)/shard_map/ppermute | solution.py:207
  38.5 0.0 copy-done
  38.5 0.8 %last.1 = (f32[64,256]{1,0:T(8,128)}, f32[64,256]{1,0:T(8,128)}) custom-call(f32[64,256]{1,0:T(8,128)S(1)} %bitcast.5, f32[64,2048]{1,0:T(8,128)S(1)} %get-tuple-element.41.y_ref, f32[64,256]{1,0:T(8,128)S(1)} %get-tuple-element.48.image_ref, f32[64,128]{1,0:T(8,128)S(1)} %get-tuple-element.49.mine_ref, f32[64,128]{1,0:T(8,128)S(1)} %collective-permute-done.9.theirs_ref), custom_call_target="tpu_custom_call" | custom-call | tf_op jit(solution)/shard_map/last/pallas_call | solution.py:272
  (11 shorter events, 0.3 us)
Async XLA Ops:
  2.5 8.1 %collective-permute-start.3 = (bf16[512,128]{1,0:T(8,128)(2,1)S(1)}, bf16[512,128]{1,0:T(8,128)(2,1)S(1)}, u32[]{:S(2)}, u32[]{:S(2)}) collective-permute-start(bf16[512,128]{1,0:T(8,128)(2,1)S(1)} %get-tuple-element.28), channel_id=1, source_target_pairs={{0,4},{4,0},{8,12},{12,8},{1,5},{5,1},{9,13},{13,9},{2,6},{6,2},{1... | collective-permute-start | bytes 393224 | tf_op jit(solution)/shard_map/ppermute | solution.py:201
  5.6 12.9 %collective-permute-start.1 = (bf16[512,128]{1,0:T(8,128)(2,1)S(1)}, bf16[512,128]{1,0:T(8,128)(2,1)S(1)}, u32[]{:S(2)}, u32[]{:S(2)}) collective-permute-start(bf16[512,128]{1,0:T(8,128)(2,1)S(1)} %get-tuple-element.28), channel_id=1, source_target_pairs={{0,8},{4,12},{8,0},{12,4},{1,9},{5,13},{9,1},{13,5},{2,10},{6,14},... | collective-permute-start | bytes 393224 | tf_op jit(solution)/shard_map/ppermute | solution.py:201
  8.1 8.8 %collective-permute-start = (bf16[512,128]{1,0:T(8,128)(2,1)S(1)}, bf16[512,128]{1,0:T(8,128)(2,1)S(1)}, u32[]{:S(2)}, u32[]{:S(2)}) collective-permute-start(bf16[512,128]{1,0:T(8,128)(2,1)S(1)} %get-tuple-element.28), channel_id=1, source_target_pairs={{0,12},{4,8},{8,4},{12,0},{1,13},{5,9},{9,5},{13,1},{2,14},{6,10},... | collective-permute-start | bytes 393224 | tf_op jit(solution)/shard_map/ppermute | solution.py:201
  10.6 7.9 %collective-permute-start.4 = (bf16[512,128]{1,0:T(8,128)(2,1)S(1)}, bf16[512,128]{1,0:T(8,128)(2,1)S(1)}, u32[]{:S(2)}, u32[]{:S(2)}) collective-permute-start(bf16[512,128]{1,0:T(8,128)(2,1)S(1)} %get-tuple-element.28), channel_id=1, source_target_pairs={{0,2},{1,3},{2,0},{3,1},{4,6},{5,7},{6,4},{7,5},{8,10},{9,11},{10,... | collective-permute-start | bytes 393224 | tf_op jit(solution)/shard_map/ppermute | solution.py:204
  12.3 6.3 %collective-permute-start.5 = (bf16[512,128]{1,0:T(8,128)(2,1)S(1)}, bf16[512,128]{1,0:T(8,128)(2,1)S(1)}, u32[]{:S(2)}, u32[]{:S(2)}) collective-permute-start(bf16[512,128]{1,0:T(8,128)(2,1)S(1)} %collective-permute-done.3), channel_id=1, source_target_pairs={{0,2},{1,3},{2,0},{3,1},{4,6},{5,7},{6,4},{7,5},{8,10},{9,11},{10,... | collective-permute-start | bytes 393224 | tf_op jit(solution)/shard_map/ppermute | solution.py:204
  18.6 4.4 %collective-permute-start.6 = (bf16[3072,128]{1,0:T(8,128)(2,1)S(1)}, bf16[3072,128]{1,0:T(8,128)(2,1)S(1)}, u32[]{:S(2)}, u32[]{:S(2)}) collective-permute-start(bf16[3072,128]{1,0:T(8,128)(2,1)S(1)} %get-tuple-element.53), channel_id=1, source_target_pairs={{0,1},{1,0},{2,3},{3,2},{4,5},{5,4},{6,7},{7,6},{8,9},{9,8},{10,11... | collective-permute-start | bytes 2359304 | tf_op jit(solution)/shard_map/ppermute | solution.py:207
  18.7 8.8 %collective-permute-start.2 = (bf16[1024,128]{1,0:T(8,128)(2,1)S(1)}, bf16[1024,128]{1,0:T(8,128)(2,1)S(1)}, u32[]{:S(2)}, u32[]{:S(2)}) collective-permute-start(bf16[1024,128]{1,0:T(8,128)(2,1)S(1)} %pad_maximum_fusion), channel_id=1, source_target_pairs={{0,2},{1,3},{2,0},{3,1},{4,6},{5,7},{6,4},{7,5},{8,10},{9,11},{10,... | collective-permute-start | bytes 786440 | tf_op jit(solution)/shard_map/ppermute | solution.py:204
  27.5 2.8 %collective-permute-start.7 = (bf16[1024,128]{1,0:T(8,128)(2,1)S(1)}, bf16[1024,128]{1,0:T(8,128)(2,1)S(1)}, u32[]{:S(2)}, u32[]{:S(2)}) collective-permute-start(bf16[1024,128]{1,0:T(8,128)(2,1)S(1)} %collective-permute-done.2.x_ref.late_ref), channel_id=1, source_target_pairs={{0,1},{1,0},{2,3},{3,2},{4,5},{5,4},{6,7},{7,6},{8,9},{9,8},{10,11... | collective-permute-start | bytes 786440 | tf_op jit(solution)/shard_map/ppermute | solution.py:207
  31.4 2.1 %collective-permute-start.8 = (f32[64,2048]{1,0:T(8,128)S(1)}, f32[64,2048]{1,0:T(8,128)S(1)}, u32[]{:S(2)}, u32[]{:S(2)}) collective-permute-start(f32[64,2048]{1,0:T(8,128)S(1)} %get-tuple-element.41.y_ref), channel_id=1, source_target_pairs={{0,1},{1,0},{2,3},{3,2},{4,5},{5,4},{6,7},{7,6},{8,9},{9,8},{10,11... | collective-permute-start | bytes 1572872 | tf_op jit(solution)/shard_map/ppermute | solution.py:207
  33.5 5.0 %copy-start = (f32[256,64]{0,1:T(8,128)S(1)}, f32[256,64]{0,1:T(8,128)}, u32[]{:S(2)}) copy-start(f32[256,64]{0,1:T(8,128)} %param.5) | copy-start | bytes 196612
  37.2 1.3 %collective-permute-start.9 = (f32[64,128]{1,0:T(8,128)S(1)}, f32[64,128]{1,0:T(8,128)S(1)}, u32[]{:S(2)}, u32[]{:S(2)}) collective-permute-start(f32[64,128]{1,0:T(8,128)S(1)} %get-tuple-element.49.mine_ref), channel_id=1, source_target_pairs={{0,1},{1,0},{2,3},{3,2},{4,5},{5,4},{6,7},{7,6},{8,9},{9,8},{10,11... | collective-permute-start | bytes 98312 | tf_op jit(solution)/shard_map/ppermute | solution.py:207

commit v6 on v5

--- a/solution.py
+++ b/solution.py
@@ -100,7 +100,7 @@
 
 
 def late_kernel(
-    n, x_ref, ae_ref, au_ref, ve_ref, vu_ref, y0_ref, b_ref, v_ref, k_ref, ye_ref, yl_ref, a
+    n, x_ref, ae_ref, au_ref, ve_ref, vu_ref, y0_ref, b_ref, k_ref, ye_ref, yl_ref, a, v_ref
 ):
     fill([x_ref], n, 0, a)
     fill([x_ref], n, 3, b_ref)
@@ -248,11 +248,11 @@
     )(early_u, b_e, y_e)
     late_x, y_e = lax.optimization_barrier((late_x, y_e))
     late_u = swap(late_x)
-    b_l, v_l, k_l, y_e, y_l = named(
+    b_l, k_l, y_e, y_l = named(
         late_kernel,
-        (bf16(late, 2 * depth), bf16(m, late), bf16(2 * early + late, late), f32(m, early), f32(m, late)),
+        (bf16(late, 2 * depth), bf16(2 * early + late, late), f32(m, early), f32(m, late)),
         "late", (2 * early + late) * late,
-        scratch=[pltpu.VMEM((late, 2 * depth), BF16)],
+        scratch=[pltpu.VMEM((late, 2 * depth), BF16), pltpu.VMEM((m, late), BF16)],
     )(late_x, a_e, a_u, v_e, v_u, y_e)
     k_u, y = named(
         late_other_kernel,

time: 39.5 us -> 39.1 us (0.990)
  Pallas kernels: 13.7 us -> 13.2 us
    pallas_call x1, Pallas kernels: 2.81 us -> 2.35 us  [pair_body(): named(late_kernel, (bf16(late, 2 * depth), bf16(2 * early + late, late),...]
  transfers between devices with their start and end apart: 10 -> 10, of which waited for: 6 -> 6; matrix products, arithmetic and copies ran while one was open for 0% -> 0% of each run, Pallas kernels for 21% -> 20%
where the time goes in v6:
time: 39.1 us; the launch traced here: 38.9 us
  Pallas kernels  13.2 us (34%)
  waiting for transfers between devices  12.5 us (32%)
  starting transfers between devices  10.3 us (26%)
  other arithmetic  1.76 us (5%)
  between operations  0.74 us (2%)
    ppermute x3, waiting for transfers between devices, along(): return lax.ppermute(x, 'blk', [(i, i ^ step) for i in range(4)])  8.21 us
    ppermute x3, starting transfers between devices, along(): return lax.ppermute(x, 'blk', [(i, i ^ step) for i in range(4)])  5.68 us
    pallas_call x1, Pallas kernels, pair_body(): named(second_kernel, (f32(m, n), f32(m, 128)), 'second', scratch=[pltpu.V...  3.66 us
    ppermute x3, starting transfers between devices, across(): return lax.ppermute(x, 'narrow', [(i, i ^ 2) for i in range(4)])  3.58 us
    pallas_call x1, Pallas kernels, pair_body(): named(early_kernel, (bf16(early, 2 * depth), bf16(early, 2 * depth), bf16...  2.77 us
    pallas_call x1, Pallas kernels, pair_body(): named(early_other_kernel, (bf16(early, 2 * depth), bf16(m, early), bf16(e...  2.45 us
    pallas_call x1, Pallas kernels, pair_body(): named(late_kernel, (bf16(late, 2 * depth), bf16(2 * early + late, late),...  2.35 us
    ppermute x4, waiting for transfers between devices, swap(): return lax.ppermute(x, 'narrow', [(i, i ^ 1) for i in range(4)])  2.29 us
  transfers between devices with their start and end apart: 10, of which 6 were waited for; matrix products, arithmetic and copies ran while one was open for 0% of the time, Pallas kernels for 20%

profile of v6, /device:TPU:0, one launch (start us, length us, event | category | flops | bytes accessed | tf_op | source)
XLA Modules:
  0.0 38.9 jit_solution(18287623928833925289)
XLA Ops:
  0.6 0.9 %fusion = (bf16[64,256]{1,0:T(8,128)(2,1)S(1)}, bf16[64,256]{1,0:T(8,128)(2,1)S(1)}) fusion(f32[256,64]{0,1:T(8,128)} %param.5), kind=kLoop, calls=%fused_computation.4 | loop fusion | flops 65536 | bytes 131072 | tf_op jit(solution)/shard_map/convert_element_type | solution.py:223
  1.5 0.9 %constant_dynamic-update-slice_fusion.22 = (bf16[2048,128]{1,0:T(8,128)(2,1)S(1)}, bf16[3072,128]{1,0:T(8,128)(2,1)S(1)}, bf16[512,128]{1,0:T(8,128)(2,1)S(1)}) fusion(f32[128]{0:T(128)} %param.4, bf16[256,128]{1,0:T(8,128)(2,1)} %param.3), kind=kLoop, calls=%fused_computation.27 | loop fusion | flops 98301 | bytes 262656
  2.5 3.1 %collective-permute-start.3 = (bf16[512,128]{1,0:T(8,128)(2,1)S(1)}, bf16[512,128]{1,0:T(8,128)(2,1)S(1)}, u32[]{:S(2)}, u32[]{:S(2)}) collective-permute-start(bf16[512,128]{1,0:T(8,128)(2,1)S(1)} %get-tuple-element.28), channel_id=1, source_target_pairs={{0,4},{4,0},{8,12},{12,8},{1,5},{5,1},{9,13},{13,9},{2,6},{6,2},{1... | collective-permute-start | bytes 393224 | tf_op jit(solution)/shard_map/ppermute | solution.py:201
  5.6 2.6 %collective-permute-start.1 = (bf16[512,128]{1,0:T(8,128)(2,1)S(1)}, bf16[512,128]{1,0:T(8,128)(2,1)S(1)}, u32[]{:S(2)}, u32[]{:S(2)}) collective-permute-start(bf16[512,128]{1,0:T(8,128)(2,1)S(1)} %get-tuple-element.28), channel_id=1, source_target_pairs={{0,8},{4,12},{8,0},{12,4},{1,9},{5,13},{9,1},{13,5},{2,10},{6,14},... | collective-permute-start | bytes 393224 | tf_op jit(solution)/shard_map/ppermute | solution.py:201
  8.1 0.0 collective-permute-start
  8.2 2.4 %collective-permute-done.3 = bf16[512,128]{1,0:T(8,128)(2,1)S(1)} collective-permute-done((bf16[512,128]{1,0:T(8,128)(2,1)S(1)}, bf16[512,128]{1,0:T(8,128)(2,1)S(1)}, u32[]{:S(2)}, u32[]{:S(2)}) %collective-permute-start.3) | collective-permute-done | bytes 131104 | tf_op jit(solution)/shard_map/ppermute | solution.py:201
  10.6 1.7 %collective-permute-start.4 = (bf16[512,128]{1,0:T(8,128)(2,1)S(1)}, bf16[512,128]{1,0:T(8,128)(2,1)S(1)}, u32[]{:S(2)}, u32[]{:S(2)}) collective-permute-start(bf16[512,128]{1,0:T(8,128)(2,1)S(1)} %get-tuple-element.28), channel_id=1, source_target_pairs={{0,2},{1,3},{2,0},{3,1},{4,6},{5,7},{6,4},{7,5},{8,10},{9,11},{10,... | collective-permute-start | bytes 393224 | tf_op jit(solution)/shard_map/ppermute | solution.py:204
  12.3 0.3 collective-permute-start.5
  12.7 4.3 %collective-permute-done = bf16[512,128]{1,0:T(8,128)(2,1)S(1)} collective-permute-done((bf16[512,128]{1,0:T(8,128)(2,1)S(1)}, bf16[512,128]{1,0:T(8,128)(2,1)S(1)}, u32[]{:S(2)}, u32[]{:S(2)}) %collective-permute-start) | collective-permute-done | bytes 131104 | tf_op jit(solution)/shard_map/ppermute | solution.py:201
  17.0 1.5 %collective-permute-done.1 = bf16[512,128]{1,0:T(8,128)(2,1)S(1)} collective-permute-done((bf16[512,128]{1,0:T(8,128)(2,1)S(1)}, bf16[512,128]{1,0:T(8,128)(2,1)S(1)}, u32[]{:S(2)}, u32[]{:S(2)}) %collective-permute-start.1) | collective-permute-done | bytes 131104 | tf_op jit(solution)/shard_map/ppermute | solution.py:201
  18.5 0.0 collective-permute-done.4
  18.6 0.0 collective-permute-done.5
  18.6 0.1 collective-permute-start.6
  18.7 1.6 %collective-permute-start.2 = (bf16[1024,128]{1,0:T(8,128)(2,1)S(1)}, bf16[1024,128]{1,0:T(8,128)(2,1)S(1)}, u32[]{:S(2)}, u32[]{:S(2)}) collective-permute-start(bf16[1024,128]{1,0:T(8,128)(2,1)S(1)} %pad_maximum_fusion), channel_id=1, source_target_pairs={{0,2},{1,3},{2,0},{3,1},{4,6},{5,7},{6,4},{7,5},{8,10},{9,11},{10,... | collective-permute-start | bytes 786440 | tf_op jit(solution)/shard_map/ppermute | solution.py:204
  20.3 2.8 %early.1 = (bf16[1536,256]{1,0:T(8,128)(2,1)S(1)}, bf16[1536,256]{1,0:T(8,128)(2,1)S(1)}, bf16[64,1536]{1,0:T(8,128)(2,1)S(1)}, bf16[1536,1536]{1,0:T(8,128)(2,1)S(1)}, f32[64,1536]{1,0:T(8,128)S(1)}) custom-call(bf16[2048,128]{1,0:T(8,128)(2,1)S(1)} %get-tuple-element.56.z_ref, bf16[1024,128]{1,0:T(8,128)(2,1)S(1)} %get-tuple-element.52.x_ref), custom_call_target="tpu_custom_call" | custom-call | flops 1509949440 | bytes 4718592 | tf_op jit(solution)/shard_map/early/pallas_call | solution.py:239
  23.1 0.0 collective-permute-done.6.u_ref
  23.1 2.4 %early_other.1 = (bf16[1536,256]{1,0:T(8,128)(2,1)S(1)}, bf16[64,1536]{1,0:T(8,128)(2,1)S(1)}, bf16[1536,1536]{1,0:T(8,128)(2,1)S(1)}, f32[64,1536]{1,0:T(8,128)S(1)}) custom-call(bf16[3072,128]{1,0:T(8,128)(2,1)S(1)} %collective-permute-done.6.u_ref, bf16[1536,256]{1,0:T(8,128)(2,1)S(1)} %get-tuple-element.29.b_ref.be_ref, ...), custom_call_target="tpu_custom_call" | custom-call | flops 1509949440 | bytes 4718592 | tf_op jit(solution)/shard_map/early_other/pallas_call | solution.py:244
  25.5 2.0 %collective-permute-done.2.x_ref.late_ref = bf16[1024,128]{1,0:T(8,128)(2,1)S(1)} collective-permute-done((bf16[1024,128]{1,0:T(8,128)(2,1)S(1)}, bf16[1024,128]{1,0:T(8,128)(2,1)S(1)}, u32[]{:S(2)}, u32[]{:S(2)}) %collective-permute-start.2) | collective-permute-done | bytes 262176 | tf_op jit(solution)/shard_map/ppermute | solution.py:204
  27.5 0.0 collective-permute-start.7
  27.5 2.4 %late.1 = (bf16[512,256]{1,0:T(8,128)(2,1)S(1)}, bf16[3584,512]{1,0:T(8,128)(2,1)S(1)}, f32[64,1536]{1,0:T(8,128)S(1)}, f32[64,512]{1,0:T(8,128)S(1)}) custom-call(bf16[1024,128]{1,0:T(8,128)(2,1)S(1)} %collective-permute-done.2.x_ref.late_ref, bf16[1536,256]{1,0:T(8,128)(2,1)S(1)} %get-tuple-element.33.ae_ref, ...), custom_call_target="tpu_custom_call" | custom-call | flops 1174405120 | bytes 3670016 | tf_op jit(solution)/shard_map/late/pallas_call | solution.py:251
  29.9 0.0 collective-permute-done.7.u_ref.late_u_ref
  29.9 1.1 %late_other.1 = (bf16[512,2048]{1,0:T(8,128)(2,1)S(1)}, f32[64,2048]{1,0:T(8,128)S(1)}) custom-call(bf16[1024,128]{1,0:T(8,128)(2,1)S(1)} %collective-permute-done.7.u_ref.late_u_ref, bf16[1536,256]{1,0:T(8,128)(2,1)S(1)} %get-tuple-element.29.b_ref.be_ref, bf16[512,256]{1,0:T(8,128)(2,1)S(1)} %get-tuple-element.38.bl_ref, ...), custom_call_target="tpu_custom_call" | custom-call | flops 671088640 | bytes 2097152 | tf_op jit(solution)/shard_map/late_other/pallas_call | solution.py:257
  31.0 0.6 %collective-permute-start.8 = (f32[64,2048]{1,0:T(8,128)S(1)}, f32[64,2048]{1,0:T(8,128)S(1)}, u32[]{:S(2)}, u32[]{:S(2)}) collective-permute-start(f32[64,2048]{1,0:T(8,128)S(1)} %get-tuple-element.41.y_ref), channel_id=1, source_target_pairs={{0,1},{1,0},{2,3},{3,2},{4,5},{5,4},{6,7},{7,6},{8,9},{9,8},{10,11... | collective-permute-start | bytes 1572872 | tf_op jit(solution)/shard_map/ppermute | solution.py:207
  31.5 0.1 targets.1
  31.7 1.4 %collective-permute-done.8.yu_ref = f32[64,2048]{1,0:T(8,128)S(1)} collective-permute-done((f32[64,2048]{1,0:T(8,128)S(1)}, f32[64,2048]{1,0:T(8,128)S(1)}, u32[]{:S(2)}, u32[]{:S(2)}) %collective-permute-start.8) | collective-permute-done | bytes 524320 | tf_op jit(solution)/shard_map/ppermute | solution.py:207
  33.1 0.0 copy-start
  33.1 3.7 %second.1 = (f32[64,256]{1,0:T(8,128)S(1)}, f32[64,128]{1,0:T(8,128)S(1)}) custom-call(f32[64,2048]{1,0:T(8,128)S(1)} %get-tuple-element.42.b_ref, f32[64,2048]{1,0:T(8,128)S(1)} %get-tuple-element.43.bu_ref, f32[64,2048]{1,0:T(8,128)S(1)} %get-tuple-element.41.y_ref, f32[64,2048]{1,0:T(8,128)S(1)} %collective-permute-done.8.yu_ref, ...), custom_call_target="tpu_custom_call" | custom-call | tf_op jit(solution)/shard_map/second/pallas_call | solution.py:267
  36.8 0.4 %collective-permute-start.9 = (f32[64,128]{1,0:T(8,128)S(1)}, f32[64,128]{1,0:T(8,128)S(1)}, u32[]{:S(2)}, u32[]{:S(2)}) collective-permute-start(f32[64,128]{1,0:T(8,128)S(1)} %get-tuple-element.49.mine_ref), channel_id=1, source_target_pairs={{0,1},{1,0},{2,3},{3,2},{4,5},{5,4},{6,7},{7,6},{8,9},{9,8},{10,11... | collective-permute-start | bytes 98312 | tf_op jit(solution)/shard_map/ppermute | solution.py:207
  37.2 0.9 %collective-permute-done.9.theirs_ref = f32[64,128]{1,0:T(8,128)S(1)} collective-permute-done((f32[64,128]{1,0:T(8,128)S(1)}, f32[64,128]{1,0:T(8,128)S(1)}, u32[]{:S(2)}, u32[]{:S(2)}) %collective-permute-start.9) | collective-permute-done | bytes 32800 | tf_op jit(solution)/shard_map/ppermute | solution.py:207
  38.1 0.0 copy-done
  38.1 0.8 %last.1 = (f32[64,256]{1,0:T(8,128)}, f32[64,256]{1,0:T(8,128)}) custom-call(f32[64,256]{1,0:T(8,128)S(1)} %bitcast.5, f32[64,2048]{1,0:T(8,128)S(1)} %get-tuple-element.41.y_ref, f32[64,256]{1,0:T(8,128)S(1)} %get-tuple-element.48.image_ref, f32[64,128]{1,0:T(8,128)S(1)} %get-tuple-element.49.mine_ref, f32[64,128]{1,0:T(8,128)S(1)} %collective-permute-done.9.theirs_ref), custom_call_target="tpu_custom_call" | custom-call | tf_op jit(solution)/shard_map/last/pallas_call | solution.py:272
  (11 shorter events, 0.3 us)
Async XLA Ops:
  2.5 8.1 %collective-permute-start.3 = (bf16[512,128]{1,0:T(8,128)(2,1)S(1)}, bf16[512,128]{1,0:T(8,128)(2,1)S(1)}, u32[]{:S(2)}, u32[]{:S(2)}) collective-permute-start(bf16[512,128]{1,0:T(8,128)(2,1)S(1)} %get-tuple-element.28), channel_id=1, source_target_pairs={{0,4},{4,0},{8,12},{12,8},{1,5},{5,1},{9,13},{13,9},{2,6},{6,2},{1... | collective-permute-start | bytes 393224 | tf_op jit(solution)/shard_map/ppermute | solution.py:201
  5.6 12.9 %collective-permute-start.1 = (bf16[512,128]{1,0:T(8,128)(2,1)S(1)}, bf16[512,128]{1,0:T(8,128)(2,1)S(1)}, u32[]{:S(2)}, u32[]{:S(2)}) collective-permute-start(bf16[512,128]{1,0:T(8,128)(2,1)S(1)} %get-tuple-element.28), channel_id=1, source_target_pairs={{0,8},{4,12},{8,0},{12,4},{1,9},{5,13},{9,1},{13,5},{2,10},{6,14},... | collective-permute-start | bytes 393224 | tf_op jit(solution)/shard_map/ppermute | solution.py:201
  8.1 8.8 %collective-permute-start = (bf16[512,128]{1,0:T(8,128)(2,1)S(1)}, bf16[512,128]{1,0:T(8,128)(2,1)S(1)}, u32[]{:S(2)}, u32[]{:S(2)}) collective-permute-start(bf16[512,128]{1,0:T(8,128)(2,1)S(1)} %get-tuple-element.28), channel_id=1, source_target_pairs={{0,12},{4,8},{8,4},{12,0},{1,13},{5,9},{9,5},{13,1},{2,14},{6,10},... | collective-permute-start | bytes 393224 | tf_op jit(solution)/shard_map/ppermute | solution.py:201
  10.6 7.9 %collective-permute-start.4 = (bf16[512,128]{1,0:T(8,128)(2,1)S(1)}, bf16[512,128]{1,0:T(8,128)(2,1)S(1)}, u32[]{:S(2)}, u32[]{:S(2)}) collective-permute-start(bf16[512,128]{1,0:T(8,128)(2,1)S(1)} %get-tuple-element.28), channel_id=1, source_target_pairs={{0,2},{1,3},{2,0},{3,1},{4,6},{5,7},{6,4},{7,5},{8,10},{9,11},{10,... | collective-permute-start | bytes 393224 | tf_op jit(solution)/shard_map/ppermute | solution.py:204
  12.3 6.3 %collective-permute-start.5 = (bf16[512,128]{1,0:T(8,128)(2,1)S(1)}, bf16[512,128]{1,0:T(8,128)(2,1)S(1)}, u32[]{:S(2)}, u32[]{:S(2)}) collective-permute-start(bf16[512,128]{1,0:T(8,128)(2,1)S(1)} %collective-permute-done.3), channel_id=1, source_target_pairs={{0,2},{1,3},{2,0},{3,1},{4,6},{5,7},{6,4},{7,5},{8,10},{9,11},{10,... | collective-permute-start | bytes 393224 | tf_op jit(solution)/shard_map/ppermute | solution.py:204
  18.6 4.4 %collective-permute-start.6 = (bf16[3072,128]{1,0:T(8,128)(2,1)S(1)}, bf16[3072,128]{1,0:T(8,128)(2,1)S(1)}, u32[]{:S(2)}, u32[]{:S(2)}) collective-permute-start(bf16[3072,128]{1,0:T(8,128)(2,1)S(1)} %get-tuple-element.53), channel_id=1, source_target_pairs={{0,1},{1,0},{2,3},{3,2},{4,5},{5,4},{6,7},{7,6},{8,9},{9,8},{10,11... | collective-permute-start | bytes 2359304 | tf_op jit(solution)/shard_map/ppermute | solution.py:207
  18.7 8.8 %collective-permute-start.2 = (bf16[1024,128]{1,0:T(8,128)(2,1)S(1)}, bf16[1024,128]{1,0:T(8,128)(2,1)S(1)}, u32[]{:S(2)}, u32[]{:S(2)}) collective-permute-start(bf16[1024,128]{1,0:T(8,128)(2,1)S(1)} %pad_maximum_fusion), channel_id=1, source_target_pairs={{0,2},{1,3},{2,0},{3,1},{4,6},{5,7},{6,4},{7,5},{8,10},{9,11},{10,... | collective-permute-start | bytes 786440 | tf_op jit(solution)/shard_map/ppermute | solution.py:204
  27.5 2.4 %collective-permute-start.7 = (bf16[1024,128]{1,0:T(8,128)(2,1)S(1)}, bf16[1024,128]{1,0:T(8,128)(2,1)S(1)}, u32[]{:S(2)}, u32[]{:S(2)}) collective-permute-start(bf16[1024,128]{1,0:T(8,128)(2,1)S(1)} %collective-permute-done.2.x_ref.late_ref), channel_id=1, source_target_pairs={{0,1},{1,0},{2,3},{3,2},{4,5},{5,4},{6,7},{7,6},{8,9},{9,8},{10,11... | collective-permute-start | bytes 786440 | tf_op jit(solution)/shard_map/ppermute | solution.py:207
  31.0 2.1 %collective-permute-start.8 = (f32[64,2048]{1,0:T(8,128)S(1)}, f32[64,2048]{1,0:T(8,128)S(1)}, u32[]{:S(2)}, u32[]{:S(2)}) collective-permute-start(f32[64,2048]{1,0:T(8,128)S(1)} %get-tuple-element.41.y_ref), channel_id=1, source_target_pairs={{0,1},{1,0},{2,3},{3,2},{4,5},{5,4},{6,7},{7,6},{8,9},{9,8},{10,11... | collective-permute-start | bytes 1572872 | tf_op jit(solution)/shard_map/ppermute | solution.py:207
  33.1 5.0 %copy-start = (f32[256,64]{0,1:T(8,128)S(1)}, f32[256,64]{0,1:T(8,128)}, u32[]{:S(2)}) copy-start(f32[256,64]{0,1:T(8,128)} %param.5) | copy-start | bytes 196612
  36.8 1.3 %collective-permute-start.9 = (f32[64,128]{1,0:T(8,128)S(1)}, f32[64,128]{1,0:T(8,128)S(1)}, u32[]{:S(2)}, u32[]{:S(2)}) collective-permute-start(f32[64,128]{1,0:T(8,128)S(1)} %get-tuple-element.49.mine_ref), channel_id=1, source_target_pairs={{0,1},{1,0},{2,3},{3,2},{4,5},{5,4},{6,7},{7,6},{8,9},{9,8},{10,11... | collective-permute-start | bytes 98312 | tf_op jit(solution)/shard_map/ppermute | solution.py:207

commit v7 on v6

--- a/solution.py
+++ b/solution.py
@@ -100,7 +100,7 @@
 
 
 def late_kernel(
-    n, x_ref, ae_ref, au_ref, ve_ref, vu_ref, y0_ref, b_ref, k_ref, ye_ref, yl_ref, a, v_ref
+    n, x_ref, ae_ref, au_ref, ve_ref, vu_ref, y0_ref, a, b_ref, k_ref, ye_ref, yl_ref, v_ref
 ):
     fill([x_ref], n, 0, a)
     fill([x_ref], n, 3, b_ref)
@@ -140,7 +140,10 @@
     y_ref[:, early:] = yl_ref[...] + across_rows(v[...], k_ref[:, early:])
 
 
-def targets_kernel(n, z_ref, x_ref, late_ref, u_ref, late_u_ref, mine_ref, theirs_ref):
+def targets_kernel(
+    n, z_ref, x_ref, late_ref, u_ref, late_u_ref, a_ref, b_ref, mine_ref, theirs_ref, k_ref
+):
+    k_ref[...] = tile(a_ref[...], b_ref[...])
     vectors([z_ref, x_ref, late_ref], n, mine_ref, low=True)
     vectors([u_ref, late_u_ref], n, theirs_ref, low=True)
 
@@ -150,7 +153,7 @@
 
 
 def second_kernel(
-    n, b_ref, bu_ref, y_ref, yu_ref, ke_ref, keu_ref, kl_ref, ku_ref, z_ref, sums_ref, p_ref, pu_ref
+    n, b_ref, bu_ref, y_ref, yu_ref, ke_ref, keu_ref, kl_ref, ku_ref, kle_ref, z_ref, sums_ref, p_ref, pu_ref
 ):
     early = ke_ref.shape[0]
     b = (b_ref[...], bu_ref[...])
@@ -166,7 +169,7 @@
     pe, pl_, ue, ul = p_ref[:, :early], p_ref[:, early:], pu_ref[:, :early], pu_ref[:, early:]
     ze = (
         across_rows(pe, ke_ref[...])
-        + across_columns(pl_, kl_ref[:early])
+        + across_rows(pl_, kle_ref[...])
         + across_rows(ue, keu_ref[...])
         + across_rows(ul, ku_ref[:, :early])
     ) + noise_level * p[:, :early]
@@ -248,11 +251,14 @@
     )(early_u, b_e, y_e)
     late_x, y_e = lax.optimization_barrier((late_x, y_e))
     late_u = swap(late_x)
-    b_l, k_l, y_e, y_l = named(
+    a_l, b_l, k_l, y_e, y_l = named(
         late_kernel,
-        (bf16(late, 2 * depth), bf16(2 * early + late, late), f32(m, early), f32(m, late)),
+        (
+            bf16(late, 2 * depth), bf16(late, 2 * depth), bf16(2 * early + late, late),
+            f32(m, early), f32(m, late),
+        ),
         "late", (2 * early + late) * late,
-        scratch=[pltpu.VMEM((late, 2 * depth), BF16), pltpu.VMEM((m, late), BF16)],
+        scratch=[pltpu.VMEM((m, late), BF16)],
     )(late_x, a_e, a_u, v_e, v_u, y_e)
     k_u, y = named(
         late_other_kernel,
@@ -261,13 +267,18 @@
         scratch=[pltpu.VMEM((late, 2 * depth), BF16), pltpu.VMEM((m, late), BF16)],
     )(late_u, b_e, b_l, y_e, y_l)
     y_u = swap(y)
-    b, b_u = named(targets_kernel, (f32(m, early + late), f32(m, early + late)), "targets")(
-        z_all, early_x, late_x, early_u, late_u
+    y, a_l = lax.optimization_barrier((y, a_l))
+    b, b_u, k_le = named(
+        targets_kernel,
+        (f32(m, early + late), f32(m, early + late), bf16(late, early)),
+        "targets", late * early,
+    )(
+        z_all, early_x, late_x, early_u, late_u, a_l, b_e
     )
     image, sums = named(
         second_kernel, (f32(m, n), f32(m, 128)), "second",
         scratch=[pltpu.VMEM((m, early + late), BF16), pltpu.VMEM((m, early + late), BF16)],
-    )(b, b_u, y, y_u, k_e, k_eu, k_l, k_u)
+    )(b, b_u, y, y_u, k_e, k_eu, k_l, k_u, k_le)
     sums_u = swap(sums)
     x, r = named(last_kernel, (f32(m, n), f32(m, n)), "last")(own, y, image, sums, sums_u)
     return x.T, r.T

time: 39.1 us -> 38.9 us (level)
  waiting for transfers between devices: 12.5 us -> 11.9 us
  Pallas kernels: 13.2 us -> 13.7 us
    ppermute x4, waiting for transfers between devices: 2.29 us -> 1.71 us  [swap(): return lax.ppermute(x, 'narrow', [(i, i ^ 1) for i in range(4)])]
    pallas_call x2, Pallas kernels: 2.45 us -> 3.03 us  [the longest x1 2.35 us: pair_body(): named(late_kernel, (bf16(late, 2 * depth), bf16(late, 2 * depth), bf16(2...]
  transfers between devices with their start and end apart: 10 -> 10, of which waited for: 6 -> 6; matrix products, arithmetic and copies ran while one was open for 0% -> 0% of each run, Pallas kernels for 20% -> 21%
where the time goes in v7:
time: 38.9 us; the launch traced here: 38.7 us
  Pallas kernels  13.7 us (35%)
  waiting for transfers between devices  11.9 us (31%)
  starting transfers between devices  10.3 us (26%)
  other arithmetic  1.76 us (5%)
  between operations  0.75 us (2%)
    ppermute x3, waiting for transfers between devices, along(): return lax.ppermute(x, 'blk', [(i, i ^ step) for i in range(4)])  8.21 us
    ppermute x3, starting transfers between devices, along(): return lax.ppermute(x, 'blk', [(i, i ^ step) for i in range(4)])  5.68 us
    ppermute x3, starting transfers between devices, across(): return lax.ppermute(x, 'narrow', [(i, i ^ 2) for i in range(4)])  3.58 us
    pallas_call x1, Pallas kernels, pair_body(): named(second_kernel, (f32(m, n), f32(m, 128)), 'second', scratch=[pltpu.V...  3.49 us
    pallas_call x1, Pallas kernels, pair_body(): named(early_kernel, (bf16(early, 2 * depth), bf16(early, 2 * depth), bf16...  2.77 us
    pallas_call x1, Pallas kernels, pair_body(): named(early_other_kernel, (bf16(early, 2 * depth), bf16(m, early), bf16(e...  2.45 us
    pallas_call x1, Pallas kernels, pair_body(): named(late_kernel, (bf16(late, 2 * depth), bf16(late, 2 * depth), bf16(2...  2.35 us
    ppermute x3, waiting for transfers between devices, across(): return lax.ppermute(x, 'narrow', [(i, i ^ 2) for i in range(4)])  1.99 us
  transfers between devices with their start and end apart: 10, of which 6 were waited for; matrix products, arithmetic and copies ran while one was open for 0% of the time, Pallas kernels for 21%

profile of v7, /device:TPU:0, one launch (start us, length us, event | category | flops | bytes accessed | tf_op | source)
XLA Modules:
  0.0 38.7 jit_solution(13677745652957534634)
XLA Ops:
  0.6 0.9 %fusion = (bf16[64,256]{1,0:T(8,128)(2,1)S(1)}, bf16[64,256]{1,0:T(8,128)(2,1)S(1)}) fusion(f32[256,64]{0,1:T(8,128)} %param.5), kind=kLoop, calls=%fused_computation.4 | loop fusion | flops 65536 | bytes 131072 | tf_op jit(solution)/shard_map/convert_element_type | solution.py:226
  1.5 0.9 %constant_dynamic-update-slice_fusion.22 = (bf16[2048,128]{1,0:T(8,128)(2,1)S(1)}, bf16[3072,128]{1,0:T(8,128)(2,1)S(1)}, bf16[512,128]{1,0:T(8,128)(2,1)S(1)}) fusion(f32[128]{0:T(128)} %param.4, bf16[256,128]{1,0:T(8,128)(2,1)} %param.3), kind=kLoop, calls=%fused_computation.27 | loop fusion | flops 98301 | bytes 262656
  2.5 3.1 %collective-permute-start.3 = (bf16[512,128]{1,0:T(8,128)(2,1)S(1)}, bf16[512,128]{1,0:T(8,128)(2,1)S(1)}, u32[]{:S(2)}, u32[]{:S(2)}) collective-permute-start(bf16[512,128]{1,0:T(8,128)(2,1)S(1)} %get-tuple-element.32), channel_id=1, source_target_pairs={{0,4},{4,0},{8,12},{12,8},{1,5},{5,1},{9,13},{13,9},{2,6},{6,2},{1... | collective-permute-start | bytes 393224 | tf_op jit(solution)/shard_map/ppermute | solution.py:204
  5.6 2.6 %collective-permute-start.1 = (bf16[512,128]{1,0:T(8,128)(2,1)S(1)}, bf16[512,128]{1,0:T(8,128)(2,1)S(1)}, u32[]{:S(2)}, u32[]{:S(2)}) collective-permute-start(bf16[512,128]{1,0:T(8,128)(2,1)S(1)} %get-tuple-element.32), channel_id=1, source_target_pairs={{0,8},{4,12},{8,0},{12,4},{1,9},{5,13},{9,1},{13,5},{2,10},{6,14},... | collective-permute-start | bytes 393224 | tf_op jit(solution)/shard_map/ppermute | solution.py:204
  8.1 0.0 collective-permute-start
  8.2 2.4 %collective-permute-done.3 = bf16[512,128]{1,0:T(8,128)(2,1)S(1)} collective-permute-done((bf16[512,128]{1,0:T(8,128)(2,1)S(1)}, bf16[512,128]{1,0:T(8,128)(2,1)S(1)}, u32[]{:S(2)}, u32[]{:S(2)}) %collective-permute-start.3) | collective-permute-done | bytes 131104 | tf_op jit(solution)/shard_map/ppermute | solution.py:204
  10.6 1.7 %collective-permute-start.4 = (bf16[512,128]{1,0:T(8,128)(2,1)S(1)}, bf16[512,128]{1,0:T(8,128)(2,1)S(1)}, u32[]{:S(2)}, u32[]{:S(2)}) collective-permute-start(bf16[512,128]{1,0:T(8,128)(2,1)S(1)} %get-tuple-element.32), channel_id=1, source_target_pairs={{0,2},{1,3},{2,0},{3,1},{4,6},{5,7},{6,4},{7,5},{8,10},{9,11},{10,... | collective-permute-start | bytes 393224 | tf_op jit(solution)/shard_map/ppermute | solution.py:207
  12.3 0.3 collective-permute-start.5
  12.7 4.3 %collective-permute-done = bf16[512,128]{1,0:T(8,128)(2,1)S(1)} collective-permute-done((bf16[512,128]{1,0:T(8,128)(2,1)S(1)}, bf16[512,128]{1,0:T(8,128)(2,1)S(1)}, u32[]{:S(2)}, u32[]{:S(2)}) %collective-permute-start) | collective-permute-done | bytes 131104 | tf_op jit(solution)/shard_map/ppermute | solution.py:204
  17.0 1.5 %collective-permute-done.1 = bf16[512,128]{1,0:T(8,128)(2,1)S(1)} collective-permute-done((bf16[512,128]{1,0:T(8,128)(2,1)S(1)}, bf16[512,128]{1,0:T(8,128)(2,1)S(1)}, u32[]{:S(2)}, u32[]{:S(2)}) %collective-permute-start.1) | collective-permute-done | bytes 131104 | tf_op jit(solution)/shard_map/ppermute | solution.py:204
  18.5 0.0 collective-permute-done.4
  18.6 0.0 collective-permute-done.5
  18.6 0.1 collective-permute-start.6
  18.7 1.6 %collective-permute-start.2 = (bf16[1024,128]{1,0:T(8,128)(2,1)S(1)}, bf16[1024,128]{1,0:T(8,128)(2,1)S(1)}, u32[]{:S(2)}, u32[]{:S(2)}) collective-permute-start(bf16[1024,128]{1,0:T(8,128)(2,1)S(1)} %pad_maximum_fusion), channel_id=1, source_target_pairs={{0,2},{1,3},{2,0},{3,1},{4,6},{5,7},{6,4},{7,5},{8,10},{9,11},{10,... | collective-permute-start | bytes 786440 | tf_op jit(solution)/shard_map/ppermute | solution.py:207
  20.3 2.8 %early.1 = (bf16[1536,256]{1,0:T(8,128)(2,1)S(1)}, bf16[1536,256]{1,0:T(8,128)(2,1)S(1)}, bf16[64,1536]{1,0:T(8,128)(2,1)S(1)}, bf16[1536,1536]{1,0:T(8,128)(2,1)S(1)}, f32[64,1536]{1,0:T(8,128)S(1)}) custom-call(bf16[2048,128]{1,0:T(8,128)(2,1)S(1)} %get-tuple-element.64.z_ref, bf16[1024,128]{1,0:T(8,128)(2,1)S(1)} %get-tuple-element.60.x_ref), custom_call_target="tpu_custom_call" | custom-call | flops 1509949440 | bytes 4718592 | tf_op jit(solution)/shard_map/early/pallas_call | solution.py:242
  23.1 0.0 collective-permute-done.6.u_ref
  23.1 2.4 %early_other.1 = (bf16[1536,256]{1,0:T(8,128)(2,1)S(1)}, bf16[64,1536]{1,0:T(8,128)(2,1)S(1)}, bf16[1536,1536]{1,0:T(8,128)(2,1)S(1)}, f32[64,1536]{1,0:T(8,128)S(1)}) custom-call(bf16[3072,128]{1,0:T(8,128)(2,1)S(1)} %collective-permute-done.6.u_ref, bf16[1536,256]{1,0:T(8,128)(2,1)S(1)} %get-tuple-element.33.b_ref.be_ref, ...), custom_call_target="tpu_custom_call" | custom-call | flops 1509949440 | bytes 4718592 | tf_op jit(solution)/shard_map/early_other/pallas_call | solution.py:247
  25.5 2.0 %collective-permute-done.2.x_ref.late_ref = bf16[1024,128]{1,0:T(8,128)(2,1)S(1)} collective-permute-done((bf16[1024,128]{1,0:T(8,128)(2,1)S(1)}, bf16[1024,128]{1,0:T(8,128)(2,1)S(1)}, u32[]{:S(2)}, u32[]{:S(2)}) %collective-permute-start.2) | collective-permute-done | bytes 262176 | tf_op jit(solution)/shard_map/ppermute | solution.py:207
  27.5 0.0 collective-permute-start.7
  27.5 2.4 %late.1 = (bf16[512,256]{1,0:T(8,128)(2,1)S(1)}, bf16[512,256]{1,0:T(8,128)(2,1)S(1)}, bf16[3584,512]{1,0:T(8,128)(2,1)S(1)}, f32[64,1536]{1,0:T(8,128)S(1)}, f32[64,512]{1,0:T(8,128)S(1)}) custom-call(bf16[1024,128]{1,0:T(8,128)(2,1)S(1)} %collective-permute-done.2.x_ref.late_ref, bf16[1536,256]{1,0:T(8,128)(2,1)S(1)} %get-tuple-element.37.ae_ref, ...), custom_call_target="tpu_custom_call" | custom-call | flops 1174405120 | bytes 3670016 | tf_op jit(solution)/shard_map/late/pallas_call | solution.py:254
  29.9 0.0 collective-permute-done.7.u_ref.late_u_ref
  29.9 1.1 %late_other.1 = (bf16[512,2048]{1,0:T(8,128)(2,1)S(1)}, f32[64,2048]{1,0:T(8,128)S(1)}) custom-call(bf16[1024,128]{1,0:T(8,128)(2,1)S(1)} %collective-permute-done.7.u_ref.late_u_ref, bf16[1536,256]{1,0:T(8,128)(2,1)S(1)} %get-tuple-element.33.b_ref.be_ref, bf16[512,256]{1,0:T(8,128)(2,1)S(1)} %get-tuple-element.42.bl_ref, ...), custom_call_target="tpu_custom_call" | custom-call | flops 671088640 | bytes 2097152 | tf_op jit(solution)/shard_map/late_other/pallas_call | solution.py:263
  31.0 0.6 %collective-permute-start.8 = (f32[64,2048]{1,0:T(8,128)S(1)}, f32[64,2048]{1,0:T(8,128)S(1)}, u32[]{:S(2)}, u32[]{:S(2)}) collective-permute-start(f32[64,2048]{1,0:T(8,128)S(1)} %get-tuple-element.47.y_ref), channel_id=1, source_target_pairs={{0,1},{1,0},{2,3},{3,2},{4,5},{5,4},{6,7},{7,6},{8,9},{9,8},{10,11... | collective-permute-start | bytes 1572872 | tf_op jit(solution)/shard_map/ppermute | solution.py:210
  31.6 0.7 %targets.1 = (f32[64,2048]{1,0:T(8,128)S(1)}, f32[64,2048]{1,0:T(8,128)S(1)}, bf16[512,1536]{1,0:T(8,128)(2,1)S(1)}) custom-call(bf16[2048,128]{1,0:T(8,128)(2,1)S(1)} %get-tuple-element.64.z_ref, bf16[1024,128]{1,0:T(8,128)(2,1)S(1)} %get-tuple-element.60.x_ref, bf16[1024,128]{1,0:T(8,128)(2,1)S(1)} %collective-permute-done.2.x_ref.late_ref, ...), custom_call_target="tpu_custom_call" | custom-call | flops 503316480 | bytes 1572864 | tf_op jit(solution)/shard_map/targets/pallas_call | solution.py:271
  32.2 0.8 %collective-permute-done.8.yu_ref = f32[64,2048]{1,0:T(8,128)S(1)} collective-permute-done((f32[64,2048]{1,0:T(8,128)S(1)}, f32[64,2048]{1,0:T(8,128)S(1)}, u32[]{:S(2)}, u32[]{:S(2)}) %collective-permute-start.8) | collective-permute-done | bytes 524320 | tf_op jit(solution)/shard_map/ppermute | solution.py:210
  33.1 0.0 copy-start
  33.1 3.5 %second.1 = (f32[64,256]{1,0:T(8,128)S(1)}, f32[64,128]{1,0:T(8,128)S(1)}) custom-call(f32[64,2048]{1,0:T(8,128)S(1)} %get-tuple-element.49.b_ref, f32[64,2048]{1,0:T(8,128)S(1)} %get-tuple-element.50.bu_ref, f32[64,2048]{1,0:T(8,128)S(1)} %get-tuple-element.47.y_ref, f32[64,2048]{1,0:T(8,128)S(1)} %collective-permute-done.8.yu_ref, ...), custom_call_target="tpu_custom_call" | custom-call | tf_op jit(solution)/shard_map/second/pallas_call | solution.py:278
  36.6 0.4 %collective-permute-start.9 = (f32[64,128]{1,0:T(8,128)S(1)}, f32[64,128]{1,0:T(8,128)S(1)}, u32[]{:S(2)}, u32[]{:S(2)}) collective-permute-start(f32[64,128]{1,0:T(8,128)S(1)} %get-tuple-element.57.mine_ref), channel_id=1, source_target_pairs={{0,1},{1,0},{2,3},{3,2},{4,5},{5,4},{6,7},{7,6},{8,9},{9,8},{10,11... | collective-permute-start | bytes 98312 | tf_op jit(solution)/shard_map/ppermute | solution.py:210
  37.0 0.9 %collective-permute-done.9.theirs_ref = f32[64,128]{1,0:T(8,128)S(1)} collective-permute-done((f32[64,128]{1,0:T(8,128)S(1)}, f32[64,128]{1,0:T(8,128)S(1)}, u32[]{:S(2)}, u32[]{:S(2)}) %collective-permute-start.9) | collective-permute-done | bytes 32800 | tf_op jit(solution)/shard_map/ppermute | solution.py:210
  37.9 0.0 copy-done
  37.9 0.8 %last.1 = (f32[64,256]{1,0:T(8,128)}, f32[64,256]{1,0:T(8,128)}) custom-call(f32[64,256]{1,0:T(8,128)S(1)} %bitcast.5, f32[64,2048]{1,0:T(8,128)S(1)} %get-tuple-element.47.y_ref, f32[64,256]{1,0:T(8,128)S(1)} %get-tuple-element.56.image_ref, f32[64,128]{1,0:T(8,128)S(1)} %get-tuple-element.57.mine_ref, f32[64,128]{1,0:T(8,128)S(1)} %collective-permute-done.9.theirs_ref), custom_call_target="tpu_custom_call" | custom-call | tf_op jit(solution)/shard_map/last/pallas_call | solution.py:283
  (11 shorter events, 0.3 us)
Async XLA Ops:
  2.5 8.1 %collective-permute-start.3 = (bf16[512,128]{1,0:T(8,128)(2,1)S(1)}, bf16[512,128]{1,0:T(8,128)(2,1)S(1)}, u32[]{:S(2)}, u32[]{:S(2)}) collective-permute-start(bf16[512,128]{1,0:T(8,128)(2,1)S(1)} %get-tuple-element.32), channel_id=1, source_target_pairs={{0,4},{4,0},{8,12},{12,8},{1,5},{5,1},{9,13},{13,9},{2,6},{6,2},{1... | collective-permute-start | bytes 393224 | tf_op jit(solution)/shard_map/ppermute | solution.py:204
  5.6 12.9 %collective-permute-start.1 = (bf16[512,128]{1,0:T(8,128)(2,1)S(1)}, bf16[512,128]{1,0:T(8,128)(2,1)S(1)}, u32[]{:S(2)}, u32[]{:S(2)}) collective-permute-start(bf16[512,128]{1,0:T(8,128)(2,1)S(1)} %get-tuple-element.32), channel_id=1, source_target_pairs={{0,8},{4,12},{8,0},{12,4},{1,9},{5,13},{9,1},{13,5},{2,10},{6,14},... | collective-permute-start | bytes 393224 | tf_op jit(solution)/shard_map/ppermute | solution.py:204
  8.1 8.8 %collective-permute-start = (bf16[512,128]{1,0:T(8,128)(2,1)S(1)}, bf16[512,128]{1,0:T(8,128)(2,1)S(1)}, u32[]{:S(2)}, u32[]{:S(2)}) collective-permute-start(bf16[512,128]{1,0:T(8,128)(2,1)S(1)} %get-tuple-element.32), channel_id=1, source_target_pairs={{0,12},{4,8},{8,4},{12,0},{1,13},{5,9},{9,5},{13,1},{2,14},{6,10},... | collective-permute-start | bytes 393224 | tf_op jit(solution)/shard_map/ppermute | solution.py:204
  10.6 7.9 %collective-permute-start.4 = (bf16[512,128]{1,0:T(8,128)(2,1)S(1)}, bf16[512,128]{1,0:T(8,128)(2,1)S(1)}, u32[]{:S(2)}, u32[]{:S(2)}) collective-permute-start(bf16[512,128]{1,0:T(8,128)(2,1)S(1)} %get-tuple-element.32), channel_id=1, source_target_pairs={{0,2},{1,3},{2,0},{3,1},{4,6},{5,7},{6,4},{7,5},{8,10},{9,11},{10,... | collective-permute-start | bytes 393224 | tf_op jit(solution)/shard_map/ppermute | solution.py:207
  12.3 6.3 %collective-permute-start.5 = (bf16[512,128]{1,0:T(8,128)(2,1)S(1)}, bf16[512,128]{1,0:T(8,128)(2,1)S(1)}, u32[]{:S(2)}, u32[]{:S(2)}) collective-permute-start(bf16[512,128]{1,0:T(8,128)(2,1)S(1)} %collective-permute-done.3), channel_id=1, source_target_pairs={{0,2},{1,3},{2,0},{3,1},{4,6},{5,7},{6,4},{7,5},{8,10},{9,11},{10,... | collective-permute-start | bytes 393224 | tf_op jit(solution)/shard_map/ppermute | solution.py:207
  18.6 4.4 %collective-permute-start.6 = (bf16[3072,128]{1,0:T(8,128)(2,1)S(1)}, bf16[3072,128]{1,0:T(8,128)(2,1)S(1)}, u32[]{:S(2)}, u32[]{:S(2)}) collective-permute-start(bf16[3072,128]{1,0:T(8,128)(2,1)S(1)} %get-tuple-element.61), channel_id=1, source_target_pairs={{0,1},{1,0},{2,3},{3,2},{4,5},{5,4},{6,7},{7,6},{8,9},{9,8},{10,11... | collective-permute-start | bytes 2359304 | tf_op jit(solution)/shard_map/ppermute | solution.py:210
  18.7 8.8 %collective-permute-start.2 = (bf16[1024,128]{1,0:T(8,128)(2,1)S(1)}, bf16[1024,128]{1,0:T(8,128)(2,1)S(1)}, u32[]{:S(2)}, u32[]{:S(2)}) collective-permute-start(bf16[1024,128]{1,0:T(8,128)(2,1)S(1)} %pad_maximum_fusion), channel_id=1, source_target_pairs={{0,2},{1,3},{2,0},{3,1},{4,6},{5,7},{6,4},{7,5},{8,10},{9,11},{10,... | collective-permute-start | bytes 786440 | tf_op jit(solution)/shard_map/ppermute | solution.py:207
  27.5 2.4 %collective-permute-start.7 = (bf16[1024,128]{1,0:T(8,128)(2,1)S(1)}, bf16[1024,128]{1,0:T(8,128)(2,1)S(1)}, u32[]{:S(2)}, u32[]{:S(2)}) collective-permute-start(bf16[1024,128]{1,0:T(8,128)(2,1)S(1)} %collective-permute-done.2.x_ref.late_ref), channel_id=1, source_target_pairs={{0,1},{1,0},{2,3},{3,2},{4,5},{5,4},{6,7},{7,6},{8,9},{9,8},{10,11... | collective-permute-start | bytes 786440 | tf_op jit(solution)/shard_map/ppermute | solution.py:210
  31.0 2.1 %collective-permute-start.8 = (f32[64,2048]{1,0:T(8,128)S(1)}, f32[64,2048]{1,0:T(8,128)S(1)}, u32[]{:S(2)}, u32[]{:S(2)}) collective-permute-start(f32[64,2048]{1,0:T(8,128)S(1)} %get-tuple-element.47.y_ref), channel_id=1, source_target_pairs={{0,1},{1,0},{2,3},{3,2},{4,5},{5,4},{6,7},{7,6},{8,9},{9,8},{10,11... | collective-permute-start | bytes 1572872 | tf_op jit(solution)/shard_map/ppermute | solution.py:210
  33.1 4.8 %copy-start = (f32[256,64]{0,1:T(8,128)S(1)}, f32[256,64]{0,1:T(8,128)}, u32[]{:S(2)}) copy-start(f32[256,64]{0,1:T(8,128)} %param.5) | copy-start | bytes 196612
  36.6 1.3 %collective-permute-start.9 = (f32[64,128]{1,0:T(8,128)S(1)}, f32[64,128]{1,0:T(8,128)S(1)}, u32[]{:S(2)}, u32[]{:S(2)}) collective-permute-start(f32[64,128]{1,0:T(8,128)S(1)} %get-tuple-element.57.mine_ref), channel_id=1, source_target_pairs={{0,1},{1,0},{2,3},{3,2},{4,5},{5,4},{6,7},{7,6},{8,9},{9,8},{10,11... | collective-permute-start | bytes 98312 | tf_op jit(solution)/shard_map/ppermute | solution.py:210
